TPU v7x, 128 devices: a whole 4x4x4 slice. The times are simulated.
128 devices in a mesh: dp: 2 (over core), seq: 32 (over x_hi, z, y), tensor: 2 (over x_lo).
Axes of the slice: x: 4 (x_hi: 2, x_lo: 2; x = x_hi * 2 + x_lo), y: 4, z: 4, core: 2. Of those that a mesh axis runs over, the one named last changes fastest.
Arguments:
- queries: bfloat16 [16384, 2048], P(('dp', 'seq'), 'tensor'), parts along dimension 0
- routed_key_rows: bfloat16 [16384, 512], P(('dp', 'seq'), 'tensor'), parts along dimension 0
- routed_value_rows: bfloat16 [16384, 512], P(('dp', 'seq'), 'tensor'), parts along dimension 0, may hold values from -6 to 6
- grad_out: bfloat16 [16384, 2048], P(('dp', 'seq'), 'tensor'), parts along dimension 0, may hold values from -6 to 6
- gate_logit: float32 [16384], P(('dp', 'seq')), parts along dimension 0, may hold values from -6 to 6
- block_ids: int32 [64, 2], P('dp'), parts along dimension 0, may hold values from 0 to 15, as said below
- block_counts: int32 [64], P('dp'), parts along dimension 0, may hold values from 1 to 2, as said below
Outputs:
- query_grads: bfloat16 [16384, 2048], P(('dp', 'seq'), 'tensor'), parts along dimension 0
- key_grads: bfloat16 [16384, 512], P(('dp', 'seq'), 'tensor'), parts along dimension 0
- value_grads: bfloat16 [16384, 512], P(('dp', 'seq'), 'tensor'), parts along dimension 0
- gate_grads: float32 [16384], P(('dp', 'seq')), parts along dimension 0
There are 2 independent parts, one for each index of `dp`. A program takes and returns all parts, laid end to end along the dimension named above; each array names one. Nothing has to cross between parts.
Inputs may be any that keep to these rules, and one draw needn't show every extreme that they name: `block_ids`: within each shard the routed block positions are distinct. Only the first block_counts[s] slots of shard s hold routed blocks; the rows of the other slots are not live.
All inputs are finite; a program needn't handle non-finite values.
Results may differ from a plain program's by a relative error of at most 0.028.
Values may be sent and summed in bfloat16 or wider, within the bound.
No kernel may reach another device: no remote copies, remote signals or barrier semaphores. Data moves between devices by JAX's collectives and lax.ppermute only.
A program may use at most 128 MiB of HBM per device.

v0:
```python
import math

import jax
import jax.numpy as jnp
from jax import lax
from jax.sharding import PartitionSpec as P

HEAD_SIZE = 128
QUERY_HEADS = 16
KEY_VALUE_HEADS = 4
BLK = 128
SPAN_BLK = 16


def token_positions(block_ids, block_counts):
    shard_count, slot_count = block_ids.shape
    shard_index = jnp.arange(shard_count, dtype=jnp.int32)[:, None]
    block_start = (shard_index * SPAN_BLK + block_ids) * BLK
    offsets = jnp.arange(BLK, dtype=jnp.int32)
    positions = (block_start[:, :, None] + offsets[None, None, :]).reshape(-1)
    slot_live = jnp.arange(slot_count, dtype=jnp.int32)[None, :] < block_counts[:, None]
    live_rows = jnp.broadcast_to(slot_live[:, :, None], (shard_count, slot_count, BLK)).reshape(-1)
    return (positions, live_rows)


def local(
    queries, routed_key_rows, routed_value_rows, grad_out, gate_logit, block_ids, block_counts
):
    row_count = queries.shape[0]
    key_width = routed_key_rows.shape[1]
    kv_local = key_width // HEAD_SIZE
    query_group_width = QUERY_HEADS // KEY_VALUE_HEADS
    seq_index = lax.axis_index("seq")
    key_total = lax.axis_size("seq") * row_count
    score_scale = HEAD_SIZE ** (-0.5)
    positions, live_rows = token_positions(block_ids, block_counts)
    first_row = seq_index * row_count
    query_pos = lax.dynamic_slice_in_dim(positions, first_row, row_count)
    query_live = lax.dynamic_slice_in_dim(live_rows, first_row, row_count)
    query_rows = first_row + jnp.arange(row_count, dtype=jnp.int32)
    last_row = first_row + row_count - 1
    block_target = row_count * max(1, 512 // row_count)
    gate_value = jax.nn.sigmoid(gate_logit)
    output_gradients = (gate_value[:, None] * grad_out.astype(jnp.float32)).astype(jnp.bfloat16)
    heads_of_queries = queries.reshape(row_count, kv_local, query_group_width, HEAD_SIZE)
    output_gradient_heads = output_gradients.reshape(
        row_count, kv_local, query_group_width, HEAD_SIZE
    )

    def block_scores(key_block, block_first):
        block_rows = key_block.shape[0]
        heads_of_keys = key_block.reshape(block_rows, kv_local, HEAD_SIZE)
        scores = (
            jnp.einsum(
                "rkgd,jkd->kgrj",
                heads_of_queries,
                heads_of_keys,
                preferred_element_type=jnp.float32,
            )
            * score_scale
        )
        key_pos = lax.dynamic_slice_in_dim(positions, block_first, block_rows)
        key_live = lax.dynamic_slice_in_dim(live_rows, block_first, block_rows)
        key_index = block_first + jnp.arange(block_rows, dtype=jnp.int32)
        allowed = key_live[None, :] & (key_pos[None, :] <= query_pos[:, None]) | (
            key_index[None, :] == query_rows[:, None]
        )
        return (scores, allowed, heads_of_keys)

    def grads_against(value_block):
        heads_of_values = value_block.reshape(value_block.shape[0], kv_local, HEAD_SIZE)
        return jnp.einsum(
            "rkgd,jkd->kgrj",
            output_gradient_heads,
            heads_of_values,
            preferred_element_type=jnp.float32,
        )

    def stats_block(state_now, key_block, value_block, block_first):
        row_max, row_total, weighted = state_now
        scores, allowed, heads_of_keys = block_scores(key_block, block_first)
        block_max = jnp.max(jnp.where(allowed, scores, -jnp.inf), axis=-1)
        new_max = jnp.maximum(row_max, block_max)
        weights = jnp.where(allowed, jnp.exp(scores - new_max[..., None]), 0.0)
        prob_grads = grads_against(value_block)
        rescale = jnp.exp(row_max - new_max)
        return (
            new_max,
            row_total * rescale + jnp.sum(weights, axis=-1),
            weighted * rescale + jnp.sum(weights * prob_grads, axis=-1),
        )

    def over_blocks(block_fn, state_now, key_piece, value_piece):
        piece_rows = key_piece.shape[0]
        sub_rows = math.gcd(piece_rows, block_target)

        def one_turn(turn_index, carried):
            offset = turn_index * sub_rows
            key_block = lax.dynamic_slice_in_dim(key_piece, offset, sub_rows)
            value_block = lax.dynamic_slice_in_dim(value_piece, offset, sub_rows)

            def compute(inner_state):
                return block_fn(inner_state, key_block, value_block, offset)

            def keep_state(inner_state):
                return inner_state

            return lax.cond(offset <= last_row, compute, keep_state, carried)

        return lax.fori_loop(0, piece_rows // sub_rows, one_turn, state_now)

    stat_shape = (kv_local, query_group_width, row_count)
    stats_seed = (
        jnp.full(stat_shape, -1e30, jnp.float32),
        jnp.zeros(stat_shape, jnp.float32),
        jnp.zeros(stat_shape, jnp.float32),
    )
    pieces = (
        lax.all_gather(routed_key_rows, "seq", axis=0, tiled=True),
        lax.all_gather(routed_value_rows, "seq", axis=0, tiled=True),
    )
    folded = over_blocks(stats_block, stats_seed, pieces[0], pieces[1])
    row_max, row_total, weighted = folded
    live_mask = query_live.astype(jnp.float32)
    delta_rows = weighted / row_total * live_mask
    delta_sum = lax.psum(jnp.sum(delta_rows, axis=(0, 1)), "tensor")
    gate_grads = (1.0 - gate_value) * delta_sum

    def block_terms(key_block, value_block, block_first):
        scores, allowed, heads_of_keys = block_scores(key_block, block_first)
        visible = allowed & query_live[:, None]
        probabilities = (
            jnp.where(visible, jnp.exp(scores - row_max[..., None]), 0.0) / row_total[..., None]
        )
        prob_grads = grads_against(value_block)
        score_gradients = (
            probabilities * (prob_grads - delta_rows[..., None]) * score_scale
        ).astype(jnp.bfloat16)
        return (probabilities.astype(jnp.bfloat16), score_gradients, heads_of_keys)

    def key_block_grads(probability_reduced, score_gradients):
        block_rows = score_gradients.shape[-1]
        key_grad = jnp.einsum(
            "fimw,mfiy->wfy", score_gradients, heads_of_queries, preferred_element_type=jnp.float32
        ).reshape(block_rows, key_width)
        value_grad = jnp.einsum(
            "fimw,mfiy->wfy",
            probability_reduced,
            output_gradient_heads,
            preferred_element_type=jnp.float32,
        ).reshape(block_rows, key_width)
        return (key_grad, value_grad)

    def full_block(state_now, key_block, value_block, block_first):
        query_grad, key_sums, value_sums = state_now
        probability_reduced, score_gradients, heads_of_keys = block_terms(
            key_block, value_block, block_first
        )
        query_grad = query_grad + jnp.einsum(
            "kgrj,jkd->rkgd", score_gradients, heads_of_keys, preferred_element_type=jnp.float32
        )
        key_grad, value_grad = key_block_grads(probability_reduced, score_gradients)
        key_sums = lax.dynamic_update_slice_in_dim(key_sums, key_grad, block_first, 0)
        value_sums = lax.dynamic_update_slice_in_dim(value_sums, value_grad, block_first, 0)
        return (query_grad, key_sums, value_sums)

    grad_seed = jnp.zeros((row_count, kv_local, query_group_width, HEAD_SIZE), jnp.float32)
    partial_seed = (
        grad_seed,
        jnp.zeros((key_total, key_width), jnp.float32),
        jnp.zeros((key_total, key_width), jnp.float32),
    )
    pieces = (
        lax.all_gather(routed_key_rows, "seq", axis=0, tiled=True),
        lax.all_gather(routed_value_rows, "seq", axis=0, tiled=True),
    )
    query_grad, key_sums, value_sums = over_blocks(full_block, partial_seed, pieces[0], pieces[1])
    key_own, value_own = (
        lax.psum_scatter(
            key_sums.astype(jnp.bfloat16), "seq", scatter_dimension=0, tiled=True
        ).astype(jnp.float32),
        lax.psum_scatter(
            value_sums.astype(jnp.bfloat16), "seq", scatter_dimension=0, tiled=True
        ).astype(jnp.float32),
    )
    return (
        query_grad.reshape(row_count, kv_local * query_group_width * HEAD_SIZE).astype(
            jnp.bfloat16
        ),
        key_own.astype(jnp.bfloat16),
        value_own.astype(jnp.bfloat16),
        gate_grads,
    )


def solution(mesh):
    in_specs = (
        P(("dp", "seq"), "tensor"),
        P(("dp", "seq"), "tensor"),
        P(("dp", "seq"), "tensor"),
        P(("dp", "seq"), "tensor"),
        P(("dp", "seq")),
        P("dp", None),
        P("dp"),
    )
    out_specs = (
        P(("dp", "seq"), "tensor"),
        P(("dp", "seq"), "tensor"),
        P(("dp", "seq"), "tensor"),
        P(("dp", "seq")),
    )
    return jax.shard_map(local, mesh=mesh, in_specs=in_specs, out_specs=out_specs, check_vma=False)
```

profile of v0, /device:TPU:0, one launch (start us, length us, event | category | flops | bytes accessed | tf_op | source)
XLA Modules:
  0.0 789.5 jit_solution(16096033716414451428)
XLA Ops:
  7.2 1.7 copy.83
  9.0 1.7 copy.85
  10.8 0.7 add_multiply_fusion
  11.5 0.7 iota_compare_fusion
  12.3 0.1 broadcast_in_dim.68
  12.4 0.7 add_divide_fusion
  13.1 1.2 multiply_convert_fusion
  14.3 0.2 copy.86
  14.5 0.3 copy.88
  14.8 0.2 copy.84
  15.0 0.3 copy.87
  15.3 0.1 iota_add_fusion.4
  15.5 76.2 %all-gather.3.cloned.1.call-done = bf16[8192,256]{0,1:T(8,128)(2,1)} async-done(((bf16[256,256]{0,1:T(8,128)(2,1)}), bf16[8192,256]{0,1:T(8,128)(2,1)}) %all-gather.3.cloned.1.call-update) | async-done | bytes 4194320 | tf_op jit(solution)/shard_map/all_gather | solution.py:174
  91.7 80.5 %all-gather.5.cloned.1.call-done = bf16[8192,256]{0,1:T(8,128)(2,1)} async-done(((bf16[256,256]{0,1:T(8,128)(2,1)}), bf16[8192,256]{0,1:T(8,128)(2,1)}) %all-gather.5.cloned.1.call-update) | async-done | bytes 4194320 | tf_op jit(solution)/shard_map/all_gather | solution.py:175
  172.3 7.5 while.36
  172.4 4.9 conditional.6
  172.5 0.1 broadcast_in_dim.78
  172.7 1.1 constant_dynamic-slice_fusion
  173.8 0.3 compare_or_fusion
  174.1 0.9 fusion.13
  175.0 1.4 fusion.12
  176.4 0.9 fusion.16
  177.5 0.1 iota_add_fusion.7
  178.1 0.1 iota_add_fusion.7
  178.8 0.1 iota_add_fusion.7
  179.8 2.4 broadcast.78.clone
  182.2 2.4 broadcast.78
  184.7 11.0 %while.37 = (s32[]{:T(128)}, f32[256,2,4,128]{3,0,2,1:T(8,128)S(1)}, bf16[8192,256]{0,1:T(8,128)(2,1)}, bf16[8192,256]{0,1:T(8,128)(2,1)}, s32[]{:T(128)}, /*ind...) while((s32[]{:T(128)}, ...), condition=%wide.region_10.0_spmd.clone, body=%wide.region_7.10_spmd.clone.sunk | while | flops 1352540928 | bytes 26838532 | solution.py:110
  184.8 8.5 %conditional.7 = ((f32[256,2,4,128]{3,0,2,1:T(8,128)S(1)}, bf16[8192,256]{0,1:T(8,128)(2,1)}, bf16[8192,256]{0,1:T(8,128)(2,1)})) conditional(s32[]{:T(128)} %convert_element_type.69, (f32[256,2,4,128]{3,0,2,1:T(8,128)S(1)}, bf16[8192,256]{0,1:T(8,128)(2,1)}, bf16[8192,256]{0,1:T(8,128)(2,1)}) %tuple.115, (s32[]{:T(128)}, ...), branch_computations={%region_8.8_spmd, %region_9.9_spmd} | conditional | flops 1352532736 | bytes 26804126 | solution.py:108
  184.9 0.1 broadcast_in_dim.79
  185.1 0.3 or_and_fusion
  185.4 1.0 constant_dynamic-slice_fusion.3
  186.4 1.0 constant_dynamic-slice_fusion.2
  187.4 1.3 fusion.22
  188.6 0.8 fusion.23
  189.5 0.8 fusion.19
  190.3 0.8 fusion.28
  191.1 1.3 fusion.25
  192.3 0.9 constant_dynamic-update-slice_fusion
  194.9 0.1 iota_add_fusion.8
  195.7 6.4 copy.93
  202.1 6.4 copy.92
  208.7 0.4 copy.91
  209.1 1.2 convert_element_type.55
  210.2 4.9 psum.7
  215.1 0.6 subtract_multiply_fusion
  215.7 377.1 %reduce-scatter.5.cloned.1.call-done = bf16[256,256]{1,0:T(8,128)(2,1)} async-done(((bf16[8192,256]{1,0:T(8,128)(2,1)}), bf16[256,256]{1,0:T(8,128)(2,1)}) %reduce-scatter.5.cloned.1.call-update) | async-done | bytes 131088 | tf_op jit(solution)/shard_map/reduce_scatter | solution.py:182
  592.8 190.2 %reduce-scatter.3.cloned.1.call-done = bf16[256,256]{1,0:T(8,128)(2,1)} async-done(((bf16[8192,256]{1,0:T(8,128)(2,1)}), bf16[256,256]{1,0:T(8,128)(2,1)}) %reduce-scatter.3.cloned.1.call-update) | async-done | bytes 131088 | tf_op jit(solution)/shard_map/reduce_scatter | solution.py:179
  (126 shorter events, 4.4 us)
Async XLA Ops:
  7.2 7.6 copy-start
  7.2 84.6 %all-gather.3.cloned.1.call-start = ((), (), s32[]{:S(2)}) async-start(), calls=%async_computation.2 | async-start | bytes 4325376 | tf_op jit(solution)/shard_map/all_gather | solution.py:174
  9.0 163.3 %all-gather.5.cloned.1.call-start = ((), (), s32[]{:S(2)}) async-start(), calls=%async_computation.3 | async-start | bytes 4325376 | tf_op jit(solution)/shard_map/all_gather | solution.py:175
  10.7 582.1 %reduce-scatter.5.cloned.1.call-start = ((), (), s32[]{:S(2)}) async-start(), calls=%async_computation.5 | async-start | bytes 4325376 | tf_op jit(solution)/shard_map/reduce_scatter | solution.py:182
  202.1 580.9 %reduce-scatter.3.cloned.1.call-start = ((), (), s32[]{:S(2)}) async-start(), calls=%async_computation.4 | async-start | bytes 4325376 | tf_op jit(solution)/shard_map/reduce_scatter | solution.py:179
  208.5 6.6 copy-start.1
Sparse Core Ops, SparseCore 0:
  11.3 80.3 all-gather.2
  95.1 77.1 all-gather.4
  202.2 390.5 reduce-scatter.4
  595.6 187.3 reduce-scatter.2
where the time goes:
time: 791 us; the launch traced here: 789 us
  waiting for transfers between devices  724 us (92%)
  local copies, waits for them, and re-layouts  28.5 us (4%)
  between operations  13.9 us (2%)
  other arithmetic  8.67 us (1%)
    reduce_scatter x1, waiting for transfers between devices, local(): lax.psum_scatter(value_sums.astype(jnp.bfloat16), 'seq', scatter_dimensio...  377 us
    reduce_scatter x1, waiting for transfers between devices, local(): lax.psum_scatter(key_sums.astype(jnp.bfloat16), 'seq', scatter_dimension=...  190 us
    all_gather x1, waiting for transfers between devices, local(): lax.all_gather(routed_value_rows, 'seq', axis=0, tiled=True)  80.5 us
    all_gather x1, waiting for transfers between devices, local(): lax.all_gather(routed_key_rows, 'seq', axis=0, tiled=True)  76.2 us
  transfers between devices with their start and end apart: 4, of which 4 were waited for; matrix products, arithmetic and copies ran while one was open for 2% of the time, Pallas kernels for 0%

commit v1 on v0

v1 whole, which is shorter than its diff:
```python
import jax
import jax.numpy as jnp
from jax import lax
from jax.experimental import pallas as pl
from jax.experimental.pallas import tpu as pltpu
from jax.sharding import PartitionSpec as P

HEAD_SIZE = 128
BLK = 128
GROUP = 4
LIVE_SLOTS = 64
SCALE = HEAD_SIZE ** (-0.5)
EXP2_SCALE = SCALE * 1.4426950408889634
CHUNK = 512
MASKED = -1.5e38
NT = (((1,), (1,)), ((), ()))


def dot_nt(a, b):
    return lax.dot_general(a, b, NT, preferred_element_type=jnp.float32)


def dot_nn(a, b):
    return jnp.dot(a, b, preferred_element_type=jnp.float32)


def grad_kernel(
    ktab, vtab, rank, live,
    q, do, k0, k1, k2, k3, v0, v1, v2, v3,
    dq, dk0, dk1, dk2, dk3, dv0, dv1, dv2, dv3, delta_out,
    kc, vc, kt, qs, dos, dka, dva, dqt,
):
    lanes = GROUP * BLK
    per_piece = LIVE_SLOTS // 4
    for piece, (kp, vp) in enumerate(((k0, v0), (k1, v1), (k2, v2), (k3, v3))):

        def pack(b, _, kp=kp, vp=vp, piece=piece):
            at = pl.multiple_of(b * BLK, BLK)
            kd = pl.multiple_of(ktab[piece * per_piece + b] * BLK, BLK)
            vd = pl.multiple_of(vtab[piece * per_piece + b] * BLK, BLK)
            block = kp[pl.ds(at, BLK), :]
            kc[pl.ds(kd, BLK), :] = block
            kt[:, pl.ds(kd, BLK)] = block.T
            vc[pl.ds(vd, BLK), :] = vp[pl.ds(at, BLK), :]
            return 0

        lax.fori_loop(0, per_piece, pack, 0)
    dka[...] = jnp.zeros_like(dka)
    dva[...] = jnp.zeros_like(dva)

    for qb in range(4):
        rows = slice(qb * BLK, (qb + 1) * BLK)

        @pl.when(live[qb] == 0)
        def _(qb=qb, rows=rows):
            dq[rows, :] = jnp.zeros((BLK, lanes), dq.dtype)
            delta_out[qb : qb + 1, :] = jnp.zeros((1, BLK), jnp.float32)

        @pl.when(live[qb] != 0)
        def _(qb=qb, rows=rows):
            my_rank = rank[qb]
            last = my_rank // (CHUNK // BLK)
            for h in range(GROUP):
                cols = slice(h * HEAD_SIZE, (h + 1) * HEAD_SIZE)
                qs[cols, :] = q[rows, cols]
                dos[cols, :] = do[rows, cols]

            def allowed(c):
                key_at = c * CHUNK + lax.broadcasted_iota(jnp.int32, (CHUNK, lanes), 0)
                lane = lax.broadcasted_iota(jnp.int32, (CHUNK, lanes), 1)
                return key_at <= my_rank * BLK + (lane & (BLK - 1))

            def stats(c, carry, masked):
                m, l, w = carry
                at = pl.multiple_of(c * CHUNK, CHUNK)
                s = dot_nt(kc[pl.ds(at, CHUNK), :], qs[...])
                dp = dot_nt(vc[pl.ds(at, CHUNK), :], dos[...])
                if masked:
                    s = jnp.where(allowed(c), s, MASKED)
                s = s.reshape(CHUNK // 8, 8, lanes)
                dp = dp.reshape(CHUNK // 8, 8, lanes)
                mn = jnp.maximum(m, jnp.max(s, axis=0))
                p = jnp.exp2((s - mn[None]) * EXP2_SCALE)
                alpha = jnp.exp2((m - mn) * EXP2_SCALE)
                l = l * alpha + jnp.sum(p, axis=0)
                w = w * alpha + jnp.sum(p * dp, axis=0)
                return mn, l, w

            seed = (
                jnp.full((8, lanes), MASKED, jnp.float32),
                jnp.zeros((8, lanes), jnp.float32),
                jnp.zeros((8, lanes), jnp.float32),
            )
            carry = lax.fori_loop(0, last, lambda c, s: stats(c, s, False), seed)
            m, l, w = stats(last, carry, True)
            top = jnp.max(m, axis=0, keepdims=True)
            fix = jnp.exp2((m - top) * EXP2_SCALE)
            total = jnp.sum(l * fix, axis=0, keepdims=True)
            delta = jnp.sum(w * fix, axis=0, keepdims=True) / total
            lse = top * EXP2_SCALE + jnp.log2(total)
            delta_out[qb : qb + 1, :] = (
                delta[:, 0:128] + delta[:, 128:256] + delta[:, 256:384] + delta[:, 384:512]
            )
            dqt[...] = jnp.zeros_like(dqt)

            def grads(c, masked):
                at = pl.multiple_of(c * CHUNK, CHUNK)
                here = pl.ds(at, CHUNK)
                s = dot_nt(kc[here, :], qs[...])
                dp = dot_nt(vc[here, :], dos[...])
                p = jnp.exp2(s * EXP2_SCALE - lse)
                if masked:
                    p = jnp.where(allowed(c), p, 0.0)
                ds = (p * (dp - delta)).astype(jnp.bfloat16)
                dva[here, :] += dot_nn(p.astype(jnp.bfloat16), dos[...])
                dka[here, :] += dot_nn(ds, qs[...])
                dqt[...] += dot_nn(kt[:, here], ds)

            def turn(c, _):
                grads(c, False)
                return 0

            lax.fori_loop(0, last, turn, 0)
            grads(last, True)
            for h in range(GROUP):
                cols = slice(h * HEAD_SIZE, (h + 1) * HEAD_SIZE)
                dq[rows, cols] = (dqt[:, cols].T * SCALE).astype(dq.dtype)

    for piece, (dkp, dvp) in enumerate(((dk0, dv0), (dk1, dv1), (dk2, dv2), (dk3, dv3))):

        def unpack(b, _, dkp=dkp, dvp=dvp, piece=piece):
            at = pl.multiple_of(b * BLK, BLK)
            kd = pl.multiple_of(ktab[piece * per_piece + b] * BLK, BLK)
            vd = pl.multiple_of(vtab[piece * per_piece + b] * BLK, BLK)
            dkp[pl.ds(at, BLK), :] = (dka[pl.ds(kd, BLK), :] * SCALE).astype(dkp.dtype)
            dvp[pl.ds(at, BLK), :] = dva[pl.ds(vd, BLK), :].astype(dvp.dtype)
            return 0

        lax.fori_loop(0, per_piece, unpack, 0)


def grad_call(ktab, vtab, rank, live, q, do, ks, vs):
    bf = jnp.bfloat16
    piece = jax.ShapeDtypeStruct(ks[0].shape, bf)
    keys = 4 * ks[0].shape[0]
    lanes = GROUP * BLK
    vm = pl.BlockSpec(memory_space=pltpu.VMEM)
    sm = pl.BlockSpec(memory_space=pltpu.SMEM)
    out = pl.pallas_call(
        grad_kernel,
        out_shape=(jax.ShapeDtypeStruct(q.shape, bf),) + (piece,) * 8
        + (jax.ShapeDtypeStruct((4, BLK), jnp.float32),),
        in_specs=[sm] * 4 + [vm] * 10,
        out_specs=(vm,) * 10,
        scratch_shapes=[
            pltpu.VMEM((keys, HEAD_SIZE), bf),
            pltpu.VMEM((keys, HEAD_SIZE), bf),
            pltpu.VMEM((HEAD_SIZE, keys), bf),
            pltpu.VMEM((lanes, HEAD_SIZE), bf),
            pltpu.VMEM((lanes, HEAD_SIZE), bf),
            pltpu.VMEM((keys, HEAD_SIZE), jnp.float32),
            pltpu.VMEM((keys, HEAD_SIZE), jnp.float32),
            pltpu.VMEM((HEAD_SIZE, lanes), jnp.float32),
        ],
        compiler_params=pltpu.CompilerParams(vmem_limit_bytes=48 * 1024 * 1024),
        name="attention_grads",
    )(ktab, vtab, rank, live, q, do, *ks, *vs)
    return out[0], out[1:5], out[5:9], out[9]


def ring_perms(axis):
    def place(s, step):
        x, z, y = s // 16, s // 4 % 4, s % 4
        if axis == "z":
            z = (z + step) % 4
        else:
            y = (y + step) % 4
        return 16 * x + 4 * z + y

    return {step: [(s, place(s, step)) for s in range(32)] for step in (1, -1, 2, -2)}


Z_RING, Y_RING = ring_perms("z"), ring_perms("y")
PAIR = [(s, 31 - s) for s in range(32)]
OFFSETS = (0, -1, 1, 2)


def send(a, perm):
    return lax.ppermute(a, "seq", perm)


def ring_gather(block, ring):
    return [block] + [send(block, ring[-step]) for step in OFFSETS[1:]]


def ring_sum(pieces, ring):
    total = pieces[0].astype(jnp.float32)
    for piece, step in zip(pieces[1:], OFFSETS[1:]):
        total = total + send(piece, ring[step]).astype(jnp.float32)
    return total


def block_tables(block_ids, block_counts, seq_index):
    shard = jnp.arange(32, dtype=jnp.int32)
    before = jnp.sum(jnp.where(shard[None, :] < shard[:, None], block_counts[None, :], 0), axis=1)
    total = jnp.sum(block_counts)
    slot = jnp.arange(2, dtype=jnp.int32)
    live = slot[None, :] < block_counts[:, None]
    other = block_ids[:, ::-1]
    first = (live[:, ::-1] & (other < block_ids)).astype(jnp.int32)
    rank_live = before[:, None] + first
    rank_dead = total + 2 * shard[:, None] - before[:, None] + slot[None, :] - block_counts[:, None]
    rank = jnp.where(live, rank_live, rank_dead).reshape(-1)
    half, z, y = seq_index // 16, seq_index // 4 % 4, seq_index % 4
    offset = jnp.asarray(OFFSETS, jnp.int32)

    def lookup(values, index):
        hit = index[:, None] == jnp.arange(64, dtype=jnp.int32)[None, :]
        return jnp.sum(jnp.where(hit, values[None, :], 0), axis=1)

    def slots_of(place):
        low = jnp.where(half == 0, place, 15 - place)
        shards = jnp.stack([low, 31 - low], axis=-1)
        return (shards[..., None] * 2 + slot).reshape(-1)

    zs, ys = (z + offset) % 4, (y + offset) % 4
    ktab = lookup(rank, slots_of(zs[:, None] * 4 + ys[None, :]))
    vtab = lookup(rank, slots_of(zs[None, :] * 4 + ys[:, None]))
    mine = slots_of(jnp.reshape(z * 4 + y, (1,)))
    return ktab, vtab, lookup(rank, mine), lookup(live.reshape(-1).astype(jnp.int32), mine)


def local(
    queries, routed_key_rows, routed_value_rows, grad_out, gate_logit, block_ids, block_counts
):
    bf = jnp.bfloat16
    rows = queries.shape[0]
    seq_index = lax.axis_index("seq")
    half = seq_index // 16
    low = half == 0

    def halves(a):
        width = a.shape[1] // 2
        left, right = a[:, :width], a[:, width:]
        return jnp.where(low, left, right), jnp.where(low, right, left)

    def rows_of(own, other):
        return jnp.concatenate([jnp.where(low, own, other), jnp.where(low, other, own)], axis=0)

    def columns_of(own, other):
        return jnp.concatenate([jnp.where(low, own, other), jnp.where(low, other, own)], axis=1)

    gate = jax.nn.sigmoid(gate_logit)
    out_grad = (gate[:, None] * grad_out.astype(jnp.float32)).astype(bf)
    k_own, k_other = halves(routed_key_rows)
    v_own, v_other = halves(routed_value_rows)
    kv_in = send(jnp.concatenate([k_other, v_other], axis=1), PAIR)
    keys = rows_of(k_own, kv_in[:, :HEAD_SIZE])
    values = rows_of(v_own, kv_in[:, HEAD_SIZE:])
    q_own, q_other = halves(queries)
    d_own, d_other = halves(out_grad)
    q_all = rows_of(q_own, send(q_other, PAIR))
    d_all = rows_of(d_own, send(d_other, PAIR))

    k_near = jnp.concatenate(ring_gather(keys, Y_RING), axis=0)
    v_near = jnp.concatenate(ring_gather(values, Z_RING), axis=0)
    k_pieces = ring_gather(k_near, Z_RING)
    v_pieces = ring_gather(v_near, Y_RING)
    ktab, vtab, rank, live = block_tables(block_ids, block_counts, seq_index)
    dq, dk_pieces, dv_pieces, delta = grad_call(
        ktab, vtab, rank, live, q_all, d_all, k_pieces, v_pieces
    )

    def split(a):
        return [a[i * 2 * rows : (i + 1) * 2 * rows] for i in range(4)]

    dk = ring_sum(split(ring_sum(dk_pieces, Z_RING).astype(bf)), Y_RING).astype(bf)
    dv = ring_sum(split(ring_sum(dv_pieces, Y_RING).astype(bf)), Z_RING).astype(bf)

    def own_other(a):
        return jnp.where(low, a[:rows], a[rows:]), jnp.where(low, a[rows:], a[:rows])

    delta_own, delta_other = own_other(delta.reshape(-1))
    delta_sum = delta_own + send(delta_other, PAIR)
    delta_sum = delta_sum + lax.ppermute(delta_sum, "tensor", [(0, 1), (1, 0)])
    dq_own, dq_other = own_other(dq)
    query_grads = columns_of(dq_own, send(dq_other, PAIR))
    dk_own, dk_other = own_other(dk)
    dv_own, dv_other = own_other(dv)
    back = send(jnp.concatenate([dk_other, dv_other], axis=1), PAIR)
    key_grads = columns_of(dk_own, back[:, :HEAD_SIZE])
    value_grads = columns_of(dv_own, back[:, HEAD_SIZE:])
    return query_grads, key_grads, value_grads, (1.0 - gate) * delta_sum


def solution(mesh):
    in_specs = (
        P(("dp", "seq"), "tensor"),
        P(("dp", "seq"), "tensor"),
        P(("dp", "seq"), "tensor"),
        P(("dp", "seq"), "tensor"),
        P(("dp", "seq")),
        P("dp", None),
        P("dp"),
    )
    out_specs = (
        P(("dp", "seq"), "tensor"),
        P(("dp", "seq"), "tensor"),
        P(("dp", "seq"), "tensor"),
        P(("dp", "seq")),
    )
    return jax.shard_map(local, mesh=mesh, in_specs=in_specs, out_specs=out_specs, check_vma=False)
```

time: 791 us -> 216 us (0.27)
  waiting for transfers between devices: 724 us -> 102 us
  starting transfers between devices: 0.16 us -> 55.1 us
  Pallas kernels: 0 us -> 44.8 us
  local copies, waits for them, and re-layouts: 28.5 us -> 2.59 us
  between operations: 13.9 us -> 1.19 us
    reduce_scatter x2 -> x0, waiting for transfers between devices: 567 us -> none  [the longest x1 377 us: local(): lax.psum_scatter(value_sums.astype(jnp.bfloat16), 'seq', scatter_dimensio...]
    all_gather x2 -> x0, waiting for transfers between devices: 157 us -> none  [the longest x1 80.5 us: local(): lax.all_gather(routed_value_rows, 'seq', axis=0, tiled=True)]
    ppermute x0 -> x31, waiting for transfers between devices: none -> 102 us  [the longest x30 102 us: send(): return lax.ppermute(a, 'seq', perm)]
    ppermute x0 -> x31, starting transfers between devices: none -> 55.1 us  [the longest x30 54.5 us: send(): return lax.ppermute(a, 'seq', perm)]
    pallas_call x0 -> x1, Pallas kernels: none -> 44.8 us  [grad_call(): pl.pallas_call(grad_kernel, out_shape=(jax.ShapeDtypeStruct(q.shape, bf),...]
    while x2 -> x0, local copies, waits for them, and re-layouts: 12.8 us -> none  [over_blocks(): return lax.fori_loop(0, piece_rows // sub_rows, one_turn, state_now)]
  transfers between devices with their start and end apart: 4 -> 31, of which waited for: 4 -> 18; matrix products, arithmetic and copies ran while one was open for 2% -> 3% of each run, Pallas kernels for 0% -> 0%
where the time goes in v1:
time: 216 us; the launch traced here: 215 us
  waiting for transfers between devices  102 us (47%)
  starting transfers between devices  55.1 us (26%)
  Pallas kernels  44.8 us (21%)
  other arithmetic  8.81 us (4%)
  local copies, waits for them, and re-layouts  2.59 us (1%)
    ppermute x30, waiting for transfers between devices, send(): return lax.ppermute(a, 'seq', perm)  102 us
    ppermute x30, starting transfers between devices, send(): return lax.ppermute(a, 'seq', perm)  54.5 us
    pallas_call x1, Pallas kernels, grad_call(): pl.pallas_call(grad_kernel, out_shape=(jax.ShapeDtypeStruct(q.shape, bf),...  44.8 us
  transfers between devices with their start and end apart: 31, of which 18 were waited for; matrix products, arithmetic and copies ran while one was open for 3% of the time, Pallas kernels for 0%

profile of v1, /device:TPU:0, one launch (start us, length us, event | category | flops | bytes accessed | tf_op | source)
XLA Modules:
  0.0 214.8 jit_solution(2088697531954139972)
XLA Ops:
  0.7 1.0 broadcast_select_fusion.25
  1.7 9.1 %collective-permute-start.2 = (bf16[256,256]{1,0:T(8,128)(2,1)S(1)}, bf16[256,256]{1,0:T(8,128)(2,1)S(1)}, u32[]{:S(2)}, u32[]{:S(2)}) collective-permute-start(bf16[256,256]{1,0:T(8,128)(2,1)S(1)} %pad_maximum_fusion.3), channel_id=1, source_target_pairs={{0,62},{2,60},{4,58},{6,56},{8,54},{10,52},{12,50},{14,48},{16,46}... | collective-permute-start | bytes 393224 | tf_op jit(solution)/shard_map/ppermute | solution.py:189
  10.8 0.8 broadcast_select_fusion.10
  11.8 0.7 broadcast_select_fusion.6
  12.5 7.7 %collective-permute-start.1 = (bf16[256,512]{1,0:T(8,128)(2,1)}, bf16[256,512]{1,0:T(8,128)(2,1)S(1)}, u32[]{:S(2)}, u32[]{:S(2)}) collective-permute-start(bf16[256,512]{1,0:T(8,128)(2,1)} %broadcast_select_fusion.6), channel_id=1, source_target_pairs={{0,62},{2,60},{4,58},{6,56},{8,54},{10,52},{12,50},{14,48},{16,46}... | collective-permute-start | bytes 786440 | tf_op jit(solution)/shard_map/ppermute | solution.py:189
  20.3 0.6 copy-done.14
  20.9 0.6 reduce_sum.55
  21.7 0.6 add_subtract_fusion
  23.7 0.7 collective-permute-start.11
  24.4 2.7 %collective-permute-start.10 = (bf16[512,128]{1,0:T(8,128)(2,1)S(1)}, bf16[512,128]{1,0:T(8,128)(2,1)S(1)}, u32[]{:S(2)}, u32[]{:S(2)}) collective-permute-start(bf16[512,128]{1,0:T(8,128)(2,1)S(1)} %pad_maximum_fusion.5), channel_id=1, source_target_pairs={{0,24},{2,26},{4,28},{6,30},{8,0},{10,2},{12,4},{14,6},{16,8},{18,... | collective-permute-start | bytes 393224 | tf_op jit(solution)/shard_map/ppermute | solution.py:189
  27.1 9.4 %collective-permute-done.9 = bf16[512,128]{1,0:T(8,128)(2,1)S(1)} collective-permute-done((bf16[512,128]{1,0:T(8,128)(2,1)S(1)}, bf16[512,128]{1,0:T(8,128)(2,1)S(1)}, u32[]{:S(2)}, u32[]{:S(2)}) %collective-permute-start.9) | collective-permute-done | bytes 131104 | tf_op jit(solution)/shard_map/ppermute | solution.py:189
  36.6 1.8 collective-permute-start.14
  38.9 1.6 collective-permute-start.4
  40.7 13.6 %collective-permute-done.3 = bf16[512,128]{1,0:T(8,128)(2,1)S(1)} collective-permute-done((bf16[512,128]{1,0:T(8,128)(2,1)S(1)}, bf16[512,128]{1,0:T(8,128)(2,1)S(1)}, u32[]{:S(2)}, u32[]{:S(2)}) %collective-permute-start.3) | collective-permute-done | bytes 131104 | tf_op jit(solution)/shard_map/ppermute | solution.py:189
  54.4 1.3 collective-permute-done.4
  55.7 2.6 %collective-permute-start.13 = (bf16[2048,128]{1,0:T(8,128)(2,1)S(1)}, bf16[2048,128]{1,0:T(8,128)(2,1)S(1)}, u32[]{:S(2)}, u32[]{:S(2)}) collective-permute-start(bf16[2048,128]{1,0:T(8,128)(2,1)S(1)} %constant_dynamic-update-slice_fusion.5.v0), channel_id=1, source_target_pairs={{0,6},{2,0},{4,2},{6,4},{8,14},{10,8},{12,10},{14,12},{16,22},{18,... | collective-permute-start | bytes 1572872 | tf_op jit(solution)/shard_map/ppermute | solution.py:189
  58.3 2.5 %collective-permute-done.5 = bf16[512,128]{1,0:T(8,128)(2,1)S(1)} collective-permute-done((bf16[512,128]{1,0:T(8,128)(2,1)S(1)}, bf16[512,128]{1,0:T(8,128)(2,1)S(1)}, u32[]{:S(2)}, u32[]{:S(2)}) %collective-permute-start.5) | collective-permute-done | bytes 131104 | tf_op jit(solution)/shard_map/ppermute | solution.py:189
  61.1 2.0 collective-permute-start.6
  63.3 6.2 %collective-permute-done.13.v2 = bf16[2048,128]{1,0:T(8,128)(2,1)S(1)} collective-permute-done((bf16[2048,128]{1,0:T(8,128)(2,1)S(1)}, bf16[2048,128]{1,0:T(8,128)(2,1)S(1)}, u32[]{:S(2)}, u32[]{:S(2)}) %collective-permute-start.13) | collective-permute-done | bytes 524320 | tf_op jit(solution)/shard_map/ppermute | solution.py:189
  69.6 4.6 %collective-permute-done.12.v1 = bf16[2048,128]{1,0:T(8,128)(2,1)S(1)} collective-permute-done((bf16[2048,128]{1,0:T(8,128)(2,1)S(1)}, bf16[2048,128]{1,0:T(8,128)(2,1)S(1)}, u32[]{:S(2)}, u32[]{:S(2)}) %collective-permute-start.12) | collective-permute-done | bytes 524320 | tf_op jit(solution)/shard_map/ppermute | solution.py:189
  74.1 3.2 %collective-permute-done.8.k3 = bf16[2048,128]{1,0:T(8,128)(2,1)S(1)} collective-permute-done((bf16[2048,128]{1,0:T(8,128)(2,1)S(1)}, bf16[2048,128]{1,0:T(8,128)(2,1)S(1)}, u32[]{:S(2)}, u32[]{:S(2)}) %collective-permute-start.8) | collective-permute-done | bytes 524320 | tf_op jit(solution)/shard_map/ppermute | solution.py:189
  77.4 5.4 %collective-permute-done.7.k2 = bf16[2048,128]{1,0:T(8,128)(2,1)S(1)} collective-permute-done((bf16[2048,128]{1,0:T(8,128)(2,1)S(1)}, bf16[2048,128]{1,0:T(8,128)(2,1)S(1)}, u32[]{:S(2)}, u32[]{:S(2)}) %collective-permute-start.7) | collective-permute-done | bytes 524320 | tf_op jit(solution)/shard_map/ppermute | solution.py:189
  82.7 3.1 %collective-permute-done.6.k1 = bf16[2048,128]{1,0:T(8,128)(2,1)S(1)} collective-permute-done((bf16[2048,128]{1,0:T(8,128)(2,1)S(1)}, bf16[2048,128]{1,0:T(8,128)(2,1)S(1)}, u32[]{:S(2)}, u32[]{:S(2)}) %collective-permute-start.6) | collective-permute-done | bytes 524320 | tf_op jit(solution)/shard_map/ppermute | solution.py:189
  85.8 0.8 copy-done.10
  86.6 44.8 %attention_grads.1 = (bf16[512,512]{1,0:T(8,128)(2,1)S(1)}, bf16[2048,128]{1,0:T(8,128)(2,1)S(1)}, bf16[2048,128]{1,0:T(8,128)(2,1)S(1)}, bf16[2048,128]{1,0:T(8...) custom-call(s32[64]{0:T(128)S(1)} %get-tuple-element.27.ktab, ...), custom_call_target="tpu_custom_call" | custom-call | tf_op jit(solution)/shard_map/attention_grads/pallas_call | solution.py:149
  131.4 3.0 %collective-permute-start.29 = (f32[256]{0:T(256)S(1)}, f32[256]{0:T(256)S(1)}, u32[]{:S(2)}, u32[]{:S(2)}) collective-permute-start(f32[256]{0:T(256)S(1)} %select_bitcast_fusion), channel_id=1, source_target_pairs={{0,62},{2,60},{4,58},{6,56},{8,54},{10,52},{12,50},{14,48},{16,46}... | collective-permute-start | bytes 3080 | tf_op jit(solution)/shard_map/ppermute | solution.py:189
  134.4 2.0 collective-permute-start.17
  136.5 4.3 %collective-permute-done.29 = f32[256]{0:T(256)S(1)} collective-permute-done((f32[256]{0:T(256)S(1)}, f32[256]{0:T(256)S(1)}, u32[]{:S(2)}, u32[]{:S(2)}) %collective-permute-start.29) | collective-permute-done | bytes 1056 | tf_op jit(solution)/shard_map/ppermute | solution.py:189
  140.8 0.6 collective-permute-start.30
  141.4 4.6 %collective-permute-start.15 = (bf16[256,512]{1,0:T(8,128)(2,1)S(1)}, bf16[256,512]{1,0:T(8,128)(2,1)S(1)}, u32[]{:S(2)}, u32[]{:S(2)}) collective-permute-start(bf16[256,512]{1,0:T(8,128)(2,1)S(1)} %broadcast_select_fusion.2), channel_id=1, source_target_pairs={{0,62},{2,60},{4,58},{6,56},{8,54},{10,52},{12,50},{14,48},{16,46}... | collective-permute-start | bytes 786440 | tf_op jit(solution)/shard_map/ppermute | solution.py:189
  146.1 0.6 add_multiply_fusion.2
  146.7 14.2 %collective-permute-done.16 = bf16[2048,128]{1,0:T(8,128)(2,1)S(1)} collective-permute-done((bf16[2048,128]{1,0:T(8,128)(2,1)S(1)}, bf16[2048,128]{1,0:T(8,128)(2,1)S(1)}, u32[]{:S(2)}, u32[]{:S(2)}) %collective-permute-start.16) | collective-permute-done | bytes 524320 | tf_op jit(solution)/shard_map/ppermute | solution.py:189
  160.8 3.4 %collective-permute-done.17 = bf16[2048,128]{1,0:T(8,128)(2,1)S(1)} collective-permute-done((bf16[2048,128]{1,0:T(8,128)(2,1)S(1)}, bf16[2048,128]{1,0:T(8,128)(2,1)S(1)}, u32[]{:S(2)}, u32[]{:S(2)}) %collective-permute-start.17) | collective-permute-done | bytes 524320 | tf_op jit(solution)/shard_map/ppermute | solution.py:189
  164.3 0.3 add_convert_fusion.1
  164.7 3.6 %collective-permute-start.21 = (bf16[512,128]{1,0:T(8,128)(2,1)S(1)}, bf16[512,128]{1,0:T(8,128)(2,1)S(1)}, u32[]{:S(2)}, u32[]{:S(2)}) collective-permute-start(bf16[512,128]{1,0:T(8,128)(2,1)S(1)} %get-tuple-element.43), channel_id=1, source_target_pairs={{0,4},{2,6},{4,0},{6,2},{8,12},{10,14},{12,8},{14,10},{16,20},{18,... | collective-permute-start | bytes 393224 | tf_op jit(solution)/shard_map/ppermute | solution.py:189
  168.3 21.6 %collective-permute-done.23 = bf16[2048,128]{1,0:T(8,128)(2,1)S(1)} collective-permute-done((bf16[2048,128]{1,0:T(8,128)(2,1)S(1)}, bf16[2048,128]{1,0:T(8,128)(2,1)S(1)}, u32[]{:S(2)}, u32[]{:S(2)}) %collective-permute-start.23) | collective-permute-done | bytes 524320 | tf_op jit(solution)/shard_map/ppermute | solution.py:189
  189.9 0.3 add_convert_fusion
  190.2 3.5 %collective-permute-start.25 = (bf16[512,128]{1,0:T(8,128)(2,1)S(1)}, bf16[512,128]{1,0:T(8,128)(2,1)S(1)}, u32[]{:S(2)}, u32[]{:S(2)}) collective-permute-start(bf16[512,128]{1,0:T(8,128)(2,1)S(1)} %get-tuple-element.45), channel_id=1, source_target_pairs={{0,24},{2,26},{4,28},{6,30},{8,0},{10,2},{12,4},{14,6},{16,8},{18,... | collective-permute-start | bytes 393224 | tf_op jit(solution)/shard_map/ppermute | solution.py:189
  193.7 1.0 collective-permute-start.26
  194.6 1.4 collective-permute-done.20
  196.1 2.0 collective-permute-done.25
  198.2 2.4 %collective-permute-done.27 = bf16[512,128]{1,0:T(8,128)(2,1)S(1)} collective-permute-done((bf16[512,128]{1,0:T(8,128)(2,1)S(1)}, bf16[512,128]{1,0:T(8,128)(2,1)S(1)}, u32[]{:S(2)}, u32[]{:S(2)}) %collective-permute-start.27) | collective-permute-done | bytes 131104 | tf_op jit(solution)/shard_map/ppermute | solution.py:189
  200.6 1.0 collective-permute-done.26
  201.7 8.3 %collective-permute-start.28 = (bf16[256,256]{1,0:T(8,128)(2,1)S(1)}, bf16[256,256]{1,0:T(8,128)(2,1)S(1)}, u32[]{:S(2)}, u32[]{:S(2)}) collective-permute-start(bf16[256,256]{1,0:T(8,128)(2,1)S(1)} %pad_maximum_fusion.6), channel_id=1, source_target_pairs={{0,62},{2,60},{4,58},{6,56},{8,54},{10,52},{12,50},{14,48},{16,46}... | collective-permute-start | bytes 393224 | tf_op jit(solution)/shard_map/ppermute | solution.py:189
  210.1 0.9 pad_maximum_fusion.2
  211.0 2.5 %collective-permute-done.28 = bf16[256,256]{1,0:T(8,128)(2,1)S(1)} collective-permute-done((bf16[256,256]{1,0:T(8,128)(2,1)S(1)}, bf16[256,256]{1,0:T(8,128)(2,1)S(1)}, u32[]{:S(2)}, u32[]{:S(2)}) %collective-permute-start.28) | collective-permute-done | bytes 131104 | tf_op jit(solution)/shard_map/ppermute | solution.py:189
  213.5 0.7 pad_maximum_fusion.8
  214.2 0.7 pad_maximum_fusion.7
  (110 shorter events, 3.2 us)
Async XLA Ops:
  0.6 10.2 %copy-start = (bf16[256,1024]{1,0:T(8,128)(2,1)S(1)}, bf16[256,1024]{1,0:T(8,128)(2,1)}, u32[]{:S(2)}) copy-start(bf16[256,1024]{1,0:T(8,128)(2,1)} %param.8) | copy-start | bytes 1572868
  1.7 9.9 %copy-start.11 = (bf16[256,1024]{1,0:T(8,128)(2,1)S(1)}, bf16[256,1024]{1,0:T(8,128)(2,1)}, u32[]{:S(2)}) copy-start(bf16[256,1024]{1,0:T(8,128)(2,1)} %param.11) | copy-start | bytes 1572868
  1.7 9.9 %copy-start.13 = (f32[256]{0:T(256)S(1)}, f32[256]{0:T(256)}, u32[]{:S(2)}) copy-start(f32[256]{0:T(256)} %param.12) | copy-start | bytes 3076
  1.7 21.5 %collective-permute-start.2 = (bf16[256,256]{1,0:T(8,128)(2,1)S(1)}, bf16[256,256]{1,0:T(8,128)(2,1)S(1)}, u32[]{:S(2)}, u32[]{:S(2)}) collective-permute-start(bf16[256,256]{1,0:T(8,128)(2,1)S(1)} %pad_maximum_fusion.3), channel_id=1, source_target_pairs={{0,62},{2,60},{4,58},{6,56},{8,54},{10,52},{12,50},{14,48},{16,46}... | collective-permute-start | bytes 393224 | tf_op jit(solution)/shard_map/ppermute | solution.py:189
  11.6 49.3 %collective-permute-start = (bf16[256,512]{1,0:T(8,128)(2,1)}, bf16[256,512]{1,0:T(8,128)(2,1)S(1)}, u32[]{:S(2)}, u32[]{:S(2)}) collective-permute-start(bf16[256,512]{1,0:T(8,128)(2,1)} %broadcast_select_fusion.10), channel_id=1, source_target_pairs={{0,62},{2,60},{4,58},{6,56},{8,54},{10,52},{12,50},{14,48},{16,46}... | collective-permute-start | bytes 786440 | tf_op jit(solution)/shard_map/ppermute | solution.py:189
  11.8 10.8 %copy-start.15 = (s32[4]{0:T(128)S(1)}, s32[4]{0:T(128)}, u32[]{:S(2)}) copy-start(s32[4]{0:T(128)} %constant.78.clone) | copy-start | bytes 52
  12.5 48.5 %collective-permute-start.1 = (bf16[256,512]{1,0:T(8,128)(2,1)}, bf16[256,512]{1,0:T(8,128)(2,1)S(1)}, u32[]{:S(2)}, u32[]{:S(2)}) collective-permute-start(bf16[256,512]{1,0:T(8,128)(2,1)} %broadcast_select_fusion.6), channel_id=1, source_target_pairs={{0,62},{2,60},{4,58},{6,56},{8,54},{10,52},{12,50},{14,48},{16,46}... | collective-permute-start | bytes 786440 | tf_op jit(solution)/shard_map/ppermute | solution.py:189
  20.3 0.7 copy-start.14
  20.3 1.4 copy-start.12
  20.3 3.0 %copy-start.1 = (bf16[256,256]{1,0:T(8,128)(2,1)S(1)}, bf16[256,256]{1,0:T(8,128)(2,1)}, u32[]{:S(2)}) copy-start(bf16[256,256]{1,0:T(8,128)(2,1)} %param.10) | copy-start | bytes 393220
  20.3 3.0 %copy-start.2 = (bf16[256,256]{1,0:T(8,128)(2,1)S(1)}, bf16[256,256]{1,0:T(8,128)(2,1)}, u32[]{:S(2)}) copy-start(bf16[256,256]{1,0:T(8,128)(2,1)} %param.9) | copy-start | bytes 393220
  23.4 13.1 %collective-permute-start.9 = (bf16[512,128]{1,0:T(8,128)(2,1)S(1)}, bf16[512,128]{1,0:T(8,128)(2,1)S(1)}, u32[]{:S(2)}, u32[]{:S(2)}) collective-permute-start(bf16[512,128]{1,0:T(8,128)(2,1)S(1)} %pad_maximum_fusion.5), channel_id=1, source_target_pairs={{0,8},{2,10},{4,12},{6,14},{8,16},{10,18},{12,20},{14,22},{16,24},... | collective-permute-start | bytes 393224 | tf_op jit(solution)/shard_map/ppermute | solution.py:189
  23.7 12.9 %collective-permute-start.11 = (bf16[512,128]{1,0:T(8,128)(2,1)S(1)}, bf16[512,128]{1,0:T(8,128)(2,1)S(1)}, u32[]{:S(2)}, u32[]{:S(2)}) collective-permute-start(bf16[512,128]{1,0:T(8,128)(2,1)S(1)} %pad_maximum_fusion.5), channel_id=1, source_target_pairs={{0,16},{2,18},{4,20},{6,22},{8,24},{10,26},{12,28},{14,30},{16,0},... | collective-permute-start | bytes 393224 | tf_op jit(solution)/shard_map/ppermute | solution.py:189
  24.4 12.1 %collective-permute-start.10 = (bf16[512,128]{1,0:T(8,128)(2,1)S(1)}, bf16[512,128]{1,0:T(8,128)(2,1)S(1)}, u32[]{:S(2)}, u32[]{:S(2)}) collective-permute-start(bf16[512,128]{1,0:T(8,128)(2,1)S(1)} %pad_maximum_fusion.5), channel_id=1, source_target_pairs={{0,24},{2,26},{4,28},{6,30},{8,0},{10,2},{12,4},{14,6},{16,8},{18,... | collective-permute-start | bytes 393224 | tf_op jit(solution)/shard_map/ppermute | solution.py:189
  36.5 17.9 %collective-permute-start.3 = (bf16[512,128]{1,0:T(8,128)(2,1)S(1)}, bf16[512,128]{1,0:T(8,128)(2,1)S(1)}, u32[]{:S(2)}, u32[]{:S(2)}) collective-permute-start(bf16[512,128]{1,0:T(8,128)(2,1)S(1)} %pad_maximum_fusion.4), channel_id=1, source_target_pairs={{0,2},{2,4},{4,6},{6,0},{8,10},{10,12},{12,14},{14,8},{16,18},{18,... | collective-permute-start | bytes 393224 | tf_op jit(solution)/shard_map/ppermute | solution.py:189
  36.6 26.5 %copy-start.3 = (bf16[2048,128]{1,0:T(8,128)(2,1)}, bf16[2048,128]{1,0:T(8,128)(2,1)S(1)}, u32[]{:S(2)}) copy-start(bf16[2048,128]{1,0:T(8,128)(2,1)S(1)} %constant_dynamic-update-slice_fusion.5.v0) | copy-start | bytes 1572868
  36.6 24.5 %collective-permute-start.14 = (bf16[2048,128]{1,0:T(8,128)(2,1)S(1)}, bf16[2048,128]{1,0:T(8,128)(2,1)S(1)}, u32[]{:S(2)}, u32[]{:S(2)}) collective-permute-start(bf16[2048,128]{1,0:T(8,128)(2,1)S(1)} %constant_dynamic-update-slice_fusion.5.v0), channel_id=1, source_target_pairs={{0,4},{2,6},{4,0},{6,2},{8,12},{10,14},{12,8},{14,10},{16,20},{18,... | collective-permute-start | bytes 1572872 | tf_op jit(solution)/shard_map/ppermute | solution.py:189
  38.9 16.8 %collective-permute-start.4 = (bf16[512,128]{1,0:T(8,128)(2,1)S(1)}, bf16[512,128]{1,0:T(8,128)(2,1)S(1)}, u32[]{:S(2)}, u32[]{:S(2)}) collective-permute-start(bf16[512,128]{1,0:T(8,128)(2,1)S(1)} %pad_maximum_fusion.4), channel_id=1, source_target_pairs={{0,6},{2,0},{4,2},{6,4},{8,14},{10,8},{12,10},{14,12},{16,22},{18,... | collective-permute-start | bytes 393224 | tf_op jit(solution)/shard_map/ppermute | solution.py:189
  54.4 6.5 %collective-permute-start.5 = (bf16[512,128]{1,0:T(8,128)(2,1)S(1)}, bf16[512,128]{1,0:T(8,128)(2,1)S(1)}, u32[]{:S(2)}, u32[]{:S(2)}) collective-permute-start(bf16[512,128]{1,0:T(8,128)(2,1)S(1)} %pad_maximum_fusion.4), channel_id=1, source_target_pairs={{0,4},{2,6},{4,0},{6,2},{8,12},{10,14},{12,8},{14,10},{16,20},{18,... | collective-permute-start | bytes 393224 | tf_op jit(solution)/shard_map/ppermute | solution.py:189
  55.7 13.9 %collective-permute-start.13 = (bf16[2048,128]{1,0:T(8,128)(2,1)S(1)}, bf16[2048,128]{1,0:T(8,128)(2,1)S(1)}, u32[]{:S(2)}, u32[]{:S(2)}) collective-permute-start(bf16[2048,128]{1,0:T(8,128)(2,1)S(1)} %constant_dynamic-update-slice_fusion.5.v0), channel_id=1, source_target_pairs={{0,6},{2,0},{4,2},{6,4},{8,14},{10,8},{12,10},{14,12},{16,22},{18,... | collective-permute-start | bytes 1572872 | tf_op jit(solution)/shard_map/ppermute | solution.py:189
  60.9 13.3 %collective-permute-start.12 = (bf16[2048,128]{1,0:T(8,128)(2,1)S(1)}, bf16[2048,128]{1,0:T(8,128)(2,1)S(1)}, u32[]{:S(2)}, u32[]{:S(2)}) collective-permute-start(bf16[2048,128]{1,0:T(8,128)(2,1)S(1)} %constant_dynamic-update-slice_fusion.5.v0), channel_id=1, source_target_pairs={{0,2},{2,4},{4,6},{6,0},{8,10},{10,12},{12,14},{14,8},{16,18},{18,... | collective-permute-start | bytes 1572872 | tf_op jit(solution)/shard_map/ppermute | solution.py:189
  60.9 2.3 %copy-start.4 = (bf16[2048,128]{1,0:T(8,128)(2,1)}, bf16[2048,128]{1,0:T(8,128)(2,1)S(1)}, u32[]{:S(2)}) copy-start(bf16[2048,128]{1,0:T(8,128)(2,1)S(1)} %constant_dynamic-update-slice_fusion.k0) | copy-start | bytes 1572868
  60.9 16.4 %collective-permute-start.8 = (bf16[2048,128]{1,0:T(8,128)(2,1)S(1)}, bf16[2048,128]{1,0:T(8,128)(2,1)S(1)}, u32[]{:S(2)}, u32[]{:S(2)}) collective-permute-start(bf16[2048,128]{1,0:T(8,128)(2,1)S(1)} %constant_dynamic-update-slice_fusion.k0), channel_id=1, source_target_pairs={{0,16},{2,18},{4,20},{6,22},{8,24},{10,26},{12,28},{14,30},{16,0},... | collective-permute-start | bytes 1572872 | tf_op jit(solution)/shard_map/ppermute | solution.py:189
  61.0 21.7 %collective-permute-start.7 = (bf16[2048,128]{1,0:T(8,128)(2,1)S(1)}, bf16[2048,128]{1,0:T(8,128)(2,1)S(1)}, u32[]{:S(2)}, u32[]{:S(2)}) collective-permute-start(bf16[2048,128]{1,0:T(8,128)(2,1)S(1)} %constant_dynamic-update-slice_fusion.k0), channel_id=1, source_target_pairs={{0,24},{2,26},{4,28},{6,30},{8,0},{10,2},{12,4},{14,6},{16,8},{18,... | collective-permute-start | bytes 1572872 | tf_op jit(solution)/shard_map/ppermute | solution.py:189
  61.1 2.1 copy-start.5
  61.1 24.7 %collective-permute-start.6 = (bf16[2048,128]{1,0:T(8,128)(2,1)S(1)}, bf16[2048,128]{1,0:T(8,128)(2,1)S(1)}, u32[]{:S(2)}, u32[]{:S(2)}) collective-permute-start(bf16[2048,128]{1,0:T(8,128)(2,1)S(1)} %constant_dynamic-update-slice_fusion.k0), channel_id=1, source_target_pairs={{0,8},{2,10},{4,12},{6,14},{8,16},{10,18},{12,20},{14,22},{16,24},... | collective-permute-start | bytes 1572872 | tf_op jit(solution)/shard_map/ppermute | solution.py:189
  69.6 16.3 %copy-start.6 = (bf16[2048,128]{1,0:T(8,128)(2,1)}, bf16[2048,128]{1,0:T(8,128)(2,1)S(1)}, u32[]{:S(2)}) copy-start(bf16[2048,128]{1,0:T(8,128)(2,1)S(1)} %collective-permute-done.13.v2) | copy-start | bytes 1572868
  74.1 11.7 %copy-start.7 = (bf16[2048,128]{1,0:T(8,128)(2,1)}, bf16[2048,128]{1,0:T(8,128)(2,1)S(1)}, u32[]{:S(2)}) copy-start(bf16[2048,128]{1,0:T(8,128)(2,1)S(1)} %collective-permute-done.12.v1) | copy-start | bytes 1572868
  77.3 8.5 %copy-start.8 = (bf16[2048,128]{1,0:T(8,128)(2,1)}, bf16[2048,128]{1,0:T(8,128)(2,1)S(1)}, u32[]{:S(2)}) copy-start(bf16[2048,128]{1,0:T(8,128)(2,1)S(1)} %collective-permute-done.8.k3) | copy-start | bytes 1572868
  82.7 3.1 %copy-start.9 = (bf16[2048,128]{1,0:T(8,128)(2,1)}, bf16[2048,128]{1,0:T(8,128)(2,1)S(1)}, u32[]{:S(2)}) copy-start(bf16[2048,128]{1,0:T(8,128)(2,1)S(1)} %collective-permute-done.7.k2) | copy-start | bytes 1572868
  85.8 0.8 copy-start.10
  131.4 9.4 %collective-permute-start.29 = (f32[256]{0:T(256)S(1)}, f32[256]{0:T(256)S(1)}, u32[]{:S(2)}, u32[]{:S(2)}) collective-permute-start(f32[256]{0:T(256)S(1)} %select_bitcast_fusion), channel_id=1, source_target_pairs={{0,62},{2,60},{4,58},{6,56},{8,54},{10,52},{12,50},{14,48},{16,46}... | collective-permute-start | bytes 3080 | tf_op jit(solution)/shard_map/ppermute | solution.py:189
  134.4 26.4 %collective-permute-start.16 = (bf16[2048,128]{1,0:T(8,128)(2,1)S(1)}, bf16[2048,128]{1,0:T(8,128)(2,1)S(1)}, u32[]{:S(2)}, u32[]{:S(2)}) collective-permute-start(bf16[2048,128]{1,0:T(8,128)(2,1)S(1)} %get-tuple-element.16), channel_id=1, source_target_pairs={{0,24},{2,26},{4,28},{6,30},{8,0},{10,2},{12,4},{14,6},{16,8},{18,... | collective-permute-start | bytes 1572872 | tf_op jit(solution)/shard_map/ppermute | solution.py:189
  134.4 29.8 %collective-permute-start.17 = (bf16[2048,128]{1,0:T(8,128)(2,1)S(1)}, bf16[2048,128]{1,0:T(8,128)(2,1)S(1)}, u32[]{:S(2)}, u32[]{:S(2)}) collective-permute-start(bf16[2048,128]{1,0:T(8,128)(2,1)S(1)} %get-tuple-element.17), channel_id=1, source_target_pairs={{0,8},{2,10},{4,12},{6,14},{8,16},{10,18},{12,20},{14,22},{16,24},... | collective-permute-start | bytes 1572872 | tf_op jit(solution)/shard_map/ppermute | solution.py:189
  136.5 27.8 %collective-permute-start.18 = (bf16[2048,128]{1,0:T(8,128)(2,1)S(1)}, bf16[2048,128]{1,0:T(8,128)(2,1)S(1)}, u32[]{:S(2)}, u32[]{:S(2)}) collective-permute-start(bf16[2048,128]{1,0:T(8,128)(2,1)S(1)} %get-tuple-element.18), channel_id=1, source_target_pairs={{0,16},{2,18},{4,20},{6,22},{8,24},{10,26},{12,28},{14,30},{16,0},... | collective-permute-start | bytes 1572872 | tf_op jit(solution)/shard_map/ppermute | solution.py:189
  140.8 5.3 %collective-permute-start.30 = (f32[256]{0:T(256)S(1)}, f32[256]{0:T(256)S(1)}, u32[]{:S(2)}, u32[]{:S(2)}) collective-permute-start(f32[256]{0:T(256)S(1)} %bitcast_add_fusion), channel_id=1, source_target_pairs={{0,1},{1,0},{2,3},{3,2},{4,5},{5,4},{6,7},{7,6},{8,9},{9,8},{10,11... | collective-permute-start | bytes 3080 | tf_op jit(solution)/shard_map/ppermute | solution.py:285
  141.4 68.6 %collective-permute-start.15 = (bf16[256,512]{1,0:T(8,128)(2,1)S(1)}, bf16[256,512]{1,0:T(8,128)(2,1)S(1)}, u32[]{:S(2)}, u32[]{:S(2)}) collective-permute-start(bf16[256,512]{1,0:T(8,128)(2,1)S(1)} %broadcast_select_fusion.2), channel_id=1, source_target_pairs={{0,62},{2,60},{4,58},{6,56},{8,54},{10,52},{12,50},{14,48},{16,46}... | collective-permute-start | bytes 786440 | tf_op jit(solution)/shard_map/ppermute | solution.py:189
  146.1 18.6 %collective-permute-start.22 = (bf16[2048,128]{1,0:T(8,128)(2,1)S(1)}, bf16[2048,128]{1,0:T(8,128)(2,1)S(1)}, u32[]{:S(2)}, u32[]{:S(2)}) collective-permute-start(bf16[2048,128]{1,0:T(8,128)(2,1)S(1)} %get-tuple-element.20), channel_id=1, source_target_pairs={{0,6},{2,0},{4,2},{6,4},{8,14},{10,8},{12,10},{14,12},{16,22},{18,... | collective-permute-start | bytes 1572872 | tf_op jit(solution)/shard_map/ppermute | solution.py:189
  160.8 29.0 %collective-permute-start.23 = (bf16[2048,128]{1,0:T(8,128)(2,1)S(1)}, bf16[2048,128]{1,0:T(8,128)(2,1)S(1)}, u32[]{:S(2)}, u32[]{:S(2)}) collective-permute-start(bf16[2048,128]{1,0:T(8,128)(2,1)S(1)} %get-tuple-element.21), channel_id=1, source_target_pairs={{0,2},{2,4},{4,6},{6,0},{8,10},{10,12},{12,14},{14,8},{16,18},{18,... | collective-permute-start | bytes 1572872 | tf_op jit(solution)/shard_map/ppermute | solution.py:189
  164.3 25.6 %collective-permute-start.24 = (bf16[2048,128]{1,0:T(8,128)(2,1)S(1)}, bf16[2048,128]{1,0:T(8,128)(2,1)S(1)}, u32[]{:S(2)}, u32[]{:S(2)}) collective-permute-start(bf16[2048,128]{1,0:T(8,128)(2,1)S(1)} %get-tuple-element.22), channel_id=1, source_target_pairs={{0,4},{2,6},{4,0},{6,2},{8,12},{10,14},{12,8},{14,10},{16,20},{18,... | collective-permute-start | bytes 1572872 | tf_op jit(solution)/shard_map/ppermute | solution.py:189
  164.6 29.1 %collective-permute-start.19 = (bf16[512,128]{1,0:T(8,128)(2,1)S(1)}, bf16[512,128]{1,0:T(8,128)(2,1)S(1)}, u32[]{:S(2)}, u32[]{:S(2)}) collective-permute-start(bf16[512,128]{1,0:T(8,128)(2,1)S(1)} %get-tuple-element.42), channel_id=1, source_target_pairs={{0,6},{2,0},{4,2},{6,4},{8,14},{10,8},{12,10},{14,12},{16,22},{18,... | collective-permute-start | bytes 393224 | tf_op jit(solution)/shard_map/ppermute | solution.py:189
  164.7 29.0 %collective-permute-start.21 = (bf16[512,128]{1,0:T(8,128)(2,1)S(1)}, bf16[512,128]{1,0:T(8,128)(2,1)S(1)}, u32[]{:S(2)}, u32[]{:S(2)}) collective-permute-start(bf16[512,128]{1,0:T(8,128)(2,1)S(1)} %get-tuple-element.43), channel_id=1, source_target_pairs={{0,4},{2,6},{4,0},{6,2},{8,12},{10,14},{12,8},{14,10},{16,20},{18,... | collective-permute-start | bytes 393224 | tf_op jit(solution)/shard_map/ppermute | solution.py:189
  189.9 6.2 %collective-permute-start.20 = (bf16[512,128]{1,0:T(8,128)(2,1)S(1)}, bf16[512,128]{1,0:T(8,128)(2,1)S(1)}, u32[]{:S(2)}, u32[]{:S(2)}) collective-permute-start(bf16[512,128]{1,0:T(8,128)(2,1)S(1)} %get-tuple-element.44), channel_id=1, source_target_pairs={{0,2},{2,4},{4,6},{6,0},{8,10},{10,12},{12,14},{14,8},{16,18},{18,... | collective-permute-start | bytes 393224 | tf_op jit(solution)/shard_map/ppermute | solution.py:189
  190.2 8.0 %collective-permute-start.25 = (bf16[512,128]{1,0:T(8,128)(2,1)S(1)}, bf16[512,128]{1,0:T(8,128)(2,1)S(1)}, u32[]{:S(2)}, u32[]{:S(2)}) collective-permute-start(bf16[512,128]{1,0:T(8,128)(2,1)S(1)} %get-tuple-element.45), channel_id=1, source_target_pairs={{0,24},{2,26},{4,28},{6,30},{8,0},{10,2},{12,4},{14,6},{16,8},{18,... | collective-permute-start | bytes 393224 | tf_op jit(solution)/shard_map/ppermute | solution.py:189
  193.7 6.9 %collective-permute-start.27 = (bf16[512,128]{1,0:T(8,128)(2,1)S(1)}, bf16[512,128]{1,0:T(8,128)(2,1)S(1)}, u32[]{:S(2)}, u32[]{:S(2)}) collective-permute-start(bf16[512,128]{1,0:T(8,128)(2,1)S(1)} %get-tuple-element.46), channel_id=1, source_target_pairs={{0,16},{2,18},{4,20},{6,22},{8,24},{10,26},{12,28},{14,30},{16,0},... | collective-permute-start | bytes 393224 | tf_op jit(solution)/shard_map/ppermute | solution.py:189
  193.7 8.0 %collective-permute-start.26 = (bf16[512,128]{1,0:T(8,128)(2,1)S(1)}, bf16[512,128]{1,0:T(8,128)(2,1)S(1)}, u32[]{:S(2)}, u32[]{:S(2)}) collective-permute-start(bf16[512,128]{1,0:T(8,128)(2,1)S(1)} %get-tuple-element.47), channel_id=1, source_target_pairs={{0,8},{2,10},{4,12},{6,14},{8,16},{10,18},{12,20},{14,22},{16,24},... | collective-permute-start | bytes 393224 | tf_op jit(solution)/shard_map/ppermute | solution.py:189
  201.7 11.7 %collective-permute-start.28 = (bf16[256,256]{1,0:T(8,128)(2,1)S(1)}, bf16[256,256]{1,0:T(8,128)(2,1)S(1)}, u32[]{:S(2)}, u32[]{:S(2)}) collective-permute-start(bf16[256,256]{1,0:T(8,128)(2,1)S(1)} %pad_maximum_fusion.6), channel_id=1, source_target_pairs={{0,62},{2,60},{4,58},{6,56},{8,54},{10,52},{12,50},{14,48},{16,46}... | collective-permute-start | bytes 393224 | tf_op jit(solution)/shard_map/ppermute | solution.py:189

commit v2 on v1

v2 whole, which is shorter than its diff:
```python
import jax
import jax.numpy as jnp
from jax import lax
from jax.experimental import pallas as pl
from jax.experimental.pallas import tpu as pltpu
from jax.sharding import PartitionSpec as P

HEAD_SIZE = 128
BLK = 128
GROUP = 4
LIVE_SLOTS = 64
SCALE = HEAD_SIZE ** (-0.5)
EXP2_SCALE = SCALE * 1.4426950408889634
CHUNK = 1024
TAIL = 512
MASKED = -1.5e38
OFFSETS = (0, -1, 1, 2)
NT = (((1,), (1,)), ((), ()))


def dot_nt(a, b):
    return lax.dot_general(a, b, NT, preferred_element_type=jnp.float32)


def dot_nn(a, b):
    return jnp.dot(a, b, preferred_element_type=jnp.float32)


def block_tables(place, ids, counts, ranks, ktab, vtab, rank, live):
    half, z, y = place // 16, place // 4 % 4, place % 4
    total = lax.fori_loop(0, 32, lambda s, n: n + counts[s], 0)

    def of_shard(s, before):
        both = (counts[s] > 1).astype(jnp.int32)
        later = (ids[2 * s + 1] < ids[2 * s]).astype(jnp.int32) * both
        ranks[2 * s] = before + later
        ranks[2 * s + 1] = jnp.where(both == 1, before + 1 - later, total + 2 * s - before)
        return before + counts[s]

    lax.fori_loop(0, 32, of_shard, 0)

    def low_shard(at):
        return jnp.where(half == 0, at, 15 - at)

    for outer, near in enumerate(OFFSETS):
        for inner, far in enumerate(OFFSETS):
            at = (outer * 4 + inner) * 4
            k_low = low_shard((z + near) % 4 * 4 + (y + far) % 4)
            v_low = low_shard((z + far) % 4 * 4 + (y + near) % 4)
            for slot in range(2):
                ktab[at + slot] = ranks[2 * k_low + slot]
                ktab[at + 2 + slot] = ranks[2 * (31 - k_low) + slot]
                vtab[at + slot] = ranks[2 * v_low + slot]
                vtab[at + 2 + slot] = ranks[2 * (31 - v_low) + slot]
    mine = low_shard(z * 4 + y)
    for i, shard in enumerate((mine, 31 - mine)):
        for slot in range(2):
            rank[2 * i + slot] = ranks[2 * shard + slot]
            live[2 * i + slot] = (slot < counts[shard]).astype(jnp.int32)


def grad_kernel(
    place, ids, counts,
    q, do, k0, k1, k2, k3, k4, v0, v1, v2, v3, v4,
    dq, dk0, dk1, dk2, dk3, dv0, dv1, dv2, dv3, delta_out,
    ktab, vtab, rank, live, ranks,
    kc, vc, kt, qs, dos, dka, dva, dqt, row_max, row_sum, row_dot,
):
    block_tables(place[0], ids, counts, ranks, ktab, vtab, rank, live)
    lanes = GROUP * BLK
    per_piece = LIVE_SLOTS // 4
    first = 0
    for kp, vp in ((k0, v0), (k1, v1), (k2, v2), (k3, v3), (k4, v4)):
        blocks = kp.shape[0] // BLK

        def pack(b, _, kp=kp, vp=vp, first=first):
            at = pl.multiple_of(b * BLK, BLK)
            kd = pl.multiple_of(ktab[first + b] * BLK, BLK)
            vd = pl.multiple_of(vtab[first + b] * BLK, BLK)
            kc[pl.ds(kd, BLK), :] = kp[pl.ds(at, BLK), :]
            vc[pl.ds(vd, BLK), :] = vp[pl.ds(at, BLK), :]
            return 0

        lax.fori_loop(0, blocks, pack, 0, unroll=8)
        first += blocks
    row = lax.broadcasted_iota(jnp.int32, (HEAD_SIZE, HEAD_SIZE), 0)
    col = lax.broadcasted_iota(jnp.int32, (HEAD_SIZE, HEAD_SIZE), 1)
    eye = (row == col).astype(jnp.bfloat16)

    def prepare(c, _):
        here = pl.ds(pl.multiple_of(c * CHUNK, CHUNK), CHUNK)
        kt[:, here] = dot_nt(eye, kc[here, :]).astype(jnp.bfloat16)
        dka[here, :] = jnp.zeros((CHUNK, HEAD_SIZE), jnp.float32)
        dva[here, :] = jnp.zeros((CHUNK, HEAD_SIZE), jnp.float32)
        return 0

    lax.fori_loop(0, LIVE_SLOTS * BLK // CHUNK, prepare, 0)

    def query_block(qb, _):
        rows = pl.ds(pl.multiple_of(qb * BLK, BLK), BLK)

        @pl.when(live[qb] == 0)
        def _():
            dq[rows, :] = jnp.zeros((BLK, lanes), dq.dtype)
            delta_out[pl.ds(qb, 1), :] = jnp.zeros((1, BLK), jnp.float32)

        @pl.when(live[qb] != 0)
        def _():
            my_rank = rank[qb]
            wide = lax.div(my_rank, CHUNK // BLK)
            tail = wide * CHUNK
            short = my_rank - wide * (CHUNK // BLK) < TAIL // BLK
            for h in range(GROUP):
                cols = slice(h * HEAD_SIZE, (h + 1) * HEAD_SIZE)
                qs[cols, :] = q[rows, cols]
                dos[cols, :] = do[rows, cols]

            def allowed(at, size):
                key_at = at + lax.broadcasted_iota(jnp.int32, (size, lanes), 0)
                lane = lax.broadcasted_iota(jnp.int32, (size, lanes), 1)
                return key_at <= my_rank * BLK + (lane & (BLK - 1))

            def stats(at, size, masked):
                here = pl.ds(pl.multiple_of(at, TAIL), size)
                s = dot_nt(kc[here, :], qs[...])
                dp = dot_nt(vc[here, :], dos[...])
                if masked:
                    s = jnp.where(allowed(at, size), s, MASKED)
                s = s.reshape(size // 8, 8, lanes)
                dp = dp.reshape(size // 8, 8, lanes)
                m, l, w = row_max[...], row_sum[...], row_dot[...]
                mn = jnp.maximum(m, jnp.max(s, axis=0))
                p = jnp.exp2((s - mn[None]) * EXP2_SCALE)
                alpha = jnp.exp2((m - mn) * EXP2_SCALE)
                row_max[...] = mn
                row_sum[...] = l * alpha + jnp.sum(p, axis=0)
                row_dot[...] = w * alpha + jnp.sum(p * dp, axis=0)

            row_max[...] = jnp.full((8, lanes), MASKED, jnp.float32)
            row_sum[...] = jnp.zeros((8, lanes), jnp.float32)
            row_dot[...] = jnp.zeros((8, lanes), jnp.float32)

            def stats_turn(c, _):
                stats(c * CHUNK, CHUNK, False)
                return 0

            lax.fori_loop(0, wide, stats_turn, 0)
            pl.when(short)(lambda: stats(tail, TAIL, True))
            pl.when(jnp.logical_not(short))(lambda: stats(tail, CHUNK, True))
            m = row_max[...]
            top = jnp.max(m, axis=0, keepdims=True)
            fix = jnp.exp2((m - top) * EXP2_SCALE)
            total = jnp.sum(row_sum[...] * fix, axis=0, keepdims=True)
            delta = jnp.sum(row_dot[...] * fix, axis=0, keepdims=True) / total
            lse = top * EXP2_SCALE + jnp.log2(total)
            delta_out[pl.ds(qb, 1), :] = (
                delta[:, 0:128] + delta[:, 128:256] + delta[:, 256:384] + delta[:, 384:512]
            )
            dqt[...] = jnp.zeros_like(dqt)

            def grads(at, size, masked):
                here = pl.ds(pl.multiple_of(at, TAIL), size)
                s = dot_nt(kc[here, :], qs[...])
                dp = dot_nt(vc[here, :], dos[...])
                p = jnp.exp2(s * EXP2_SCALE - lse)
                if masked:
                    p = jnp.where(allowed(at, size), p, 0.0)
                ds = (p * (dp - delta)).astype(jnp.bfloat16)
                dva[here, :] += dot_nn(p.astype(jnp.bfloat16), dos[...])
                dka[here, :] += dot_nn(ds, qs[...])
                dqt[...] += dot_nn(kt[:, here], ds)

            def grads_turn(c, _):
                grads(c * CHUNK, CHUNK, False)
                return 0

            lax.fori_loop(0, wide, grads_turn, 0)
            pl.when(short)(lambda: grads(tail, TAIL, True))
            pl.when(jnp.logical_not(short))(lambda: grads(tail, CHUNK, True))
            for h in range(GROUP):
                cols = slice(h * HEAD_SIZE, (h + 1) * HEAD_SIZE)
                dq[rows, cols] = (dqt[:, cols].T * SCALE).astype(dq.dtype)

        return 0

    lax.fori_loop(0, 4, query_block, 0)
    for piece, (dkp, dvp) in enumerate(((dk0, dv0), (dk1, dv1), (dk2, dv2), (dk3, dv3))):

        def unpack(b, _, dkp=dkp, dvp=dvp, piece=piece):
            at = pl.multiple_of(b * BLK, BLK)
            kd = pl.multiple_of(ktab[piece * per_piece + b] * BLK, BLK)
            vd = pl.multiple_of(vtab[piece * per_piece + b] * BLK, BLK)
            dkp[pl.ds(at, BLK), :] = (dka[pl.ds(kd, BLK), :] * SCALE).astype(dkp.dtype)
            dvp[pl.ds(at, BLK), :] = dva[pl.ds(vd, BLK), :].astype(dvp.dtype)
            return 0

        lax.fori_loop(0, per_piece, unpack, 0, unroll=8)


def grad_call(place, ids, counts, q, do, ks, vs):
    bf = jnp.bfloat16
    piece = jax.ShapeDtypeStruct(ks[0].shape, bf)
    keys = 4 * ks[0].shape[0]
    lanes = GROUP * BLK
    vm = pl.BlockSpec(memory_space=pltpu.VMEM)
    sm = pl.BlockSpec(memory_space=pltpu.SMEM)
    out = pl.pallas_call(
        grad_kernel,
        out_shape=(jax.ShapeDtypeStruct(q.shape, bf),) + (piece,) * 8
        + (jax.ShapeDtypeStruct((4, BLK), jnp.float32),),
        in_specs=[sm] * 3 + [vm] * 12,
        out_specs=(vm,) * 10,
        scratch_shapes=[
            pltpu.SMEM((LIVE_SLOTS,), jnp.int32),
            pltpu.SMEM((LIVE_SLOTS,), jnp.int32),
            pltpu.SMEM((4,), jnp.int32),
            pltpu.SMEM((4,), jnp.int32),
            pltpu.SMEM((LIVE_SLOTS,), jnp.int32),
            pltpu.VMEM((keys, HEAD_SIZE), bf),
            pltpu.VMEM((keys, HEAD_SIZE), bf),
            pltpu.VMEM((HEAD_SIZE, keys), bf),
            pltpu.VMEM((lanes, HEAD_SIZE), bf),
            pltpu.VMEM((lanes, HEAD_SIZE), bf),
            pltpu.VMEM((keys, HEAD_SIZE), jnp.float32),
            pltpu.VMEM((keys, HEAD_SIZE), jnp.float32),
            pltpu.VMEM((HEAD_SIZE, lanes), jnp.float32),
            pltpu.VMEM((8, lanes), jnp.float32),
            pltpu.VMEM((8, lanes), jnp.float32),
            pltpu.VMEM((8, lanes), jnp.float32),
        ],
        compiler_params=pltpu.CompilerParams(vmem_limit_bytes=40 * 1024 * 1024),
        name="attention_grads",
    )(place, ids, counts, q, do, *ks, *vs)
    return out[0], out[1:5], out[5:9], out[9]


def ring_perms(axis):
    def place(s, step):
        x, z, y = s // 16, s // 4 % 4, s % 4
        if axis == "z":
            z = (z + step) % 4
        else:
            y = (y + step) % 4
        return 16 * x + 4 * z + y

    return {step: [(s, place(s, step)) for s in range(32)] for step in (1, -1, 2, -2)}


Z_RING, Y_RING = ring_perms("z"), ring_perms("y")
PAIR = [(s, 31 - s) for s in range(32)]


def send(a, perm):
    return lax.ppermute(a, "seq", perm)


def in_step(*arrays):
    return lax.optimization_barrier(arrays)


def exchange(pairs):
    arrays = in_step(*[a for a, _ in pairs])
    return in_step(*[send(a, perm) for a, (_, perm) in zip(arrays, pairs)])


def ring_exchange(first_up, second_up, first_down, second_down, first_ring, second_ring):
    return exchange(
        [
            (first_up, first_ring[1]),
            (second_up, second_ring[1]),
            (first_down, first_ring[-1]),
            (second_down, second_ring[-1]),
        ]
    )


def all_directions(first_parts, second_parts, first_ring, second_ring):
    pairs = []
    for step in (2, 1, -1):
        pairs += [(first_parts[step], first_ring[step]), (second_parts[step], second_ring[step])]
    got = exchange(pairs)
    return got[0::2], got[1::2]


def gather_near(first, first_ring, second, second_ring):
    (f_far, f_prev, f_next), (s_far, s_prev, s_next) = all_directions(
        {step: first for step in (1, -1, 2)}, {step: second for step in (1, -1, 2)},
        first_ring, second_ring,
    )
    return [first, f_prev, f_next, f_far], [second, s_prev, s_next, s_far]


def gather_far(first, first_ring, second, second_ring):
    half = first.shape[0] // 2
    f_prev, s_prev, f_next, s_next = ring_exchange(
        first, second, first, second, first_ring, second_ring
    )
    f_far, s_far, f_end, s_end = ring_exchange(
        f_prev[:half], s_prev[:half], f_next[half:], s_next[half:], first_ring, second_ring
    )
    return [first, f_prev, f_next, f_far, f_end], [second, s_prev, s_next, s_far, s_end]


def total(*parts):
    return sum(a.astype(jnp.float32) for a in parts).astype(jnp.bfloat16)


def scatter_far(first, first_ring, second, second_ring, beside):
    half = first[0].shape[0] // 2

    def joined(kept, added, via):
        lower, upper = kept[:half], kept[half:]
        if via == 0:
            return jnp.concatenate([total(lower, added), upper], axis=0)
        return jnp.concatenate([lower, total(upper, added)], axis=0)

    f_up, s_up, f_down, s_down = ring_exchange(
        first[3][:half], second[3][:half], first[3][half:], second[3][half:],
        first_ring, second_ring,
    )
    f_up, s_up, f_down, s_down, *beside = in_step(f_up, s_up, f_down, s_down, *beside)
    f_prev, s_prev, f_next, s_next = ring_exchange(
        joined(first[2], f_up, 0), joined(second[2], s_up, 0),
        joined(first[1], f_down, 1), joined(second[1], s_down, 1),
        first_ring, second_ring,
    )
    return total(first[0], f_prev, f_next), total(second[0], s_prev, s_next), beside


def scatter_near(first, first_ring, second, second_ring):
    f_got, s_got = all_directions(
        {-1: first[1], 1: first[2], 2: first[3]}, {-1: second[1], 1: second[2], 2: second[3]},
        first_ring, second_ring,
    )
    return total(first[0], *f_got), total(second[0], *s_got)


def local(
    queries, routed_key_rows, routed_value_rows, grad_out, gate_logit, block_ids, block_counts
):
    bf = jnp.bfloat16
    rows = queries.shape[0]
    seq_index = lax.axis_index("seq")
    half = seq_index // 16
    low = half == 0

    def halves(a):
        width = a.shape[1] // 2
        left, right = a[:, :width], a[:, width:]
        return jnp.where(low, left, right), jnp.where(low, right, left)

    def rows_of(own, other):
        return jnp.concatenate([jnp.where(low, own, other), jnp.where(low, other, own)], axis=0)

    def columns_of(own, other):
        return jnp.concatenate([jnp.where(low, own, other), jnp.where(low, other, own)], axis=1)

    gate = jax.nn.sigmoid(gate_logit)
    out_grad = (gate[:, None] * grad_out.astype(jnp.float32)).astype(bf)
    k_own, k_other = halves(routed_key_rows)
    v_own, v_other = halves(routed_value_rows)
    kv_in = send(jnp.concatenate([k_other, v_other], axis=1), PAIR)
    q_own, q_other = halves(queries)
    d_own, d_other = halves(out_grad)
    qd_in = send(jnp.concatenate([q_other, d_other], axis=1), PAIR)
    keys = rows_of(k_own, kv_in[:, :HEAD_SIZE])
    values = rows_of(v_own, kv_in[:, HEAD_SIZE:])
    k_near, v_near = gather_near(keys, Y_RING, values, Z_RING)
    k_pieces, v_pieces = gather_far(
        jnp.concatenate(k_near, axis=0), Z_RING, jnp.concatenate(v_near, axis=0), Y_RING
    )
    q_all = rows_of(q_own, qd_in[:, : GROUP * HEAD_SIZE])
    d_all = rows_of(d_own, qd_in[:, GROUP * HEAD_SIZE :])
    dq, dk_pieces, dv_pieces, delta = grad_call(
        seq_index.reshape(1), block_ids.reshape(-1), block_counts, q_all, d_all, k_pieces, v_pieces
    )

    def split(a):
        return [a[i * 2 * rows : (i + 1) * 2 * rows] for i in range(4)]

    def own_other(a):
        return jnp.where(low, a[:rows], a[rows:]), jnp.where(low, a[rows:], a[:rows])

    delta_own, delta_other = own_other(delta.reshape(-1))
    dq_own, dq_other = own_other(dq)
    dk, dv, (dq_other, delta_other) = scatter_far(
        dk_pieces, Z_RING, dv_pieces, Y_RING, (dq_other, delta_other)
    )
    dq_in = send(dq_other, PAIR)
    delta_sum = delta_own + send(delta_other, PAIR)
    delta_sum = delta_sum + lax.ppermute(delta_sum, "tensor", [(0, 1), (1, 0)])
    dk, dv = scatter_near(split(dk), Y_RING, split(dv), Z_RING)
    dk_own, dk_other = own_other(dk)
    dv_own, dv_other = own_other(dv)
    back = send(jnp.concatenate([dk_other, dv_other], axis=1), PAIR)
    query_grads = columns_of(dq_own, dq_in)
    key_grads = columns_of(dk_own, back[:, :HEAD_SIZE])
    value_grads = columns_of(dv_own, back[:, HEAD_SIZE:])
    return query_grads, key_grads, value_grads, (1.0 - gate) * delta_sum


def solution(mesh):
    in_specs = (
        P(("dp", "seq"), "tensor"),
        P(("dp", "seq"), "tensor"),
        P(("dp", "seq"), "tensor"),
        P(("dp", "seq"), "tensor"),
        P(("dp", "seq")),
        P("dp", None),
        P("dp"),
    )
    out_specs = (
        P(("dp", "seq"), "tensor"),
        P(("dp", "seq"), "tensor"),
        P(("dp", "seq"), "tensor"),
        P(("dp", "seq")),
    )
    return jax.shard_map(local, mesh=mesh, in_specs=in_specs, out_specs=out_specs, check_vma=False)
```

time: 216 us -> 161 us (0.75); the launches traced: 215 us -> 163 us
  waiting for transfers between devices: 102 us -> 41.7 us
  starting transfers between devices: 55.1 us -> 73.5 us
  Pallas kernels: 44.8 us -> 38.6 us
    ppermute x30 -> x33, waiting for transfers between devices: 102 us -> 41.7 us  [send(): return lax.ppermute(a, 'seq', perm)]
    ppermute x30 -> x33, starting transfers between devices: 54.5 us -> 72.2 us  [send(): return lax.ppermute(a, 'seq', perm)]
    pallas_call x1, Pallas kernels: 44.8 us -> 38.6 us  [grad_call(): pl.pallas_call(grad_kernel, out_shape=(jax.ShapeDtypeStruct(q.shape, bf),...]
  transfers between devices with their start and end apart: 31 -> 34, of which waited for: 18 -> 18; matrix products, arithmetic and copies ran while one was open for 3% -> 3% of each run, Pallas kernels for 0% -> 0%
where the time goes in v2:
time: 161 us; the launch traced here: 163 us
  starting transfers between devices  73.5 us (46%)
  waiting for transfers between devices  41.7 us (26%)
  Pallas kernels  38.6 us (24%)
  other arithmetic  7.36 us (5%)
    ppermute x33, starting transfers between devices, send(): return lax.ppermute(a, 'seq', perm)  72.2 us
    ppermute x33, waiting for transfers between devices, send(): return lax.ppermute(a, 'seq', perm)  41.7 us
    pallas_call x1, Pallas kernels, grad_call(): pl.pallas_call(grad_kernel, out_shape=(jax.ShapeDtypeStruct(q.shape, bf),...  38.6 us
  transfers between devices with their start and end apart: 34, of which 18 were waited for; matrix products, arithmetic and copies ran while one was open for 3% of the time, Pallas kernels for 0%

profile of v2, /device:TPU:0, one launch (start us, length us, event | category | flops | bytes accessed | tf_op | source)
XLA Modules:
  0.0 163.2 jit_solution(11796780891080395146)
XLA Ops:
  0.7 1.0 broadcast_select_fusion.25
  1.7 9.1 %collective-permute-start.1 = (bf16[256,256]{1,0:T(8,128)(2,1)S(1)}, bf16[256,256]{1,0:T(8,128)(2,1)S(1)}, u32[]{:S(2)}, u32[]{:S(2)}) collective-permute-start(bf16[256,256]{1,0:T(8,128)(2,1)S(1)} %pad_maximum_fusion.8), channel_id=1, source_target_pairs={{0,62},{2,60},{4,58},{6,56},{8,54},{10,52},{12,50},{14,48},{16,46}... | collective-permute-start | bytes 393224 | tf_op jit(solution)/shard_map/ppermute | solution.py:254
  10.8 3.5 %collective-permute-done.1 = bf16[256,256]{1,0:T(8,128)(2,1)S(1)} collective-permute-done((bf16[256,256]{1,0:T(8,128)(2,1)S(1)}, bf16[256,256]{1,0:T(8,128)(2,1)S(1)}, u32[]{:S(2)}, u32[]{:S(2)}) %collective-permute-start.1) | collective-permute-done | bytes 131104 | tf_op jit(solution)/shard_map/ppermute | solution.py:254
  14.5 0.7 collective-permute-start.2
  15.6 2.4 %collective-permute-start.3 = (bf16[512,128]{1,0:T(8,128)(2,1)S(1)}, bf16[512,128]{1,0:T(8,128)(2,1)S(1)}, u32[]{:S(2)}, u32[]{:S(2)}) collective-permute-start(bf16[512,128]{1,0:T(8,128)(2,1)S(1)} %pad_maximum_fusion.10), channel_id=1, source_target_pairs={{0,16},{2,18},{4,20},{6,22},{8,24},{10,26},{12,28},{14,30},{16,0},... | collective-permute-start | bytes 393224 | tf_op jit(solution)/shard_map/ppermute | solution.py:254
  18.0 1.9 %collective-permute-start.4 = (bf16[512,128]{1,0:T(8,128)(2,1)S(1)}, bf16[512,128]{1,0:T(8,128)(2,1)S(1)}, u32[]{:S(2)}, u32[]{:S(2)}) collective-permute-start(bf16[512,128]{1,0:T(8,128)(2,1)S(1)} %pad_maximum_fusion.9), channel_id=1, source_target_pairs={{0,2},{2,4},{4,6},{6,0},{8,10},{10,12},{12,14},{14,8},{16,18},{18,... | collective-permute-start | bytes 393224 | tf_op jit(solution)/shard_map/ppermute | solution.py:254
  19.9 2.2 %collective-permute-start.5 = (bf16[512,128]{1,0:T(8,128)(2,1)S(1)}, bf16[512,128]{1,0:T(8,128)(2,1)S(1)}, u32[]{:S(2)}, u32[]{:S(2)}) collective-permute-start(bf16[512,128]{1,0:T(8,128)(2,1)S(1)} %pad_maximum_fusion.10), channel_id=1, source_target_pairs={{0,8},{2,10},{4,12},{6,14},{8,16},{10,18},{12,20},{14,22},{16,24},... | collective-permute-start | bytes 393224 | tf_op jit(solution)/shard_map/ppermute | solution.py:254
  22.1 1.3 collective-permute-start.6
  23.4 1.5 collective-permute-start.7
  25.0 1.1 collective-permute-done.5
  26.0 1.0 collective-permute-done.6
  27.1 1.4 collective-permute-done.7
  28.7 0.7 collective-permute-start.9
  29.4 3.2 %collective-permute-start.10 = (bf16[2048,128]{1,0:T(8,128)(2,1)S(1)}, bf16[2048,128]{1,0:T(8,128)(2,1)S(1)}, u32[]{:S(2)}, u32[]{:S(2)}) collective-permute-start(bf16[2048,128]{1,0:T(8,128)(2,1)S(1)} %constant_dynamic-update-slice_fusion.k0), channel_id=1, source_target_pairs={{0,24},{2,26},{4,28},{6,30},{8,0},{10,2},{12,4},{14,6},{16,8},{18,... | collective-permute-start | bytes 1572872 | tf_op jit(solution)/shard_map/ppermute | solution.py:254
  32.6 2.6 %collective-permute-start.11 = (bf16[2048,128]{1,0:T(8,128)(2,1)S(1)}, bf16[2048,128]{1,0:T(8,128)(2,1)S(1)}, u32[]{:S(2)}, u32[]{:S(2)}) collective-permute-start(bf16[2048,128]{1,0:T(8,128)(2,1)S(1)} %constant_dynamic-update-slice_fusion.5.v0), channel_id=1, source_target_pairs={{0,6},{2,0},{4,2},{6,4},{8,14},{10,8},{12,10},{14,12},{16,22},{18,... | collective-permute-start | bytes 1572872 | tf_op jit(solution)/shard_map/ppermute | solution.py:254
  35.1 0.9 pad_maximum_fusion
  36.0 4.2 %collective-permute-start = (bf16[256,1024]{1,0:T(8,128)(2,1)}, bf16[256,1024]{1,0:T(8,128)(2,1)}, u32[]{:S(2)}, u32[]{:S(2)}) collective-permute-start(bf16[256,1024]{1,0:T(8,128)(2,1)} %pad_maximum_fusion), channel_id=1, source_target_pairs={{0,62},{2,60},{4,58},{6,56},{8,54},{10,52},{12,50},{14,48},{16,46}... | collective-permute-start | bytes 1572872 | tf_op jit(solution)/shard_map/ppermute | solution.py:254
  40.4 11.2 %collective-permute-done.8.k1 = bf16[2048,128]{1,0:T(8,128)(2,1)S(1)} collective-permute-done((bf16[2048,128]{1,0:T(8,128)(2,1)S(1)}, bf16[2048,128]{1,0:T(8,128)(2,1)S(1)}, u32[]{:S(2)}, u32[]{:S(2)}) %collective-permute-start.8) | collective-permute-done | bytes 524320 | tf_op jit(solution)/shard_map/ppermute | solution.py:254
  52.0 1.5 collective-permute-done.11.v2
  53.8 1.0 collective-permute-start.13
  54.8 3.2 %collective-permute-start.14 = (bf16[1024,128]{1,0:T(8,128)(2,1)S(1)}, bf16[1024,128]{1,0:T(8,128)(2,1)S(1)}, u32[]{:S(2)}, u32[]{:S(2)}) collective-permute-start(bf16[1024,128]{1,0:T(8,128)(2,1)S(1)} %slice.162), channel_id=1, source_target_pairs={{0,24},{2,26},{4,28},{6,30},{8,0},{10,2},{12,4},{14,6},{16,8},{18,... | collective-permute-start | bytes 786440 | tf_op jit(solution)/shard_map/ppermute | solution.py:254
  58.0 2.7 %collective-permute-start.15 = (bf16[1024,128]{1,0:T(8,128)(2,1)S(1)}, bf16[1024,128]{1,0:T(8,128)(2,1)S(1)}, u32[]{:S(2)}, u32[]{:S(2)}) collective-permute-start(bf16[1024,128]{1,0:T(8,128)(2,1)S(1)} %slice.163), channel_id=1, source_target_pairs={{0,6},{2,0},{4,2},{6,4},{8,14},{10,8},{12,10},{14,12},{16,22},{18,... | collective-permute-start | bytes 786440 | tf_op jit(solution)/shard_map/ppermute | solution.py:254
  60.7 1.1 broadcast_select_fusion.5
  62.0 2.6 %collective-permute-done.15.v4 = bf16[1024,128]{1,0:T(8,128)(2,1)S(1)} collective-permute-done((bf16[1024,128]{1,0:T(8,128)(2,1)S(1)}, bf16[1024,128]{1,0:T(8,128)(2,1)S(1)}, u32[]{:S(2)}, u32[]{:S(2)}) %collective-permute-start.15) | collective-permute-done | bytes 262176 | tf_op jit(solution)/shard_map/ppermute | solution.py:254
  64.6 38.6 %attention_grads.1 = (bf16[512,512]{1,0:T(8,128)(2,1)S(1)}, bf16[2048,128]{1,0:T(8,128)(2,1)S(1)}, bf16[2048,128]{1,0:T(8,128)(2,1)S(1)}, bf16[2048,128]{1,0:T(8...) custom-call(s32[1]{0:T(128)} %bitcast.place, ...), custom_call_target="tpu_custom_call" | custom-call | tf_op jit(solution)/shard_map/attention_grads/pallas_call | solution.py:207
  103.4 2.0 %collective-permute-start.17 = (bf16[1024,128]{1,0:T(8,128)(2,1)S(1)}, bf16[1024,128]{1,0:T(8,128)(2,1)S(1)}, u32[]{:S(2)}, u32[]{:S(2)}) collective-permute-start(bf16[1024,128]{1,0:T(8,128)(2,1)S(1)} %get-tuple-element.108), channel_id=1, source_target_pairs={{0,2},{2,4},{4,6},{6,0},{8,10},{10,12},{12,14},{14,8},{16,18},{18,... | collective-permute-start | bytes 786440 | tf_op jit(solution)/shard_map/ppermute | solution.py:254
  105.3 3.2 %collective-permute-start.18 = (bf16[1024,128]{1,0:T(8,128)(2,1)S(1)}, bf16[1024,128]{1,0:T(8,128)(2,1)S(1)}, u32[]{:S(2)}, u32[]{:S(2)}) collective-permute-start(bf16[1024,128]{1,0:T(8,128)(2,1)S(1)} %get-tuple-element.109), channel_id=1, source_target_pairs={{0,24},{2,26},{4,28},{6,30},{8,0},{10,2},{12,4},{14,6},{16,8},{18,... | collective-permute-start | bytes 786440 | tf_op jit(solution)/shard_map/ppermute | solution.py:254
  108.5 1.3 collective-permute-start.19
  110.0 3.7 %collective-permute-done.16 = bf16[1024,128]{1,0:T(8,128)(2,1)S(1)} collective-permute-done((bf16[1024,128]{1,0:T(8,128)(2,1)S(1)}, bf16[1024,128]{1,0:T(8,128)(2,1)S(1)}, u32[]{:S(2)}, u32[]{:S(2)}) %collective-permute-start.16) | collective-permute-done | bytes 262176 | tf_op jit(solution)/shard_map/ppermute | solution.py:254
  113.8 1.3 collective-permute-done.18
  115.1 2.6 %collective-permute-done.19 = bf16[1024,128]{1,0:T(8,128)(2,1)S(1)} collective-permute-done((bf16[1024,128]{1,0:T(8,128)(2,1)S(1)}, bf16[1024,128]{1,0:T(8,128)(2,1)S(1)}, u32[]{:S(2)}, u32[]{:S(2)}) %collective-permute-start.19) | collective-permute-done | bytes 262176 | tf_op jit(solution)/shard_map/ppermute | solution.py:254
  118.4 3.1 %collective-permute-start.23 = (bf16[2048,128]{1,0:T(8,128)(2,1)S(1)}, bf16[2048,128]{1,0:T(8,128)(2,1)S(1)}, u32[]{:S(2)}, u32[]{:S(2)}) collective-permute-start(bf16[2048,128]{1,0:T(8,128)(2,1)S(1)} %pad_maximum_fusion.6), channel_id=1, source_target_pairs={{0,24},{2,26},{4,28},{6,30},{8,0},{10,2},{12,4},{14,6},{16,8},{18,... | collective-permute-start | bytes 1572872 | tf_op jit(solution)/shard_map/ppermute | solution.py:254
  121.5 3.2 %collective-permute-start.24 = (bf16[2048,128]{1,0:T(8,128)(2,1)S(1)}, bf16[2048,128]{1,0:T(8,128)(2,1)S(1)}, u32[]{:S(2)}, u32[]{:S(2)}) collective-permute-start(bf16[2048,128]{1,0:T(8,128)(2,1)S(1)} %pad_maximum_fusion.7), channel_id=1, source_target_pairs={{0,6},{2,0},{4,2},{6,4},{8,14},{10,8},{12,10},{14,12},{16,22},{18,... | collective-permute-start | bytes 1572872 | tf_op jit(solution)/shard_map/ppermute | solution.py:254
  124.8 3.2 %collective-permute-start.32 = (f32[256]{0:T(256)S(1)}, f32[256]{0:T(256)S(1)}, u32[]{:S(2)}, u32[]{:S(2)}) collective-permute-start(f32[256]{0:T(256)S(1)} %select_bitcast_fusion), channel_id=1, source_target_pairs={{0,62},{2,60},{4,58},{6,56},{8,54},{10,52},{12,50},{14,48},{16,46}... | collective-permute-start | bytes 3080 | tf_op jit(solution)/shard_map/ppermute | solution.py:254
  128.0 3.1 %collective-permute-done.21 = bf16[2048,128]{1,0:T(8,128)(2,1)S(1)} collective-permute-done((bf16[2048,128]{1,0:T(8,128)(2,1)S(1)}, bf16[2048,128]{1,0:T(8,128)(2,1)S(1)}, u32[]{:S(2)}, u32[]{:S(2)}) %collective-permute-start.21) | collective-permute-done | bytes 524320 | tf_op jit(solution)/shard_map/ppermute | solution.py:254
  131.6 1.3 collective-permute-done.24
  133.4 3.3 %collective-permute-start.25 = (bf16[512,128]{1,0:T(8,128)(2,1)S(1)}, bf16[512,128]{1,0:T(8,128)(2,1)S(1)}, u32[]{:S(2)}, u32[]{:S(2)}) collective-permute-start(bf16[512,128]{1,0:T(8,128)(2,1)S(1)} %get-tuple-element.135), channel_id=1, source_target_pairs={{0,4},{2,6},{4,0},{6,2},{8,12},{10,14},{12,8},{14,10},{16,20},{18,... | collective-permute-start | bytes 393224 | tf_op jit(solution)/shard_map/ppermute | solution.py:254
  136.7 1.3 collective-permute-start.33
  138.0 4.6 %collective-permute-start.27 = (bf16[512,128]{1,0:T(8,128)(2,1)S(1)}, bf16[512,128]{1,0:T(8,128)(2,1)S(1)}, u32[]{:S(2)}, u32[]{:S(2)}) collective-permute-start(bf16[512,128]{1,0:T(8,128)(2,1)S(1)} %get-tuple-element.137), channel_id=1, source_target_pairs={{0,2},{2,4},{4,6},{6,0},{8,10},{10,12},{12,14},{14,8},{16,18},{18,... | collective-permute-start | bytes 393224 | tf_op jit(solution)/shard_map/ppermute | solution.py:254
  142.6 1.7 %collective-permute-start.29 = (bf16[512,128]{1,0:T(8,128)(2,1)S(1)}, bf16[512,128]{1,0:T(8,128)(2,1)S(1)}, u32[]{:S(2)}, u32[]{:S(2)}) collective-permute-start(bf16[512,128]{1,0:T(8,128)(2,1)S(1)} %get-tuple-element.139), channel_id=1, source_target_pairs={{0,6},{2,0},{4,2},{6,4},{8,14},{10,8},{12,10},{14,12},{16,22},{18,... | collective-permute-start | bytes 393224 | tf_op jit(solution)/shard_map/ppermute | solution.py:254
  144.3 1.6 collective-permute-start.30
  146.5 4.3 %collective-permute-start.20 = (bf16[256,512]{1,0:T(8,128)(2,1)S(1)}, bf16[256,512]{1,0:T(8,128)(2,1)S(1)}, u32[]{:S(2)}, u32[]{:S(2)}) collective-permute-start(bf16[256,512]{1,0:T(8,128)(2,1)S(1)} %broadcast_select_fusion.2), channel_id=1, source_target_pairs={{0,62},{2,60},{4,58},{6,56},{8,54},{10,52},{12,50},{14,48},{16,46}... | collective-permute-start | bytes 786440 | tf_op jit(solution)/shard_map/ppermute | solution.py:254
  151.1 3.5 %collective-permute-start.31 = (bf16[256,256]{1,0:T(8,128)(2,1)S(1)}, bf16[256,256]{1,0:T(8,128)(2,1)S(1)}, u32[]{:S(2)}, u32[]{:S(2)}) collective-permute-start(bf16[256,256]{1,0:T(8,128)(2,1)S(1)} %pad_maximum_fusion.11), channel_id=1, source_target_pairs={{0,62},{2,60},{4,58},{6,56},{8,54},{10,52},{12,50},{14,48},{16,46}... | collective-permute-start | bytes 393224 | tf_op jit(solution)/shard_map/ppermute | solution.py:254
  154.6 4.0 %collective-permute-done.20 = bf16[256,512]{1,0:T(8,128)(2,1)S(1)} collective-permute-done((bf16[256,512]{1,0:T(8,128)(2,1)S(1)}, bf16[256,512]{1,0:T(8,128)(2,1)S(1)}, u32[]{:S(2)}, u32[]{:S(2)}) %collective-permute-start.20) | collective-permute-done | bytes 262176 | tf_op jit(solution)/shard_map/ppermute | solution.py:254
  158.7 0.9 pad_maximum_fusion.3
  159.5 2.3 %collective-permute-done.31 = bf16[256,256]{1,0:T(8,128)(2,1)S(1)} collective-permute-done((bf16[256,256]{1,0:T(8,128)(2,1)S(1)}, bf16[256,256]{1,0:T(8,128)(2,1)S(1)}, u32[]{:S(2)}, u32[]{:S(2)}) %collective-permute-start.31) | collective-permute-done | bytes 131104 | tf_op jit(solution)/shard_map/ppermute | solution.py:254
  161.9 0.7 pad_maximum_fusion.13
  162.5 0.7 pad_maximum_fusion.12
  (98 shorter events, 4.5 us)
Async XLA Ops:
  0.6 10.1 %copy-start.8 = (f32[256]{0:T(256)S(1)}, f32[256]{0:T(256)}, u32[]{:S(2)}) copy-start(f32[256]{0:T(256)} %param.11) | copy-start | bytes 3076
  1.6 12.7 %copy-start.5 = (bf16[256,256]{1,0:T(8,128)(2,1)S(1)}, bf16[256,256]{1,0:T(8,128)(2,1)}, u32[]{:S(2)}) copy-start(bf16[256,256]{1,0:T(8,128)(2,1)} %param.9) | copy-start | bytes 393220
  1.6 12.6 %copy-start.6 = (bf16[256,256]{1,0:T(8,128)(2,1)S(1)}, bf16[256,256]{1,0:T(8,128)(2,1)}, u32[]{:S(2)}) copy-start(bf16[256,256]{1,0:T(8,128)(2,1)} %param.8) | copy-start | bytes 393220
  1.7 12.6 %collective-permute-start.1 = (bf16[256,256]{1,0:T(8,128)(2,1)S(1)}, bf16[256,256]{1,0:T(8,128)(2,1)S(1)}, u32[]{:S(2)}, u32[]{:S(2)}) collective-permute-start(bf16[256,256]{1,0:T(8,128)(2,1)S(1)} %pad_maximum_fusion.8), channel_id=1, source_target_pairs={{0,62},{2,60},{4,58},{6,56},{8,54},{10,52},{12,50},{14,48},{16,46}... | collective-permute-start | bytes 393224 | tf_op jit(solution)/shard_map/ppermute | solution.py:254
  14.3 1.0 copy-start.7
  14.5 10.4 %copy-start.3 = (bf16[256,1024]{1,0:T(8,128)(2,1)S(1)}, bf16[256,1024]{1,0:T(8,128)(2,1)}, u32[]{:S(2)}) copy-start(bf16[256,1024]{1,0:T(8,128)(2,1)} %param.7) | copy-start | bytes 1572868
  14.5 9.0 %collective-permute-start.2 = (bf16[512,128]{1,0:T(8,128)(2,1)S(1)}, bf16[512,128]{1,0:T(8,128)(2,1)S(1)}, u32[]{:S(2)}, u32[]{:S(2)}) collective-permute-start(bf16[512,128]{1,0:T(8,128)(2,1)S(1)} %pad_maximum_fusion.9), channel_id=1, source_target_pairs={{0,4},{2,6},{4,0},{6,2},{8,12},{10,14},{12,8},{14,10},{16,20},{18,... | collective-permute-start | bytes 393224 | tf_op jit(solution)/shard_map/ppermute | solution.py:254
  15.5 9.4 %copy-start.1 = (bf16[256,1024]{1,0:T(8,128)(2,1)}, bf16[256,1024]{1,0:T(8,128)(2,1)S(1)}, u32[]{:S(2)}) copy-start(bf16[256,1024]{1,0:T(8,128)(2,1)S(1)} %multiply_convert_fusion) | copy-start | bytes 1572868
  15.6 9.4 %collective-permute-start.3 = (bf16[512,128]{1,0:T(8,128)(2,1)S(1)}, bf16[512,128]{1,0:T(8,128)(2,1)S(1)}, u32[]{:S(2)}, u32[]{:S(2)}) collective-permute-start(bf16[512,128]{1,0:T(8,128)(2,1)S(1)} %pad_maximum_fusion.10), channel_id=1, source_target_pairs={{0,16},{2,18},{4,20},{6,22},{8,24},{10,26},{12,28},{14,30},{16,0},... | collective-permute-start | bytes 393224 | tf_op jit(solution)/shard_map/ppermute | solution.py:254
  18.0 7.0 %collective-permute-start.4 = (bf16[512,128]{1,0:T(8,128)(2,1)S(1)}, bf16[512,128]{1,0:T(8,128)(2,1)S(1)}, u32[]{:S(2)}, u32[]{:S(2)}) collective-permute-start(bf16[512,128]{1,0:T(8,128)(2,1)S(1)} %pad_maximum_fusion.9), channel_id=1, source_target_pairs={{0,2},{2,4},{4,6},{6,0},{8,10},{10,12},{12,14},{14,8},{16,18},{18,... | collective-permute-start | bytes 393224 | tf_op jit(solution)/shard_map/ppermute | solution.py:254
  19.9 6.2 %collective-permute-start.5 = (bf16[512,128]{1,0:T(8,128)(2,1)S(1)}, bf16[512,128]{1,0:T(8,128)(2,1)S(1)}, u32[]{:S(2)}, u32[]{:S(2)}) collective-permute-start(bf16[512,128]{1,0:T(8,128)(2,1)S(1)} %pad_maximum_fusion.10), channel_id=1, source_target_pairs={{0,8},{2,10},{4,12},{6,14},{8,16},{10,18},{12,20},{14,22},{16,24},... | collective-permute-start | bytes 393224 | tf_op jit(solution)/shard_map/ppermute | solution.py:254
  22.1 5.0 %collective-permute-start.6 = (bf16[512,128]{1,0:T(8,128)(2,1)S(1)}, bf16[512,128]{1,0:T(8,128)(2,1)S(1)}, u32[]{:S(2)}, u32[]{:S(2)}) collective-permute-start(bf16[512,128]{1,0:T(8,128)(2,1)S(1)} %pad_maximum_fusion.9), channel_id=1, source_target_pairs={{0,6},{2,0},{4,2},{6,4},{8,14},{10,8},{12,10},{14,12},{16,22},{18,... | collective-permute-start | bytes 393224 | tf_op jit(solution)/shard_map/ppermute | solution.py:254
  23.4 5.0 %collective-permute-start.7 = (bf16[512,128]{1,0:T(8,128)(2,1)S(1)}, bf16[512,128]{1,0:T(8,128)(2,1)S(1)}, u32[]{:S(2)}, u32[]{:S(2)}) collective-permute-start(bf16[512,128]{1,0:T(8,128)(2,1)S(1)} %pad_maximum_fusion.10), channel_id=1, source_target_pairs={{0,24},{2,26},{4,28},{6,30},{8,0},{10,2},{12,4},{14,6},{16,8},{18,... | collective-permute-start | bytes 393224 | tf_op jit(solution)/shard_map/ppermute | solution.py:254
  28.6 23.1 %collective-permute-start.8 = (bf16[2048,128]{1,0:T(8,128)(2,1)S(1)}, bf16[2048,128]{1,0:T(8,128)(2,1)S(1)}, u32[]{:S(2)}, u32[]{:S(2)}) collective-permute-start(bf16[2048,128]{1,0:T(8,128)(2,1)S(1)} %constant_dynamic-update-slice_fusion.k0), channel_id=1, source_target_pairs={{0,8},{2,10},{4,12},{6,14},{8,16},{10,18},{12,20},{14,22},{16,24},... | collective-permute-start | bytes 1572872 | tf_op jit(solution)/shard_map/ppermute | solution.py:254
  28.7 23.1 %collective-permute-start.9 = (bf16[2048,128]{1,0:T(8,128)(2,1)S(1)}, bf16[2048,128]{1,0:T(8,128)(2,1)S(1)}, u32[]{:S(2)}, u32[]{:S(2)}) collective-permute-start(bf16[2048,128]{1,0:T(8,128)(2,1)S(1)} %constant_dynamic-update-slice_fusion.5.v0), channel_id=1, source_target_pairs={{0,2},{2,4},{4,6},{6,0},{8,10},{10,12},{12,14},{14,8},{16,18},{18,... | collective-permute-start | bytes 1572872 | tf_op jit(solution)/shard_map/ppermute | solution.py:254
  29.4 22.6 %collective-permute-start.10 = (bf16[2048,128]{1,0:T(8,128)(2,1)S(1)}, bf16[2048,128]{1,0:T(8,128)(2,1)S(1)}, u32[]{:S(2)}, u32[]{:S(2)}) collective-permute-start(bf16[2048,128]{1,0:T(8,128)(2,1)S(1)} %constant_dynamic-update-slice_fusion.k0), channel_id=1, source_target_pairs={{0,24},{2,26},{4,28},{6,30},{8,0},{10,2},{12,4},{14,6},{16,8},{18,... | collective-permute-start | bytes 1572872 | tf_op jit(solution)/shard_map/ppermute | solution.py:254
  32.6 21.0 %collective-permute-start.11 = (bf16[2048,128]{1,0:T(8,128)(2,1)S(1)}, bf16[2048,128]{1,0:T(8,128)(2,1)S(1)}, u32[]{:S(2)}, u32[]{:S(2)}) collective-permute-start(bf16[2048,128]{1,0:T(8,128)(2,1)S(1)} %constant_dynamic-update-slice_fusion.5.v0), channel_id=1, source_target_pairs={{0,6},{2,0},{4,2},{6,4},{8,14},{10,8},{12,10},{14,12},{16,22},{18,... | collective-permute-start | bytes 1572872 | tf_op jit(solution)/shard_map/ppermute | solution.py:254
  35.1 5.1 %copy-start.9 = (s32[32,2]{0,1:T(2,128)S(1)}, s32[32,2]{0,1:T(2,128)}, u32[]{:S(2)}) copy-start(s32[32,2]{0,1:T(2,128)} %param.12) | copy-start | bytes 772
  36.0 24.7 %collective-permute-start = (bf16[256,1024]{1,0:T(8,128)(2,1)}, bf16[256,1024]{1,0:T(8,128)(2,1)}, u32[]{:S(2)}, u32[]{:S(2)}) collective-permute-start(bf16[256,1024]{1,0:T(8,128)(2,1)} %pad_maximum_fusion), channel_id=1, source_target_pairs={{0,62},{2,60},{4,58},{6,56},{8,54},{10,52},{12,50},{14,48},{16,46}... | collective-permute-start | bytes 1572872 | tf_op jit(solution)/shard_map/ppermute | solution.py:254
  53.6 7.1 %copy-start.2 = (bf16[256,1024]{1,0:T(8,128)(2,1)S(1)}, bf16[256,1024]{1,0:T(8,128)(2,1)}, u32[]{:S(2)}) copy-start(bf16[256,1024]{1,0:T(8,128)(2,1)} %copy-done.1) | copy-start | bytes 1572868
  53.6 7.1 %copy-start.4 = (bf16[256,1024]{1,0:T(8,128)(2,1)S(1)}, bf16[256,1024]{1,0:T(8,128)(2,1)}, u32[]{:S(2)}) copy-start(bf16[256,1024]{1,0:T(8,128)(2,1)} %param.7) | copy-start | bytes 1572868
  53.7 8.3 %collective-permute-start.12 = (bf16[1024,128]{1,0:T(8,128)(2,1)S(1)}, bf16[1024,128]{1,0:T(8,128)(2,1)S(1)}, u32[]{:S(2)}, u32[]{:S(2)}) collective-permute-start(bf16[1024,128]{1,0:T(8,128)(2,1)S(1)} %slice.160), channel_id=1, source_target_pairs={{0,8},{2,10},{4,12},{6,14},{8,16},{10,18},{12,20},{14,22},{16,24},... | collective-permute-start | bytes 786440 | tf_op jit(solution)/shard_map/ppermute | solution.py:254
  53.8 8.2 %collective-permute-start.13 = (bf16[1024,128]{1,0:T(8,128)(2,1)S(1)}, bf16[1024,128]{1,0:T(8,128)(2,1)S(1)}, u32[]{:S(2)}, u32[]{:S(2)}) collective-permute-start(bf16[1024,128]{1,0:T(8,128)(2,1)S(1)} %slice.161), channel_id=1, source_target_pairs={{0,2},{2,4},{4,6},{6,0},{8,10},{10,12},{12,14},{14,8},{16,18},{18,... | collective-permute-start | bytes 786440 | tf_op jit(solution)/shard_map/ppermute | solution.py:254
  54.8 7.2 %collective-permute-start.14 = (bf16[1024,128]{1,0:T(8,128)(2,1)S(1)}, bf16[1024,128]{1,0:T(8,128)(2,1)S(1)}, u32[]{:S(2)}, u32[]{:S(2)}) collective-permute-start(bf16[1024,128]{1,0:T(8,128)(2,1)S(1)} %slice.162), channel_id=1, source_target_pairs={{0,24},{2,26},{4,28},{6,30},{8,0},{10,2},{12,4},{14,6},{16,8},{18,... | collective-permute-start | bytes 786440 | tf_op jit(solution)/shard_map/ppermute | solution.py:254
  58.0 6.6 %collective-permute-start.15 = (bf16[1024,128]{1,0:T(8,128)(2,1)S(1)}, bf16[1024,128]{1,0:T(8,128)(2,1)S(1)}, u32[]{:S(2)}, u32[]{:S(2)}) collective-permute-start(bf16[1024,128]{1,0:T(8,128)(2,1)S(1)} %slice.163), channel_id=1, source_target_pairs={{0,6},{2,0},{4,2},{6,4},{8,14},{10,8},{12,10},{14,12},{16,22},{18,... | collective-permute-start | bytes 786440 | tf_op jit(solution)/shard_map/ppermute | solution.py:254
  61.9 2.6 %copy-start = (s32[32]{0:T(128)S(1)}, s32[32]{0:T(128)}, u32[]{:S(2)}) copy-start(s32[32]{0:T(128)} %counts.1) | copy-start | bytes 388
  103.3 10.4 %collective-permute-start.16 = (bf16[1024,128]{1,0:T(8,128)(2,1)S(1)}, bf16[1024,128]{1,0:T(8,128)(2,1)S(1)}, u32[]{:S(2)}, u32[]{:S(2)}) collective-permute-start(bf16[1024,128]{1,0:T(8,128)(2,1)S(1)} %get-tuple-element.107), channel_id=1, source_target_pairs={{0,8},{2,10},{4,12},{6,14},{8,16},{10,18},{12,20},{14,22},{16,24},... | collective-permute-start | bytes 786440 | tf_op jit(solution)/shard_map/ppermute | solution.py:254
  103.4 10.5 %collective-permute-start.17 = (bf16[1024,128]{1,0:T(8,128)(2,1)S(1)}, bf16[1024,128]{1,0:T(8,128)(2,1)S(1)}, u32[]{:S(2)}, u32[]{:S(2)}) collective-permute-start(bf16[1024,128]{1,0:T(8,128)(2,1)S(1)} %get-tuple-element.108), channel_id=1, source_target_pairs={{0,2},{2,4},{4,6},{6,0},{8,10},{10,12},{12,14},{14,8},{16,18},{18,... | collective-permute-start | bytes 786440 | tf_op jit(solution)/shard_map/ppermute | solution.py:254
  105.3 9.8 %collective-permute-start.18 = (bf16[1024,128]{1,0:T(8,128)(2,1)S(1)}, bf16[1024,128]{1,0:T(8,128)(2,1)S(1)}, u32[]{:S(2)}, u32[]{:S(2)}) collective-permute-start(bf16[1024,128]{1,0:T(8,128)(2,1)S(1)} %get-tuple-element.109), channel_id=1, source_target_pairs={{0,24},{2,26},{4,28},{6,30},{8,0},{10,2},{12,4},{14,6},{16,8},{18,... | collective-permute-start | bytes 786440 | tf_op jit(solution)/shard_map/ppermute | solution.py:254
  108.5 9.2 %collective-permute-start.19 = (bf16[1024,128]{1,0:T(8,128)(2,1)S(1)}, bf16[1024,128]{1,0:T(8,128)(2,1)S(1)}, u32[]{:S(2)}, u32[]{:S(2)}) collective-permute-start(bf16[1024,128]{1,0:T(8,128)(2,1)S(1)} %get-tuple-element.110), channel_id=1, source_target_pairs={{0,6},{2,0},{4,2},{6,4},{8,14},{10,8},{12,10},{14,12},{16,22},{18,... | collective-permute-start | bytes 786440 | tf_op jit(solution)/shard_map/ppermute | solution.py:254
  118.2 12.9 %collective-permute-start.21 = (bf16[2048,128]{1,0:T(8,128)(2,1)S(1)}, bf16[2048,128]{1,0:T(8,128)(2,1)S(1)}, u32[]{:S(2)}, u32[]{:S(2)}) collective-permute-start(bf16[2048,128]{1,0:T(8,128)(2,1)S(1)} %pad_maximum_fusion.4), channel_id=1, source_target_pairs={{0,8},{2,10},{4,12},{6,14},{8,16},{10,18},{12,20},{14,22},{16,24},... | collective-permute-start | bytes 1572872 | tf_op jit(solution)/shard_map/ppermute | solution.py:254
  118.3 13.3 %collective-permute-start.22 = (bf16[2048,128]{1,0:T(8,128)(2,1)S(1)}, bf16[2048,128]{1,0:T(8,128)(2,1)S(1)}, u32[]{:S(2)}, u32[]{:S(2)}) collective-permute-start(bf16[2048,128]{1,0:T(8,128)(2,1)S(1)} %pad_maximum_fusion.5), channel_id=1, source_target_pairs={{0,2},{2,4},{4,6},{6,0},{8,10},{10,12},{12,14},{14,8},{16,18},{18,... | collective-permute-start | bytes 1572872 | tf_op jit(solution)/shard_map/ppermute | solution.py:254
  118.4 13.2 %collective-permute-start.23 = (bf16[2048,128]{1,0:T(8,128)(2,1)S(1)}, bf16[2048,128]{1,0:T(8,128)(2,1)S(1)}, u32[]{:S(2)}, u32[]{:S(2)}) collective-permute-start(bf16[2048,128]{1,0:T(8,128)(2,1)S(1)} %pad_maximum_fusion.6), channel_id=1, source_target_pairs={{0,24},{2,26},{4,28},{6,30},{8,0},{10,2},{12,4},{14,6},{16,8},{18,... | collective-permute-start | bytes 1572872 | tf_op jit(solution)/shard_map/ppermute | solution.py:254
  121.5 11.3 %collective-permute-start.24 = (bf16[2048,128]{1,0:T(8,128)(2,1)S(1)}, bf16[2048,128]{1,0:T(8,128)(2,1)S(1)}, u32[]{:S(2)}, u32[]{:S(2)}) collective-permute-start(bf16[2048,128]{1,0:T(8,128)(2,1)S(1)} %pad_maximum_fusion.7), channel_id=1, source_target_pairs={{0,6},{2,0},{4,2},{6,4},{8,14},{10,8},{12,10},{14,12},{16,22},{18,... | collective-permute-start | bytes 1572872 | tf_op jit(solution)/shard_map/ppermute | solution.py:254
  124.8 11.9 %collective-permute-start.32 = (f32[256]{0:T(256)S(1)}, f32[256]{0:T(256)S(1)}, u32[]{:S(2)}, u32[]{:S(2)}) collective-permute-start(f32[256]{0:T(256)S(1)} %select_bitcast_fusion), channel_id=1, source_target_pairs={{0,62},{2,60},{4,58},{6,56},{8,54},{10,52},{12,50},{14,48},{16,46}... | collective-permute-start | bytes 3080 | tf_op jit(solution)/shard_map/ppermute | solution.py:254
  133.4 10.9 %collective-permute-start.25 = (bf16[512,128]{1,0:T(8,128)(2,1)S(1)}, bf16[512,128]{1,0:T(8,128)(2,1)S(1)}, u32[]{:S(2)}, u32[]{:S(2)}) collective-permute-start(bf16[512,128]{1,0:T(8,128)(2,1)S(1)} %get-tuple-element.135), channel_id=1, source_target_pairs={{0,4},{2,6},{4,0},{6,2},{8,12},{10,14},{12,8},{14,10},{16,20},{18,... | collective-permute-start | bytes 393224 | tf_op jit(solution)/shard_map/ppermute | solution.py:254
  136.7 6.0 %collective-permute-start.33 = (f32[256]{0:T(256)S(1)}, f32[256]{0:T(256)S(1)}, u32[]{:S(2)}, u32[]{:S(2)}) collective-permute-start(f32[256]{0:T(256)S(1)} %bitcast_add_fusion), channel_id=1, source_target_pairs={{0,1},{1,0},{2,3},{3,2},{4,5},{5,4},{6,7},{7,6},{8,9},{9,8},{10,11... | collective-permute-start | bytes 3080 | tf_op jit(solution)/shard_map/ppermute | solution.py:391
  138.0 8.5 %collective-permute-start.26 = (bf16[512,128]{1,0:T(8,128)(2,1)S(1)}, bf16[512,128]{1,0:T(8,128)(2,1)S(1)}, u32[]{:S(2)}, u32[]{:S(2)}) collective-permute-start(bf16[512,128]{1,0:T(8,128)(2,1)S(1)} %get-tuple-element.136), channel_id=1, source_target_pairs={{0,16},{2,18},{4,20},{6,22},{8,24},{10,26},{12,28},{14,30},{16,0},... | collective-permute-start | bytes 393224 | tf_op jit(solution)/shard_map/ppermute | solution.py:254
  138.0 12.8 %collective-permute-start.27 = (bf16[512,128]{1,0:T(8,128)(2,1)S(1)}, bf16[512,128]{1,0:T(8,128)(2,1)S(1)}, u32[]{:S(2)}, u32[]{:S(2)}) collective-permute-start(bf16[512,128]{1,0:T(8,128)(2,1)S(1)} %get-tuple-element.137), channel_id=1, source_target_pairs={{0,2},{2,4},{4,6},{6,0},{8,10},{10,12},{12,14},{14,8},{16,18},{18,... | collective-permute-start | bytes 393224 | tf_op jit(solution)/shard_map/ppermute | solution.py:254
  142.6 8.2 %collective-permute-start.28 = (bf16[512,128]{1,0:T(8,128)(2,1)S(1)}, bf16[512,128]{1,0:T(8,128)(2,1)S(1)}, u32[]{:S(2)}, u32[]{:S(2)}) collective-permute-start(bf16[512,128]{1,0:T(8,128)(2,1)S(1)} %get-tuple-element.138), channel_id=1, source_target_pairs={{0,8},{2,10},{4,12},{6,14},{8,16},{10,18},{12,20},{14,22},{16,24},... | collective-permute-start | bytes 393224 | tf_op jit(solution)/shard_map/ppermute | solution.py:254
  142.6 8.2 %collective-permute-start.29 = (bf16[512,128]{1,0:T(8,128)(2,1)S(1)}, bf16[512,128]{1,0:T(8,128)(2,1)S(1)}, u32[]{:S(2)}, u32[]{:S(2)}) collective-permute-start(bf16[512,128]{1,0:T(8,128)(2,1)S(1)} %get-tuple-element.139), channel_id=1, source_target_pairs={{0,6},{2,0},{4,2},{6,4},{8,14},{10,8},{12,10},{14,12},{16,22},{18,... | collective-permute-start | bytes 393224 | tf_op jit(solution)/shard_map/ppermute | solution.py:254
  144.3 6.5 %collective-permute-start.30 = (bf16[512,128]{1,0:T(8,128)(2,1)S(1)}, bf16[512,128]{1,0:T(8,128)(2,1)S(1)}, u32[]{:S(2)}, u32[]{:S(2)}) collective-permute-start(bf16[512,128]{1,0:T(8,128)(2,1)S(1)} %get-tuple-element.140), channel_id=1, source_target_pairs={{0,24},{2,26},{4,28},{6,30},{8,0},{10,2},{12,4},{14,6},{16,8},{18,... | collective-permute-start | bytes 393224 | tf_op jit(solution)/shard_map/ppermute | solution.py:254
  146.5 12.1 %collective-permute-start.20 = (bf16[256,512]{1,0:T(8,128)(2,1)S(1)}, bf16[256,512]{1,0:T(8,128)(2,1)S(1)}, u32[]{:S(2)}, u32[]{:S(2)}) collective-permute-start(bf16[256,512]{1,0:T(8,128)(2,1)S(1)} %broadcast_select_fusion.2), channel_id=1, source_target_pairs={{0,62},{2,60},{4,58},{6,56},{8,54},{10,52},{12,50},{14,48},{16,46}... | collective-permute-start | bytes 786440 | tf_op jit(solution)/shard_map/ppermute | solution.py:254
  151.1 10.8 %collective-permute-start.31 = (bf16[256,256]{1,0:T(8,128)(2,1)S(1)}, bf16[256,256]{1,0:T(8,128)(2,1)S(1)}, u32[]{:S(2)}, u32[]{:S(2)}) collective-permute-start(bf16[256,256]{1,0:T(8,128)(2,1)S(1)} %pad_maximum_fusion.11), channel_id=1, source_target_pairs={{0,62},{2,60},{4,58},{6,56},{8,54},{10,52},{12,50},{14,48},{16,46}... | collective-permute-start | bytes 393224 | tf_op jit(solution)/shard_map/ppermute | solution.py:254

commit v3 on v1

v3 whole, which is shorter than its diff:
```python
import jax
import jax.numpy as jnp
from jax import lax
from jax.experimental import pallas as pl
from jax.experimental.pallas import tpu as pltpu
from jax.sharding import PartitionSpec as P

HEAD_SIZE = 128
BLK = 128
GROUP = 4
LANES = GROUP * BLK
SLOTS = 64
SEEN, LIVE, TABLE = 64, 72, 76
NEAR_AT, FAR_AT = 0, 48
SCALE = HEAD_SIZE ** (-0.5)
EXP2_SCALE = SCALE * 1.4426950408889634
CHUNK = 1024
TAIL = 512
MASKED = -1.5e38
OFFSETS = (0, -1, 1, 2)
NEAR, FAR = (0, -1, 1), (2,)
NT = (((1,), (1,)), ((), ()))


def dot_nt(a, b):
    return lax.dot_general(a, b, NT, preferred_element_type=jnp.float32)


def dot_nn(a, b):
    return jnp.dot(a, b, preferred_element_type=jnp.float32)


def table_kernel(place_ref, ids, counts, table, ranks, before_of):
    place = place_ref[0]
    half, z, y = place // 16, place // 4 % 4, place % 4
    live_total = lax.fori_loop(0, 32, lambda s, n: n + counts[s], 0)

    def of_shard(s, before):
        both = (counts[s] > 1).astype(jnp.int32)
        later = (ids[2 * s + 1] < ids[2 * s]).astype(jnp.int32) * both
        ranks[2 * s] = before + later
        ranks[2 * s + 1] = jnp.where(both == 1, before + 1 - later, live_total + 2 * s - before)
        return before + counts[s]

    lax.fori_loop(0, 32, of_shard, 0)
    start, seen_at = 0, SEEN
    for held in (NEAR, FAR):

        def clear(r, _):
            before_of[r] = 0
            return 0

        lax.fori_loop(0, SLOTS, clear, 0)
        n = start
        for stream in range(2):
            for outer in held:
                for inner in OFFSETS:
                    dz, dy = (outer, inner) if stream == 0 else (inner, outer)
                    shard = 16 * half + (z + dz) % 4 * 4 + (y + dy) % 4
                    if stream == 1:
                        shard = 31 - shard
                    for slot in range(2):
                        r = ranks[2 * shard + slot]
                        table[n] = r
                        before_of[r] = 1
                        n += 1

        def prefix(r, total):
            here = before_of[r]
            before_of[r] = total
            return total + here

        lax.fori_loop(0, SLOTS, prefix, 0)

        def packed(i, _):
            table[i] = before_of[table[i]]
            return 0

        lax.fori_loop(start, n, packed, 0)
        for qb in range(4):
            shard = place if qb < 2 else 31 - place
            table[seen_at + qb] = before_of[ranks[2 * shard + qb % 2]]
            table[LIVE + qb] = (qb % 2 < counts[shard]).astype(jnp.int32)
        start, seen_at = n, seen_at + 4


def each_block(pieces, tab, first, move):
    for piece in pieces:
        blocks = piece.shape[0] // (2 * BLK)

        def turn(b, _, piece=piece, first=first):
            k_at = pl.multiple_of(b // 2 * 4 * BLK + b % 2 * BLK, BLK)
            to = pl.multiple_of(tab[first + b] * BLK, BLK)
            move(piece, k_at, pl.multiple_of(k_at + 2 * BLK, BLK), to)
            return 0

        lax.fori_loop(0, blocks, turn, 0, unroll=4)
        first += blocks


def pack(pieces, tab, first, kc, vc):
    def move(piece, k_at, v_at, to):
        kc[pl.ds(to, BLK), :] = piece[pl.ds(k_at, BLK), :]
        vc[pl.ds(to, BLK), :] = piece[pl.ds(v_at, BLK), :]

    each_block(pieces, tab, first, move)


def unpack(pieces, tab, first, dka, dva):
    def move(piece, k_at, v_at, to):
        piece[pl.ds(k_at, BLK), :] = (dka[pl.ds(to, BLK), :] * SCALE).astype(piece.dtype)
        piece[pl.ds(v_at, BLK), :] = dva[pl.ds(to, BLK), :].astype(piece.dtype)

    each_block(pieces, tab, first, move)


def prepare(kc, kt, dka, dva):
    row = lax.broadcasted_iota(jnp.int32, (HEAD_SIZE, HEAD_SIZE), 0)
    col = lax.broadcasted_iota(jnp.int32, (HEAD_SIZE, HEAD_SIZE), 1)
    eye = (row == col).astype(jnp.bfloat16)

    def turn(c, _):
        here = pl.ds(pl.multiple_of(c * CHUNK, CHUNK), CHUNK)
        kt[:, here] = dot_nt(eye, kc[here, :]).astype(jnp.bfloat16)
        dka[here, :] = jnp.zeros((CHUNK, HEAD_SIZE), jnp.float32)
        dva[here, :] = jnp.zeros((CHUNK, HEAD_SIZE), jnp.float32)
        return 0

    lax.fori_loop(0, kc.shape[0] // CHUNK, turn, 0)


def stack_heads(qb, q, do, qs, dos):
    rows = pl.ds(pl.multiple_of(qb * BLK, BLK), BLK)
    for h in range(GROUP):
        cols = slice(h * HEAD_SIZE, (h + 1) * HEAD_SIZE)
        qs[cols, :] = q[rows, cols]
        dos[cols, :] = do[rows, cols]


def over_keys(step, seen, diagonal):
    wide = lax.div(seen, CHUNK // BLK)
    tail = wide * CHUNK
    left = seen - wide * (CHUNK // BLK) + (1 if diagonal else 0)
    lane = lax.broadcasted_iota(jnp.int32, (1, LANES), 1)
    bound = seen * BLK + ((lane & (BLK - 1)) if diagonal else -1)

    def turn(c, _):
        step(c * CHUNK, CHUNK, None)
        return 0

    lax.fori_loop(0, wide, turn, 0)
    pl.when((left > 0) & (left <= TAIL // BLK))(lambda: step(tail, TAIL, bound))
    pl.when(left > TAIL // BLK)(lambda: step(tail, CHUNK, bound))


def allowed(at, size, bound):
    return at + lax.broadcasted_iota(jnp.int32, (size, LANES), 0) <= bound


def stats_pass(kc, vc, qs, dos, top, total, dot, seen, diagonal):
    def step(at, size, bound):
        here = pl.ds(pl.multiple_of(at, TAIL), size)
        s = dot_nt(kc[here, :], qs[...])
        dp = dot_nt(vc[here, :], dos[...])
        if bound is not None:
            s = jnp.where(allowed(at, size, bound), s, MASKED)
        s = s.reshape(size // 8, 8, LANES)
        dp = dp.reshape(size // 8, 8, LANES)
        old = top[...]
        new = jnp.maximum(old, jnp.max(s, axis=0))
        p = jnp.exp2((s - new[None]) * EXP2_SCALE)
        fix = jnp.exp2((old - new) * EXP2_SCALE)
        top[...] = new
        total[...] = total[...] * fix + jnp.sum(p, axis=0)
        dot[...] = dot[...] * fix + jnp.sum(p * dp, axis=0)

    over_keys(step, seen, diagonal)


def grads_pass(kc, vc, kt, qs, dos, lse, delta, dka, dva, dqt, seen, diagonal):
    lse, delta = lse[...], delta[...]

    def step(at, size, bound):
        here = pl.ds(pl.multiple_of(at, TAIL), size)
        s = dot_nt(kc[here, :], qs[...])
        dp = dot_nt(vc[here, :], dos[...])
        p = jnp.exp2(s * EXP2_SCALE - lse)
        if bound is not None:
            p = jnp.where(allowed(at, size, bound), p, 0.0)
        ds = (p * (dp - delta)).astype(jnp.bfloat16)
        dva[here, :] += dot_nn(p.astype(jnp.bfloat16), dos[...])
        dka[here, :] += dot_nn(ds, qs[...])
        dqt[...] += dot_nn(kt[:, here], ds)

    over_keys(step, seen, diagonal)


def near_stats_kernel(
    tab, q, do, p0, p1, p2, p3, p4, p5,
    top, total, dot,
    kc, vc, qs, dos,
):
    pack((p0, p1, p2, p3, p4, p5), tab, NEAR_AT, kc, vc)

    def query_block(qb, _):
        live = tab[LIVE + qb] != 0
        top[qb] = jnp.full((8, LANES), MASKED, jnp.float32)
        total[qb] = jnp.zeros((8, LANES), jnp.float32)
        dot[qb] = jnp.zeros((8, LANES), jnp.float32)

        @pl.when(live)
        def _():
            stack_heads(qb, q, do, qs, dos)
            stats_pass(
                kc, vc, qs, dos, top.at[qb], total.at[qb], dot.at[qb], tab[SEEN + qb], True
            )

        return 0

    lax.fori_loop(0, 4, query_block, 0)


def far_kernel(
    tab, q, do, p0, p1, p2, p3, top_in, total_in, dot_in,
    o0, o1, o2, o3, lse, delta, delta_out, dqt,
    kc, vc, kt, dka, dva, qs, dos, top, total, dot,
):
    pack((p0, p1, p2, p3), tab, FAR_AT, kc, vc)
    prepare(kc, kt, dka, dva)

    def query_block(qb, _):
        live = tab[LIVE + qb] != 0
        lse[qb] = jnp.zeros((1, LANES), jnp.float32)
        delta[qb] = jnp.zeros((1, LANES), jnp.float32)
        delta_out[qb] = jnp.zeros((1, BLK), jnp.float32)
        dqt[qb] = jnp.zeros((HEAD_SIZE, LANES), jnp.float32)

        @pl.when(live)
        def _():
            stack_heads(qb, q, do, qs, dos)
            seen = tab[SEEN + 4 + qb]
            top[...] = top_in[qb]
            total[...] = total_in[qb]
            dot[...] = dot_in[qb]
            stats_pass(kc, vc, qs, dos, top, total, dot, seen, False)
            most = jnp.max(top[...], axis=0, keepdims=True)
            fix = jnp.exp2((top[...] - most) * EXP2_SCALE)
            whole = jnp.sum(total[...] * fix, axis=0, keepdims=True)
            d = jnp.sum(dot[...] * fix, axis=0, keepdims=True) / whole
            lse[qb] = most * EXP2_SCALE + jnp.log2(whole)
            delta[qb] = d
            delta_out[qb] = d[:, 0:128] + d[:, 128:256] + d[:, 256:384] + d[:, 384:512]
            grads_pass(
                kc, vc, kt, qs, dos, lse.at[qb], delta.at[qb], dka, dva, dqt.at[qb], seen, False
            )

        return 0

    lax.fori_loop(0, 4, query_block, 0)
    unpack((o0, o1, o2, o3), tab, FAR_AT, dka, dva)


def near_grads_kernel(
    tab, q, do, p0, p1, p2, p3, p4, p5, lse, delta, dqt_in,
    dq, o0, o1, o2, o3, o4, o5,
    kc, vc, kt, dka, dva, qs, dos, dqt,
):
    pack((p0, p1, p2, p3, p4, p5), tab, NEAR_AT, kc, vc)
    prepare(kc, kt, dka, dva)

    def query_block(qb, _):
        live = tab[LIVE + qb] != 0
        rows = pl.ds(pl.multiple_of(qb * BLK, BLK), BLK)

        @pl.when(jnp.logical_not(live))
        def _():
            dq[rows, :] = jnp.zeros((BLK, LANES), dq.dtype)

        @pl.when(live)
        def _():
            stack_heads(qb, q, do, qs, dos)
            dqt[...] = dqt_in[qb]
            grads_pass(
                kc, vc, kt, qs, dos, lse.at[qb], delta.at[qb], dka, dva, dqt, tab[SEEN + qb], True
            )
            for h in range(GROUP):
                cols = slice(h * HEAD_SIZE, (h + 1) * HEAD_SIZE)
                dq[rows, cols] = (dqt[:, cols].T * SCALE).astype(dq.dtype)

        return 0

    lax.fori_loop(0, 4, query_block, 0)
    unpack((o0, o1, o2, o3, o4, o5), tab, NEAR_AT, dka, dva)


def shape(*sizes, dtype=jnp.float32):
    return jax.ShapeDtypeStruct(sizes, dtype)


def call(kernel, outs, keys, with_grads, extra, matmuls, name, *args):
    bf = jnp.bfloat16
    vm = pl.BlockSpec(memory_space=pltpu.VMEM)
    sm = pl.BlockSpec(memory_space=pltpu.SMEM)
    scratch = [
        pltpu.VMEM((keys, HEAD_SIZE), bf),
        pltpu.VMEM((keys, HEAD_SIZE), bf),
    ]
    if with_grads:
        scratch += [
            pltpu.VMEM((HEAD_SIZE, keys), bf),
            pltpu.VMEM((keys, HEAD_SIZE), jnp.float32),
            pltpu.VMEM((keys, HEAD_SIZE), jnp.float32),
        ]
    scratch += [pltpu.VMEM((LANES, HEAD_SIZE), bf)] * 2
    scratch += [pltpu.VMEM(s, jnp.float32) for s in extra]
    return pl.pallas_call(
        kernel,
        out_shape=outs,
        in_specs=[sm] + [vm] * (len(args) - 1),
        out_specs=[vm] * len(outs),
        scratch_shapes=scratch,
        compiler_params=pltpu.CompilerParams(vmem_limit_bytes=40 * 1024 * 1024),
        cost_estimate=pl.CostEstimate(
            flops=matmuls * 2 * HEAD_SIZE * LANES * keys * 4,
            bytes_accessed=8 * keys * HEAD_SIZE,
            transcendentals=LANES * keys * 2,
        ),
        name=name,
    )(*args)


def ring_perms(axis):
    def place(s, step):
        x, z, y = s // 16, s // 4 % 4, s % 4
        if axis == "z":
            z = (z + step) % 4
        else:
            y = (y + step) % 4
        return 16 * x + 4 * z + y

    return {step: [(s, place(s, step)) for s in range(32)] for step in (1, -1, 2)}


Z_RING, Y_RING = ring_perms("z"), ring_perms("y")
PAIR = [(s, 31 - s) for s in range(32)]


def send(a, perm):
    return lax.ppermute(a, "seq", perm)


def in_step(*arrays):
    return lax.optimization_barrier(arrays)


def exchange(pairs):
    arrays = in_step(*[a for a, _ in pairs])
    return in_step(*[send(a, perm) for a, (_, perm) in zip(arrays, pairs)])


def total(*parts):
    return sum(a.astype(jnp.float32) for a in parts).astype(jnp.bfloat16)


def gather_near(block, ring):
    far, prev, nxt = exchange([(block, ring[2]), (block, ring[1]), (block, ring[-1])])
    return jnp.concatenate([block, prev, nxt, far], axis=0)


def both_ways(up, down, ring):
    return exchange([(up, ring[1]), (down, ring[-1])])


def local(
    queries, routed_key_rows, routed_value_rows, grad_out, gate_logit, block_ids, block_counts
):
    bf = jnp.bfloat16
    f32 = jnp.float32
    rows = queries.shape[0]
    seq_index = lax.axis_index("seq")
    low = seq_index < 16

    def halves(a):
        width = a.shape[1] // 2
        left, right = a[:, :width], a[:, width:]
        return jnp.where(low, left, right), jnp.where(low, right, left)

    def columns_of(own, other):
        return jnp.concatenate([jnp.where(low, own, other), jnp.where(low, other, own)], axis=1)

    sm = pl.BlockSpec(memory_space=pltpu.SMEM)
    table = pl.pallas_call(
        table_kernel,
        out_shape=shape(TABLE, dtype=jnp.int32),
        in_specs=[sm] * 3,
        out_specs=sm,
        scratch_shapes=[pltpu.SMEM((SLOTS,), jnp.int32)] * 2,
        name="block_table",
    )(seq_index.reshape(1), block_ids.reshape(-1), block_counts)
    gate = jax.nn.sigmoid(gate_logit)
    out_grad = (gate[:, None] * grad_out.astype(f32)).astype(bf)
    k_own, k_other = halves(routed_key_rows)
    v_own, v_other = halves(routed_value_rows)
    own = jnp.concatenate([k_own, v_own], axis=0)
    partner = send(jnp.concatenate([k_other, v_other], axis=0), PAIR)
    q_own, q_other = halves(queries)
    d_own, d_other = halves(out_grad)
    own = gather_near(own, Y_RING)
    half = own.shape[0] // 2
    o_prev, o_next = both_ways(own, own, Z_RING)
    partner = gather_near(partner, Z_RING)
    partner, qd_other = in_step(partner, jnp.concatenate([q_other, d_other], axis=1))
    p_prev, p_next = both_ways(partner, partner, Y_RING)
    qd_in = send(qd_other, PAIR)
    far = (
        *both_ways(o_prev[:half], o_next[half:], Z_RING),
        *both_ways(p_prev[:half], p_next[half:], Y_RING),
    )
    q_all = jnp.concatenate([q_own, qd_in[:, :LANES]], axis=0)
    d_all = jnp.concatenate([d_own, qd_in[:, LANES:]], axis=0)
    near = (own, o_prev, o_next, partner, p_prev, p_next)
    common = (table, q_all, d_all)
    stats = call(
        near_stats_kernel, [shape(4, 8, LANES)] * 3, 6144, False, (), 2, "near_stats",
        *common, *near,
    )
    *far_grads, lse, delta, delta_sum, dqt = call(
        far_kernel,
        [shape(half, HEAD_SIZE, dtype=bf)] * 4
        + [shape(4, 1, LANES), shape(4, 1, LANES), shape(4, 1, BLK), shape(4, HEAD_SIZE, LANES)],
        2048, True, ((8, LANES),) * 3, 7, "far_grads", *common, *far, *stats,
    )
    dq, o_0, o_p, o_n, p_0, p_p, p_n = call(
        near_grads_kernel,
        [shape(2 * rows, LANES, dtype=bf)] + [shape(2 * half, HEAD_SIZE, dtype=bf)] * 6,
        6144, True, ((HEAD_SIZE, LANES),), 5, "near_grads", *common, *near, lse, delta, dqt,
    )

    up_p, down_p = both_ways(far_grads[2], far_grads[3], Y_RING)
    up_o, down_o = both_ways(far_grads[0], far_grads[1], Z_RING)

    def plus_lower(kept, added):
        return jnp.concatenate([total(kept[:half], added), kept[half:]], axis=0)

    def plus_upper(kept, added):
        return jnp.concatenate([kept[:half], total(kept[half:], added)], axis=0)

    p_up, p_down = both_ways(plus_lower(p_n, up_p), plus_upper(p_p, down_p), Y_RING)
    o_up, o_down = both_ways(plus_lower(o_n, up_o), plus_upper(o_p, down_o), Z_RING)

    def scatter_near(parts, ring):
        part = parts.reshape(4, 2 * rows, HEAD_SIZE)
        got = exchange([(part[3], ring[2]), (part[1], ring[-1]), (part[2], ring[1])])
        return total(part[0], *got)

    p_part, dq_other, delta_other = in_step(
        total(p_0, p_up, p_down), dq[rows:], delta_sum.reshape(-1)[rows:]
    )
    partner_sum = scatter_near(p_part, Z_RING)
    dq_in = send(dq_other, PAIR)
    delta_sum = delta_sum.reshape(-1)[:rows] + send(delta_other, PAIR)
    own_sum = scatter_near(total(o_0, o_up, o_down), Y_RING)
    back = send(partner_sum, PAIR)
    delta_sum = delta_sum + lax.ppermute(delta_sum, "tensor", [(0, 1), (1, 0)])
    query_grads = columns_of(dq[:rows], dq_in)
    key_grads = columns_of(own_sum[:rows], back[:rows])
    value_grads = columns_of(own_sum[rows:], back[rows:])
    return query_grads, key_grads, value_grads, (1.0 - gate) * delta_sum


def solution(mesh):
    in_specs = (
        P(("dp", "seq"), "tensor"),
        P(("dp", "seq"), "tensor"),
        P(("dp", "seq"), "tensor"),
        P(("dp", "seq"), "tensor"),
        P(("dp", "seq")),
        P("dp", None),
        P("dp"),
    )
    out_specs = (
        P(("dp", "seq"), "tensor"),
        P(("dp", "seq"), "tensor"),
        P(("dp", "seq"), "tensor"),
        P(("dp", "seq")),
    )
    return jax.shard_map(local, mesh=mesh, in_specs=in_specs, out_specs=out_specs, check_vma=False)
```

time: 216 us -> 149 us (0.69)
  waiting for transfers between devices: 102 us -> 26.7 us
  starting transfers between devices: 55.1 us -> 65.3 us
    ppermute x30 -> x33, waiting for transfers between devices: 102 us -> 24.1 us  [send(): return lax.ppermute(a, 'seq', perm)]
    ppermute x30 -> x33, starting transfers between devices: 54.5 us -> 64.4 us  [send(): return lax.ppermute(a, 'seq', perm)]
    ppermute x1, waiting for transfers between devices: 0.01 us -> 2.63 us  [local(): delta_sum = delta_sum + lax.ppermute(delta_sum, 'tensor', [(0, 1), (1, 0)])]
    pallas_call x1 -> x4, Pallas kernels: 44.8 us -> 45.8 us  [the longest x3 41.9 us: call(): pl.pallas_call(kernel, out_shape=outs, in_specs=[sm] + [vm] * (len(args)...]
  transfers between devices with their start and end apart: 31 -> 34, of which waited for: 18 -> 9; matrix products, arithmetic and copies ran while one was open for 3% -> 4% of each run, Pallas kernels for 0% -> 25%
where the time goes in v3:
time: 149 us
  starting transfers between devices  65.3 us (44%)
  Pallas kernels  45.8 us (31%)
  waiting for transfers between devices  26.7 us (18%)
  other arithmetic  6.8 us (5%)
  local copies, waits for them, and re-layouts  3.56 us (2%)
    ppermute x33, starting transfers between devices, send(): return lax.ppermute(a, 'seq', perm)  64.4 us
    pallas_call x3, Pallas kernels, call(): pl.pallas_call(kernel, out_shape=outs, in_specs=[sm] + [vm] * (len(args)...  41.9 us
    ppermute x33, waiting for transfers between devices, send(): return lax.ppermute(a, 'seq', perm)  24.1 us
    pallas_call x1, Pallas kernels, local(): pl.pallas_call(table_kernel, out_shape=shape(TABLE, dtype=jnp.int32), in_...  3.92 us
  transfers between devices with their start and end apart: 34, of which 9 were waited for; matrix products, arithmetic and copies ran while one was open for 4% of the time, Pallas kernels for 25%

profile of v3, /device:TPU:0, one launch (start us, length us, event | category | flops | bytes accessed | tf_op | source)
XLA Modules:
  0.0 149.3 jit_solution(17480914433609150490)
XLA Ops:
  0.7 1.0 constant_dynamic-update-slice_fusion.4
  1.7 9.1 %collective-permute-start = (bf16[512,128]{1,0:T(8,128)(2,1)S(1)}, bf16[512,128]{1,0:T(8,128)(2,1)S(1)}, u32[]{:S(2)}, u32[]{:S(2)}) collective-permute-start(bf16[512,128]{1,0:T(8,128)(2,1)S(1)} %pad_maximum_fusion.9), channel_id=1, source_target_pairs={{0,62},{2,60},{4,58},{6,56},{8,54},{10,52},{12,50},{14,48},{16,46}... | collective-permute-start | bytes 393224 | tf_op jit(solution)/shard_map/ppermute | solution.py:349
  10.8 0.7 collective-permute-start.5
  11.5 0.5 collective-permute-start.6
  12.0 2.8 %collective-permute-start.7 = (bf16[512,128]{1,0:T(8,128)(2,1)S(1)}, bf16[512,128]{1,0:T(8,128)(2,1)S(1)}, u32[]{:S(2)}, u32[]{:S(2)}) collective-permute-start(bf16[512,128]{1,0:T(8,128)(2,1)S(1)} %pad_maximum_fusion.10), channel_id=1, source_target_pairs={{0,6},{2,0},{4,2},{6,4},{8,14},{10,8},{12,10},{14,12},{16,22},{18,... | collective-permute-start | bytes 393224 | tf_op jit(solution)/shard_map/ppermute | solution.py:349
  15.0 0.9 copy-done.2
  15.8 0.8 broadcast_select_fusion.2
  16.6 0.9 pad_maximum_fusion.1
  17.7 1.1 collective-permute-done.5
  18.8 2.0 %collective-permute-start.3 = (bf16[512,128]{1,0:T(8,128)(2,1)S(1)}, bf16[512,128]{1,0:T(8,128)(2,1)S(1)}, u32[]{:S(2)}, u32[]{:S(2)}) collective-permute-start(bf16[512,128]{1,0:T(8,128)(2,1)S(1)} %collective-permute-done), channel_id=1, source_target_pairs={{0,24},{2,26},{4,28},{6,30},{8,0},{10,2},{12,4},{14,6},{16,8},{18,... | collective-permute-start | bytes 393224 | tf_op jit(solution)/shard_map/ppermute | solution.py:349
  20.8 0.3 collective-permute-start.8
  21.2 3.0 %collective-permute-start.9 = (bf16[2048,128]{1,0:T(8,128)(2,1)S(1)}, bf16[2048,128]{1,0:T(8,128)(2,1)S(1)}, u32[]{:S(2)}, u32[]{:S(2)}) collective-permute-start(bf16[2048,128]{1,0:T(8,128)(2,1)S(1)} %constant_dynamic-update-slice_fusion.p0), channel_id=1, source_target_pairs={{0,24},{2,26},{4,28},{6,30},{8,0},{10,2},{12,4},{14,6},{16,8},{18,... | collective-permute-start | bytes 1572872 | tf_op jit(solution)/shard_map/ppermute | solution.py:349
  24.1 1.3 collective-permute-done.1
  25.4 1.0 collective-permute-done.2
  26.6 3.2 %collective-permute-start.11 = (bf16[2048,128]{1,0:T(8,128)(2,1)S(1)}, bf16[2048,128]{1,0:T(8,128)(2,1)S(1)}, u32[]{:S(2)}, u32[]{:S(2)}) collective-permute-start(bf16[2048,128]{1,0:T(8,128)(2,1)S(1)} %pad_maximum_fusion.p3), channel_id=1, source_target_pairs={{0,6},{2,0},{4,2},{6,4},{8,14},{10,8},{12,10},{14,12},{16,22},{18,... | collective-permute-start | bytes 1572872 | tf_op jit(solution)/shard_map/ppermute | solution.py:349
  29.8 4.8 %collective-permute-start.4 = (bf16[256,1024]{1,0:T(8,128)(2,1)}, bf16[256,1024]{1,0:T(8,128)(2,1)}, u32[]{:S(2)}, u32[]{:S(2)}) collective-permute-start(bf16[256,1024]{1,0:T(8,128)(2,1)} %pad_maximum_fusion.1), channel_id=1, source_target_pairs={{0,62},{2,60},{4,58},{6,56},{8,54},{10,52},{12,50},{14,48},{16,46}... | collective-permute-start | bytes 1572872 | tf_op jit(solution)/shard_map/ppermute | solution.py:349
  34.7 0.6 reshape.38.ids
  35.3 3.9 %block_table.1.tab = s32[76]{0:T(128)} custom-call(s32[1]{0:T(128)} %bitcast.place_ref, s32[64]{0:T(128)} %reshape.38.ids, s32[32]{0:T(128)} %counts.1), custom_call_target="tpu_custom_call" | custom-call | tf_op jit(solution)/shard_map/block_table/pallas_call | solution.py:392
  39.2 8.9 %collective-permute-done.8.p1 = bf16[2048,128]{1,0:T(8,128)(2,1)S(1)} collective-permute-done((bf16[2048,128]{1,0:T(8,128)(2,1)S(1)}, bf16[2048,128]{1,0:T(8,128)(2,1)S(1)}, u32[]{:S(2)}, u32[]{:S(2)}) %collective-permute-start.8) | collective-permute-done | bytes 524320 | tf_op jit(solution)/shard_map/ppermute | solution.py:349
  48.2 0.4 collective-permute-start.12
  48.5 2.9 %collective-permute-start.13 = (bf16[1024,128]{1,0:T(8,128)(2,1)S(1)}, bf16[1024,128]{1,0:T(8,128)(2,1)S(1)}, u32[]{:S(2)}, u32[]{:S(2)}) collective-permute-start(bf16[1024,128]{1,0:T(8,128)(2,1)S(1)} %slice.139), channel_id=1, source_target_pairs={{0,24},{2,26},{4,28},{6,30},{8,0},{10,2},{12,4},{14,6},{16,8},{18,... | collective-permute-start | bytes 786440 | tf_op jit(solution)/shard_map/ppermute | solution.py:349
  51.6 3.2 %collective-permute-start.15 = (bf16[1024,128]{1,0:T(8,128)(2,1)S(1)}, bf16[1024,128]{1,0:T(8,128)(2,1)S(1)}, u32[]{:S(2)}, u32[]{:S(2)}) collective-permute-start(bf16[1024,128]{1,0:T(8,128)(2,1)S(1)} %slice.141), channel_id=1, source_target_pairs={{0,6},{2,0},{4,2},{6,4},{8,14},{10,8},{12,10},{14,12},{16,22},{18,... | collective-permute-start | bytes 786440 | tf_op jit(solution)/shard_map/ppermute | solution.py:349
  54.8 1.1 fusion.2
  56.0 0.6 copy-done
  56.6 11.6 %near_stats.1 = (f32[4,8,512]{2,1,0:T(8,128)S(1)}, f32[4,8,512]{2,1,0:T(8,128)S(1)}, f32[4,8,512]{2,1,0:T(8,128)S(1)}) custom-call(s32[76]{0:T(128)S(1)} %copy-done, bf16[512,512]{1,0:T(8,128)(2,1)S(1)} %pad_maximum_fusion.2.q, bf16[512,512]{1,0:T(8,128)(2,1)S(1)} %pad_maximum_fusion.3.do, bf16[2048,128]{1,0:T(8,128)(2,1)S(1)} %constant_dynamic-update-slice_fusion.p0, ...), custom_call_target="tpu_custom_call" | custom-call | flops 6442450944 | bytes 6291456 | tf_op jit(solution)/shard_map/near_stats/pallas_call | solution.py:316
  68.2 9.1 %far_grads.1 = (bf16[1024,128]{1,0:T(8,128)(2,1)S(1)}, bf16[1024,128]{1,0:T(8,128)(2,1)S(1)}, bf16[1024,128]{1,0:T(8,128)(2,1)S(1)}, bf16[1024,128]{1,0:T(8,128)...) custom-call(s32[76]{0:T(128)S(1)} %copy-done, ...), custom_call_target="tpu_custom_call" | custom-call | flops 7516192768 | bytes 2097152 | tf_op jit(solution)/shard_map/far_grads/pallas_call | solution.py:316
  77.4 3.2 %collective-permute-start.22 = (bf16[1024,128]{1,0:T(8,128)(2,1)S(1)}, bf16[1024,128]{1,0:T(8,128)(2,1)S(1)}, u32[]{:S(2)}, u32[]{:S(2)}) collective-permute-start(bf16[1024,128]{1,0:T(8,128)(2,1)S(1)} %get-tuple-element.140), channel_id=1, source_target_pairs={{0,24},{2,26},{4,28},{6,30},{8,0},{10,2},{12,4},{14,6},{16,8},{18,... | collective-permute-start | bytes 786440 | tf_op jit(solution)/shard_map/ppermute | solution.py:349
  80.7 3.2 %collective-permute-start.17 = (bf16[1024,128]{1,0:T(8,128)(2,1)S(1)}, bf16[1024,128]{1,0:T(8,128)(2,1)S(1)}, u32[]{:S(2)}, u32[]{:S(2)}) collective-permute-start(bf16[1024,128]{1,0:T(8,128)(2,1)S(1)} %get-tuple-element.125), channel_id=1, source_target_pairs={{0,6},{2,0},{4,2},{6,4},{8,14},{10,8},{12,10},{14,12},{16,22},{18,... | collective-permute-start | bytes 786440 | tf_op jit(solution)/shard_map/ppermute | solution.py:349
  83.9 21.2 %near_grads.1 = (bf16[512,512]{1,0:T(8,128)(2,1)S(1)}, bf16[2048,128]{1,0:T(8,128)(2,1)S(1)}, bf16[2048,128]{1,0:T(8,128)(2,1)S(1)}, bf16[2048,128]{1,0:T(8,128)...) custom-call(s32[76]{0:T(128)S(1)} %copy-done, ...), custom_call_target="tpu_custom_call" | custom-call | flops 16106127360 | bytes 6291456 | tf_op jit(solution)/shard_map/near_grads/pallas_call | solution.py:316
  105.7 3.2 %collective-permute-start.19 = (bf16[2048,128]{1,0:T(8,128)(2,1)S(1)}, bf16[2048,128]{1,0:T(8,128)(2,1)S(1)}, u32[]{:S(2)}, u32[]{:S(2)}) collective-permute-start(bf16[2048,128]{1,0:T(8,128)(2,1)S(1)} %pad_maximum_fusion.5), channel_id=1, source_target_pairs={{0,6},{2,0},{4,2},{6,4},{8,14},{10,8},{12,10},{14,12},{16,22},{18,... | collective-permute-start | bytes 1572872 | tf_op jit(solution)/shard_map/ppermute | solution.py:349
  109.2 3.2 %collective-permute-start.24 = (bf16[2048,128]{1,0:T(8,128)(2,1)S(1)}, bf16[2048,128]{1,0:T(8,128)(2,1)S(1)}, u32[]{:S(2)}, u32[]{:S(2)}) collective-permute-start(bf16[2048,128]{1,0:T(8,128)(2,1)S(1)} %pad_maximum_fusion.8), channel_id=1, source_target_pairs={{0,24},{2,26},{4,28},{6,30},{8,0},{10,2},{12,4},{14,6},{16,8},{18,... | collective-permute-start | bytes 1572872 | tf_op jit(solution)/shard_map/ppermute | solution.py:349
  112.4 6.1 %collective-permute-done.18 = bf16[2048,128]{1,0:T(8,128)(2,1)S(1)} collective-permute-done((bf16[2048,128]{1,0:T(8,128)(2,1)S(1)}, bf16[2048,128]{1,0:T(8,128)(2,1)S(1)}, u32[]{:S(2)}, u32[]{:S(2)}) %collective-permute-start.18) | collective-permute-done | bytes 524320 | tf_op jit(solution)/shard_map/ppermute | solution.py:349
  118.7 2.6 %collective-permute-start.32 = (f32[256]{0:T(256)S(1)}, f32[256]{0:T(256)S(1)}, u32[]{:S(2)}, u32[]{:S(2)}) collective-permute-start(f32[256]{0:T(256)S(1)} %bitcast.4), channel_id=1, source_target_pairs={{0,62},{2,60},{4,58},{6,56},{8,54},{10,52},{12,50},{14,48},{16,46}... | collective-permute-start | bytes 3080 | tf_op jit(solution)/shard_map/ppermute | solution.py:349
  121.3 5.2 %collective-permute-start.20 = (bf16[256,512]{1,0:T(8,128)(2,1)S(1)}, bf16[256,512]{1,0:T(8,128)(2,1)S(1)}, u32[]{:S(2)}, u32[]{:S(2)}) collective-permute-start(bf16[256,512]{1,0:T(8,128)(2,1)S(1)} %slice.147), channel_id=1, source_target_pairs={{0,62},{2,60},{4,58},{6,56},{8,54},{10,52},{12,50},{14,48},{16,46}... | collective-permute-start | bytes 786440 | tf_op jit(solution)/shard_map/ppermute | solution.py:349
  126.8 2.0 %collective-permute-start.30 = (bf16[512,128]{1,0:T(8,128)(2,1)S(1)}, bf16[512,128]{1,0:T(8,128)(2,1)S(1)}, u32[]{:S(2)}, u32[]{:S(2)}) collective-permute-start(bf16[512,128]{1,0:T(8,128)(2,1)S(1)} %get-tuple-element.157), channel_id=1, source_target_pairs={{0,8},{2,10},{4,12},{6,14},{8,16},{10,18},{12,20},{14,22},{16,24},... | collective-permute-start | bytes 393224 | tf_op jit(solution)/shard_map/ppermute | solution.py:349
  129.0 1.0 collective-permute-start.33
  130.0 2.6 %collective-permute-done.33 = f32[256]{0:T(256)S(1)} collective-permute-done((f32[256]{0:T(256)S(1)}, f32[256]{0:T(256)S(1)}, u32[]{:S(2)}, u32[]{:S(2)}) %collective-permute-start.33) | collective-permute-done | bytes 1056 | tf_op jit(solution)/shard_map/ppermute | solution.py:464
  132.6 0.2 collective-permute-start.25
  132.9 0.6 add_multiply_fusion
  133.5 1.3 collective-permute-done.28
  134.8 2.1 %collective-permute-start.26 = (bf16[512,128]{1,0:T(8,128)(2,1)S(1)}, bf16[512,128]{1,0:T(8,128)(2,1)S(1)}, u32[]{:S(2)}, u32[]{:S(2)}) collective-permute-start(bf16[512,128]{1,0:T(8,128)(2,1)S(1)} %get-tuple-element.149), channel_id=1, source_target_pairs={{0,6},{2,0},{4,2},{6,4},{8,14},{10,8},{12,10},{14,12},{16,22},{18,... | collective-permute-start | bytes 393224 | tf_op jit(solution)/shard_map/ppermute | solution.py:349
  136.8 0.3 collective-permute-start.27
  137.2 5.4 %collective-permute-start.31 = (bf16[512,128]{1,0:T(8,128)(2,1)S(1)}, bf16[512,128]{1,0:T(8,128)(2,1)S(1)}, u32[]{:S(2)}, u32[]{:S(2)}) collective-permute-start(bf16[512,128]{1,0:T(8,128)(2,1)S(1)} %add_convert_fusion.6), channel_id=1, source_target_pairs={{0,62},{2,60},{4,58},{6,56},{8,54},{10,52},{12,50},{14,48},{16,46}... | collective-permute-start | bytes 393224 | tf_op jit(solution)/shard_map/ppermute | solution.py:349
  142.6 0.4 collective-permute-done.27
  143.1 0.9 pad_maximum_fusion.6
  144.0 4.0 %collective-permute-done.31 = bf16[512,128]{1,0:T(8,128)(2,1)S(1)} collective-permute-done((bf16[512,128]{1,0:T(8,128)(2,1)S(1)}, bf16[512,128]{1,0:T(8,128)(2,1)S(1)}, u32[]{:S(2)}, u32[]{:S(2)}) %collective-permute-start.31) | collective-permute-done | bytes 131104 | tf_op jit(solution)/shard_map/ppermute | solution.py:349
  148.0 0.7 pad_maximum_fusion.12
  148.7 0.7 pad_maximum_fusion.11
  (86 shorter events, 2.7 us)
Async XLA Ops:
  0.6 1.0 copy-start.4
  0.6 14.1 %copy-start.3 = (bf16[256,1024]{1,0:T(8,128)(2,1)S(1)}, bf16[256,1024]{1,0:T(8,128)(2,1)}, u32[]{:S(2)}) copy-start(bf16[256,1024]{1,0:T(8,128)(2,1)} %param.10) | copy-start | bytes 1572868
  1.7 15.8 %collective-permute-start = (bf16[512,128]{1,0:T(8,128)(2,1)S(1)}, bf16[512,128]{1,0:T(8,128)(2,1)S(1)}, u32[]{:S(2)}, u32[]{:S(2)}) collective-permute-start(bf16[512,128]{1,0:T(8,128)(2,1)S(1)} %pad_maximum_fusion.9), channel_id=1, source_target_pairs={{0,62},{2,60},{4,58},{6,56},{8,54},{10,52},{12,50},{14,48},{16,46}... | collective-permute-start | bytes 393224 | tf_op jit(solution)/shard_map/ppermute | solution.py:349
  10.8 4.0 %copy-start.5 = (f32[256]{0:T(256)S(1)}, f32[256]{0:T(256)}, u32[]{:S(2)}) copy-start(f32[256]{0:T(256)} %param.11) | copy-start | bytes 3076
  10.8 8.0 %collective-permute-start.5 = (bf16[512,128]{1,0:T(8,128)(2,1)S(1)}, bf16[512,128]{1,0:T(8,128)(2,1)S(1)}, u32[]{:S(2)}, u32[]{:S(2)}) collective-permute-start(bf16[512,128]{1,0:T(8,128)(2,1)S(1)} %pad_maximum_fusion.10), channel_id=1, source_target_pairs={{0,4},{2,6},{4,0},{6,2},{8,12},{10,14},{12,8},{14,10},{16,20},{18,... | collective-permute-start | bytes 393224 | tf_op jit(solution)/shard_map/ppermute | solution.py:349
  11.5 9.2 %collective-permute-start.6 = (bf16[512,128]{1,0:T(8,128)(2,1)S(1)}, bf16[512,128]{1,0:T(8,128)(2,1)S(1)}, u32[]{:S(2)}, u32[]{:S(2)}) collective-permute-start(bf16[512,128]{1,0:T(8,128)(2,1)S(1)} %pad_maximum_fusion.10), channel_id=1, source_target_pairs={{0,2},{2,4},{4,6},{6,0},{8,10},{10,12},{12,14},{14,8},{16,18},{18,... | collective-permute-start | bytes 393224 | tf_op jit(solution)/shard_map/ppermute | solution.py:349
  12.0 8.8 %collective-permute-start.7 = (bf16[512,128]{1,0:T(8,128)(2,1)S(1)}, bf16[512,128]{1,0:T(8,128)(2,1)S(1)}, u32[]{:S(2)}, u32[]{:S(2)}) collective-permute-start(bf16[512,128]{1,0:T(8,128)(2,1)S(1)} %pad_maximum_fusion.10), channel_id=1, source_target_pairs={{0,6},{2,0},{4,2},{6,4},{8,14},{10,8},{12,10},{14,12},{16,22},{18,... | collective-permute-start | bytes 393224 | tf_op jit(solution)/shard_map/ppermute | solution.py:349
  14.8 1.1 copy-start.2
  17.5 7.9 %collective-permute-start.1 = (bf16[512,128]{1,0:T(8,128)(2,1)S(1)}, bf16[512,128]{1,0:T(8,128)(2,1)S(1)}, u32[]{:S(2)}, u32[]{:S(2)}) collective-permute-start(bf16[512,128]{1,0:T(8,128)(2,1)S(1)} %collective-permute-done), channel_id=1, source_target_pairs={{0,16},{2,18},{4,20},{6,22},{8,24},{10,26},{12,28},{14,30},{16,0},... | collective-permute-start | bytes 393224 | tf_op jit(solution)/shard_map/ppermute | solution.py:349
  17.5 9.0 %collective-permute-start.2 = (bf16[512,128]{1,0:T(8,128)(2,1)S(1)}, bf16[512,128]{1,0:T(8,128)(2,1)S(1)}, u32[]{:S(2)}, u32[]{:S(2)}) collective-permute-start(bf16[512,128]{1,0:T(8,128)(2,1)S(1)} %collective-permute-done), channel_id=1, source_target_pairs={{0,8},{2,10},{4,12},{6,14},{8,16},{10,18},{12,20},{14,22},{16,24},... | collective-permute-start | bytes 393224 | tf_op jit(solution)/shard_map/ppermute | solution.py:349
  18.8 7.7 %collective-permute-start.3 = (bf16[512,128]{1,0:T(8,128)(2,1)S(1)}, bf16[512,128]{1,0:T(8,128)(2,1)S(1)}, u32[]{:S(2)}, u32[]{:S(2)}) collective-permute-start(bf16[512,128]{1,0:T(8,128)(2,1)S(1)} %collective-permute-done), channel_id=1, source_target_pairs={{0,24},{2,26},{4,28},{6,30},{8,0},{10,2},{12,4},{14,6},{16,8},{18,... | collective-permute-start | bytes 393224 | tf_op jit(solution)/shard_map/ppermute | solution.py:349
  20.8 13.8 %copy-start.6 = (s32[32,2]{0,1:T(2,128)S(1)}, s32[32,2]{0,1:T(2,128)}, u32[]{:S(2)}) copy-start(s32[32,2]{0,1:T(2,128)} %param.12) | copy-start | bytes 772
  20.8 27.3 %collective-permute-start.8 = (bf16[2048,128]{1,0:T(8,128)(2,1)S(1)}, bf16[2048,128]{1,0:T(8,128)(2,1)S(1)}, u32[]{:S(2)}, u32[]{:S(2)}) collective-permute-start(bf16[2048,128]{1,0:T(8,128)(2,1)S(1)} %constant_dynamic-update-slice_fusion.p0), channel_id=1, source_target_pairs={{0,8},{2,10},{4,12},{6,14},{8,16},{10,18},{12,20},{14,22},{16,24},... | collective-permute-start | bytes 1572872 | tf_op jit(solution)/shard_map/ppermute | solution.py:349
  21.2 26.9 %collective-permute-start.9 = (bf16[2048,128]{1,0:T(8,128)(2,1)S(1)}, bf16[2048,128]{1,0:T(8,128)(2,1)S(1)}, u32[]{:S(2)}, u32[]{:S(2)}) collective-permute-start(bf16[2048,128]{1,0:T(8,128)(2,1)S(1)} %constant_dynamic-update-slice_fusion.p0), channel_id=1, source_target_pairs={{0,24},{2,26},{4,28},{6,30},{8,0},{10,2},{12,4},{14,6},{16,8},{18,... | collective-permute-start | bytes 1572872 | tf_op jit(solution)/shard_map/ppermute | solution.py:349
  26.5 25.0 %collective-permute-start.10 = (bf16[2048,128]{1,0:T(8,128)(2,1)S(1)}, bf16[2048,128]{1,0:T(8,128)(2,1)S(1)}, u32[]{:S(2)}, u32[]{:S(2)}) collective-permute-start(bf16[2048,128]{1,0:T(8,128)(2,1)S(1)} %pad_maximum_fusion.p3), channel_id=1, source_target_pairs={{0,2},{2,4},{4,6},{6,0},{8,10},{10,12},{12,14},{14,8},{16,18},{18,... | collective-permute-start | bytes 1572872 | tf_op jit(solution)/shard_map/ppermute | solution.py:349
  26.6 24.9 %collective-permute-start.11 = (bf16[2048,128]{1,0:T(8,128)(2,1)S(1)}, bf16[2048,128]{1,0:T(8,128)(2,1)S(1)}, u32[]{:S(2)}, u32[]{:S(2)}) collective-permute-start(bf16[2048,128]{1,0:T(8,128)(2,1)S(1)} %pad_maximum_fusion.p3), channel_id=1, source_target_pairs={{0,6},{2,0},{4,2},{6,4},{8,14},{10,8},{12,10},{14,12},{16,22},{18,... | collective-permute-start | bytes 1572872 | tf_op jit(solution)/shard_map/ppermute | solution.py:349
  29.8 25.0 %collective-permute-start.4 = (bf16[256,1024]{1,0:T(8,128)(2,1)}, bf16[256,1024]{1,0:T(8,128)(2,1)}, u32[]{:S(2)}, u32[]{:S(2)}) collective-permute-start(bf16[256,1024]{1,0:T(8,128)(2,1)} %pad_maximum_fusion.1), channel_id=1, source_target_pairs={{0,62},{2,60},{4,58},{6,56},{8,54},{10,52},{12,50},{14,48},{16,46}... | collective-permute-start | bytes 1572872 | tf_op jit(solution)/shard_map/ppermute | solution.py:349
  48.2 20.0 %collective-permute-start.12 = (bf16[1024,128]{1,0:T(8,128)(2,1)S(1)}, bf16[1024,128]{1,0:T(8,128)(2,1)S(1)}, u32[]{:S(2)}, u32[]{:S(2)}) collective-permute-start(bf16[1024,128]{1,0:T(8,128)(2,1)S(1)} %slice.138), channel_id=1, source_target_pairs={{0,8},{2,10},{4,12},{6,14},{8,16},{10,18},{12,20},{14,22},{16,24},... | collective-permute-start | bytes 786440 | tf_op jit(solution)/shard_map/ppermute | solution.py:349
  48.5 19.7 %collective-permute-start.13 = (bf16[1024,128]{1,0:T(8,128)(2,1)S(1)}, bf16[1024,128]{1,0:T(8,128)(2,1)S(1)}, u32[]{:S(2)}, u32[]{:S(2)}) collective-permute-start(bf16[1024,128]{1,0:T(8,128)(2,1)S(1)} %slice.139), channel_id=1, source_target_pairs={{0,24},{2,26},{4,28},{6,30},{8,0},{10,2},{12,4},{14,6},{16,8},{18,... | collective-permute-start | bytes 786440 | tf_op jit(solution)/shard_map/ppermute | solution.py:349
  51.5 4.4 %copy-start.1 = (bf16[256,512]{1,0:T(8,128)(2,1)S(1)}, bf16[256,512]{1,0:T(8,128)(2,1)}, u32[]{:S(2)}) copy-start(bf16[256,512]{1,0:T(8,128)(2,1)} %get-tuple-element.174) | copy-start | bytes 786436
  51.5 16.7 %collective-permute-start.14 = (bf16[1024,128]{1,0:T(8,128)(2,1)S(1)}, bf16[1024,128]{1,0:T(8,128)(2,1)S(1)}, u32[]{:S(2)}, u32[]{:S(2)}) collective-permute-start(bf16[1024,128]{1,0:T(8,128)(2,1)S(1)} %slice.140), channel_id=1, source_target_pairs={{0,2},{2,4},{4,6},{6,0},{8,10},{10,12},{12,14},{14,8},{16,18},{18,... | collective-permute-start | bytes 786440 | tf_op jit(solution)/shard_map/ppermute | solution.py:349
  51.6 16.6 %collective-permute-start.15 = (bf16[1024,128]{1,0:T(8,128)(2,1)S(1)}, bf16[1024,128]{1,0:T(8,128)(2,1)S(1)}, u32[]{:S(2)}, u32[]{:S(2)}) collective-permute-start(bf16[1024,128]{1,0:T(8,128)(2,1)S(1)} %slice.141), channel_id=1, source_target_pairs={{0,6},{2,0},{4,2},{6,4},{8,14},{10,8},{12,10},{14,12},{16,22},{18,... | collective-permute-start | bytes 786440 | tf_op jit(solution)/shard_map/ppermute | solution.py:349
  56.0 0.7 copy-start
  77.3 27.9 %collective-permute-start.21 = (bf16[1024,128]{1,0:T(8,128)(2,1)S(1)}, bf16[1024,128]{1,0:T(8,128)(2,1)S(1)}, u32[]{:S(2)}, u32[]{:S(2)}) collective-permute-start(bf16[1024,128]{1,0:T(8,128)(2,1)S(1)} %get-tuple-element.139), channel_id=1, source_target_pairs={{0,8},{2,10},{4,12},{6,14},{8,16},{10,18},{12,20},{14,22},{16,24},... | collective-permute-start | bytes 786440 | tf_op jit(solution)/shard_map/ppermute | solution.py:349
  77.4 27.8 %collective-permute-start.22 = (bf16[1024,128]{1,0:T(8,128)(2,1)S(1)}, bf16[1024,128]{1,0:T(8,128)(2,1)S(1)}, u32[]{:S(2)}, u32[]{:S(2)}) collective-permute-start(bf16[1024,128]{1,0:T(8,128)(2,1)S(1)} %get-tuple-element.140), channel_id=1, source_target_pairs={{0,24},{2,26},{4,28},{6,30},{8,0},{10,2},{12,4},{14,6},{16,8},{18,... | collective-permute-start | bytes 786440 | tf_op jit(solution)/shard_map/ppermute | solution.py:349
  80.7 24.7 %collective-permute-start.16 = (bf16[1024,128]{1,0:T(8,128)(2,1)S(1)}, bf16[1024,128]{1,0:T(8,128)(2,1)S(1)}, u32[]{:S(2)}, u32[]{:S(2)}) collective-permute-start(bf16[1024,128]{1,0:T(8,128)(2,1)S(1)} %get-tuple-element.124), channel_id=1, source_target_pairs={{0,2},{2,4},{4,6},{6,0},{8,10},{10,12},{12,14},{14,8},{16,18},{18,... | collective-permute-start | bytes 786440 | tf_op jit(solution)/shard_map/ppermute | solution.py:349
  80.7 24.7 %collective-permute-start.17 = (bf16[1024,128]{1,0:T(8,128)(2,1)S(1)}, bf16[1024,128]{1,0:T(8,128)(2,1)S(1)}, u32[]{:S(2)}, u32[]{:S(2)}) collective-permute-start(bf16[1024,128]{1,0:T(8,128)(2,1)S(1)} %get-tuple-element.125), channel_id=1, source_target_pairs={{0,6},{2,0},{4,2},{6,4},{8,14},{10,8},{12,10},{14,12},{16,22},{18,... | collective-permute-start | bytes 786440 | tf_op jit(solution)/shard_map/ppermute | solution.py:349
  105.6 12.9 %collective-permute-start.18 = (bf16[2048,128]{1,0:T(8,128)(2,1)S(1)}, bf16[2048,128]{1,0:T(8,128)(2,1)S(1)}, u32[]{:S(2)}, u32[]{:S(2)}) collective-permute-start(bf16[2048,128]{1,0:T(8,128)(2,1)S(1)} %pad_maximum_fusion.4), channel_id=1, source_target_pairs={{0,2},{2,4},{4,6},{6,0},{8,10},{10,12},{12,14},{14,8},{16,18},{18,... | collective-permute-start | bytes 1572872 | tf_op jit(solution)/shard_map/ppermute | solution.py:349
  105.7 12.8 %collective-permute-start.19 = (bf16[2048,128]{1,0:T(8,128)(2,1)S(1)}, bf16[2048,128]{1,0:T(8,128)(2,1)S(1)}, u32[]{:S(2)}, u32[]{:S(2)}) collective-permute-start(bf16[2048,128]{1,0:T(8,128)(2,1)S(1)} %pad_maximum_fusion.5), channel_id=1, source_target_pairs={{0,6},{2,0},{4,2},{6,4},{8,14},{10,8},{12,10},{14,12},{16,22},{18,... | collective-permute-start | bytes 1572872 | tf_op jit(solution)/shard_map/ppermute | solution.py:349
  109.1 17.6 %collective-permute-start.23 = (bf16[2048,128]{1,0:T(8,128)(2,1)S(1)}, bf16[2048,128]{1,0:T(8,128)(2,1)S(1)}, u32[]{:S(2)}, u32[]{:S(2)}) collective-permute-start(bf16[2048,128]{1,0:T(8,128)(2,1)S(1)} %pad_maximum_fusion.7), channel_id=1, source_target_pairs={{0,8},{2,10},{4,12},{6,14},{8,16},{10,18},{12,20},{14,22},{16,24},... | collective-permute-start | bytes 1572872 | tf_op jit(solution)/shard_map/ppermute | solution.py:349
  109.2 17.6 %collective-permute-start.24 = (bf16[2048,128]{1,0:T(8,128)(2,1)S(1)}, bf16[2048,128]{1,0:T(8,128)(2,1)S(1)}, u32[]{:S(2)}, u32[]{:S(2)}) collective-permute-start(bf16[2048,128]{1,0:T(8,128)(2,1)S(1)} %pad_maximum_fusion.8), channel_id=1, source_target_pairs={{0,24},{2,26},{4,28},{6,30},{8,0},{10,2},{12,4},{14,6},{16,8},{18,... | collective-permute-start | bytes 1572872 | tf_op jit(solution)/shard_map/ppermute | solution.py:349
  118.7 10.3 %collective-permute-start.32 = (f32[256]{0:T(256)S(1)}, f32[256]{0:T(256)S(1)}, u32[]{:S(2)}, u32[]{:S(2)}) collective-permute-start(f32[256]{0:T(256)S(1)} %bitcast.4), channel_id=1, source_target_pairs={{0,62},{2,60},{4,58},{6,56},{8,54},{10,52},{12,50},{14,48},{16,46}... | collective-permute-start | bytes 3080 | tf_op jit(solution)/shard_map/ppermute | solution.py:349
  121.3 21.8 %collective-permute-start.20 = (bf16[256,512]{1,0:T(8,128)(2,1)S(1)}, bf16[256,512]{1,0:T(8,128)(2,1)S(1)}, u32[]{:S(2)}, u32[]{:S(2)}) collective-permute-start(bf16[256,512]{1,0:T(8,128)(2,1)S(1)} %slice.147), channel_id=1, source_target_pairs={{0,62},{2,60},{4,58},{6,56},{8,54},{10,52},{12,50},{14,48},{16,46}... | collective-permute-start | bytes 786440 | tf_op jit(solution)/shard_map/ppermute | solution.py:349
  126.6 8.2 %collective-permute-start.28 = (bf16[512,128]{1,0:T(8,128)(2,1)S(1)}, bf16[512,128]{1,0:T(8,128)(2,1)S(1)}, u32[]{:S(2)}, u32[]{:S(2)}) collective-permute-start(bf16[512,128]{1,0:T(8,128)(2,1)S(1)} %get-tuple-element.155), channel_id=1, source_target_pairs={{0,16},{2,18},{4,20},{6,22},{8,24},{10,26},{12,28},{14,30},{16,0},... | collective-permute-start | bytes 393224 | tf_op jit(solution)/shard_map/ppermute | solution.py:349
  126.7 10.2 %collective-permute-start.29 = (bf16[512,128]{1,0:T(8,128)(2,1)S(1)}, bf16[512,128]{1,0:T(8,128)(2,1)S(1)}, u32[]{:S(2)}, u32[]{:S(2)}) collective-permute-start(bf16[512,128]{1,0:T(8,128)(2,1)S(1)} %get-tuple-element.156), channel_id=1, source_target_pairs={{0,24},{2,26},{4,28},{6,30},{8,0},{10,2},{12,4},{14,6},{16,8},{18,... | collective-permute-start | bytes 393224 | tf_op jit(solution)/shard_map/ppermute | solution.py:349
  126.8 10.4 %collective-permute-start.30 = (bf16[512,128]{1,0:T(8,128)(2,1)S(1)}, bf16[512,128]{1,0:T(8,128)(2,1)S(1)}, u32[]{:S(2)}, u32[]{:S(2)}) collective-permute-start(bf16[512,128]{1,0:T(8,128)(2,1)S(1)} %get-tuple-element.157), channel_id=1, source_target_pairs={{0,8},{2,10},{4,12},{6,14},{8,16},{10,18},{12,20},{14,22},{16,24},... | collective-permute-start | bytes 393224 | tf_op jit(solution)/shard_map/ppermute | solution.py:349
  129.0 3.6 %collective-permute-start.33 = (f32[256]{0:T(256)S(1)}, f32[256]{0:T(256)S(1)}, u32[]{:S(2)}, u32[]{:S(2)}) collective-permute-start(f32[256]{0:T(256)S(1)} %add.66), channel_id=1, source_target_pairs={{0,1},{1,0},{2,3},{3,2},{4,5},{5,4},{6,7},{7,6},{8,9},{9,8},{10,11... | collective-permute-start | bytes 3080 | tf_op jit(solution)/shard_map/ppermute | solution.py:464
  132.6 10.0 %collective-permute-start.25 = (bf16[512,128]{1,0:T(8,128)(2,1)S(1)}, bf16[512,128]{1,0:T(8,128)(2,1)S(1)}, u32[]{:S(2)}, u32[]{:S(2)}) collective-permute-start(bf16[512,128]{1,0:T(8,128)(2,1)S(1)} %get-tuple-element.148), channel_id=1, source_target_pairs={{0,4},{2,6},{4,0},{6,2},{8,12},{10,14},{12,8},{14,10},{16,20},{18,... | collective-permute-start | bytes 393224 | tf_op jit(solution)/shard_map/ppermute | solution.py:349
  134.8 7.9 %collective-permute-start.26 = (bf16[512,128]{1,0:T(8,128)(2,1)S(1)}, bf16[512,128]{1,0:T(8,128)(2,1)S(1)}, u32[]{:S(2)}, u32[]{:S(2)}) collective-permute-start(bf16[512,128]{1,0:T(8,128)(2,1)S(1)} %get-tuple-element.149), channel_id=1, source_target_pairs={{0,6},{2,0},{4,2},{6,4},{8,14},{10,8},{12,10},{14,12},{16,22},{18,... | collective-permute-start | bytes 393224 | tf_op jit(solution)/shard_map/ppermute | solution.py:349
  136.8 6.2 %collective-permute-start.27 = (bf16[512,128]{1,0:T(8,128)(2,1)S(1)}, bf16[512,128]{1,0:T(8,128)(2,1)S(1)}, u32[]{:S(2)}, u32[]{:S(2)}) collective-permute-start(bf16[512,128]{1,0:T(8,128)(2,1)S(1)} %get-tuple-element.150), channel_id=1, source_target_pairs={{0,2},{2,4},{4,6},{6,0},{8,10},{10,12},{12,14},{14,8},{16,18},{18,... | collective-permute-start | bytes 393224 | tf_op jit(solution)/shard_map/ppermute | solution.py:349
  137.2 10.8 %collective-permute-start.31 = (bf16[512,128]{1,0:T(8,128)(2,1)S(1)}, bf16[512,128]{1,0:T(8,128)(2,1)S(1)}, u32[]{:S(2)}, u32[]{:S(2)}) collective-permute-start(bf16[512,128]{1,0:T(8,128)(2,1)S(1)} %add_convert_fusion.6), channel_id=1, source_target_pairs={{0,62},{2,60},{4,58},{6,56},{8,54},{10,52},{12,50},{14,48},{16,46}... | collective-permute-start | bytes 393224 | tf_op jit(solution)/shard_map/ppermute | solution.py:349

commit v4 on v3

--- a/solution.py
+++ b/solution.py
@@ -436,8 +436,15 @@
         6144, True, ((HEAD_SIZE, LANES),), 5, "near_grads", *common, *near, lse, delta, dqt,
     )
 
-    up_p, down_p = both_ways(far_grads[2], far_grads[3], Y_RING)
-    up_o, down_o = both_ways(far_grads[0], far_grads[1], Z_RING)
+    parts = in_step(*far_grads, delta_sum.reshape(-1))
+    up_p, down_p, up_o, down_o, delta_in = in_step(
+        send(parts[2], Y_RING[1]),
+        send(parts[3], Y_RING[-1]),
+        send(parts[0], Z_RING[1]),
+        send(parts[1], Z_RING[-1]),
+        lax.ppermute(parts[4], "tensor", [(0, 1), (1, 0)]),
+    )
+    delta_sum = parts[4] + delta_in
 
     def plus_lower(kept, added):
         return jnp.concatenate([total(kept[:half], added), kept[half:]], axis=0)
@@ -453,15 +460,21 @@
         got = exchange([(part[3], ring[2]), (part[1], ring[-1]), (part[2], ring[1])])
         return total(part[0], *got)
 
-    p_part, dq_other, delta_other = in_step(
-        total(p_0, p_up, p_down), dq[rows:], delta_sum.reshape(-1)[rows:]
+    delta_own, delta_other = delta_sum.reshape(2, rows)
+    delta_high = lax.reduce_precision(delta_other, 8, 7)
+    delta_parts = jnp.concatenate([delta_high, delta_other - delta_high]).astype(bf)
+    delta_rows = jnp.pad(delta_parts.reshape(1, 2 * rows), ((0, 15), (0, 0)))
+    p_part = total(p_0, p_up, p_down)
+    own_part, dq_other = in_step(
+        total(o_0, o_up, o_down), jnp.concatenate([dq[rows:], delta_rows], axis=0)
     )
     partner_sum = scatter_near(p_part, Z_RING)
     dq_in = send(dq_other, PAIR)
-    delta_sum = delta_sum.reshape(-1)[:rows] + send(delta_other, PAIR)
-    own_sum = scatter_near(total(o_0, o_up, o_down), Y_RING)
+    own_sum = scatter_near(own_part, Y_RING)
     back = send(partner_sum, PAIR)
-    delta_sum = delta_sum + lax.ppermute(delta_sum, "tensor", [(0, 1), (1, 0)])
+    delta_in = dq_in[rows].astype(f32)
+    dq_in = dq_in[:rows]
+    delta_sum = delta_own + (delta_in[:rows] + delta_in[rows:])
     query_grads = columns_of(dq[:rows], dq_in)
     key_grads = columns_of(own_sum[:rows], back[:rows])
     value_grads = columns_of(own_sum[rows:], back[rows:])

time: 149 us -> 145 us (0.973)
  Pallas kernels: 45.8 us -> 26.3 us
  starting transfers between devices: 65.3 us -> 73.9 us
  waiting for transfers between devices: 26.7 us -> 33.7 us
    pallas_call x3, Pallas kernels: 41.9 us -> 22.4 us  [call(): pl.pallas_call(kernel, out_shape=outs, in_specs=[sm] + [vm] * (len(args)...]
    ppermute x33 -> x32, waiting for transfers between devices: 24.1 us -> 33.7 us  [send(): return lax.ppermute(a, 'seq', perm)]
    ppermute x33 -> x32, starting transfers between devices: 64.4 us -> 73.2 us  [send(): return lax.ppermute(a, 'seq', perm)]
    ppermute x1, waiting for transfers between devices: 2.63 us -> 0.01 us  [local(): lax.ppermute(parts[4], 'tensor', [(0, 1), (1, 0)])]
  transfers between devices with their start and end apart: 34 -> 33, of which waited for: 9 -> 9; matrix products, arithmetic and copies ran while one was open for 4% -> 4% of each run, Pallas kernels for 25% -> 14%
where the time goes in v4:
time: 145 us
  starting transfers between devices  73.9 us (51%)
  waiting for transfers between devices  33.7 us (23%)
  Pallas kernels  26.3 us (18%)
  other arithmetic  6.85 us (5%)
  local copies, waits for them, and re-layouts  3.57 us (2%)
    ppermute x32, starting transfers between devices, send(): return lax.ppermute(a, 'seq', perm)  73.2 us
    ppermute x32, waiting for transfers between devices, send(): return lax.ppermute(a, 'seq', perm)  33.7 us
    pallas_call x3, Pallas kernels, call(): pl.pallas_call(kernel, out_shape=outs, in_specs=[sm] + [vm] * (len(args)...  22.4 us
    pallas_call x1, Pallas kernels, local(): pl.pallas_call(table_kernel, out_shape=shape(TABLE, dtype=jnp.int32), in_...  3.92 us
  transfers between devices with their start and end apart: 33, of which 9 were waited for; matrix products, arithmetic and copies ran while one was open for 4% of the time, Pallas kernels for 14%

profile of v4, /device:TPU:0, one launch (start us, length us, event | category | flops | bytes accessed | tf_op | source)
XLA Modules:
  0.0 145.5 jit_solution(16764920345378367451)
XLA Ops:
  0.7 1.0 constant_dynamic-update-slice_fusion.4
  1.7 9.1 %collective-permute-start = (bf16[512,128]{1,0:T(8,128)(2,1)S(1)}, bf16[512,128]{1,0:T(8,128)(2,1)S(1)}, u32[]{:S(2)}, u32[]{:S(2)}) collective-permute-start(bf16[512,128]{1,0:T(8,128)(2,1)S(1)} %pad_maximum_fusion.10), channel_id=1, source_target_pairs={{0,62},{2,60},{4,58},{6,56},{8,54},{10,52},{12,50},{14,48},{16,46}... | collective-permute-start | bytes 393224 | tf_op jit(solution)/shard_map/ppermute | solution.py:349
  10.8 0.7 collective-permute-start.5
  11.5 0.5 collective-permute-start.6
  12.0 2.8 %collective-permute-start.7 = (bf16[512,128]{1,0:T(8,128)(2,1)S(1)}, bf16[512,128]{1,0:T(8,128)(2,1)S(1)}, u32[]{:S(2)}, u32[]{:S(2)}) collective-permute-start(bf16[512,128]{1,0:T(8,128)(2,1)S(1)} %pad_maximum_fusion.11), channel_id=1, source_target_pairs={{0,6},{2,0},{4,2},{6,4},{8,14},{10,8},{12,10},{14,12},{16,22},{18,... | collective-permute-start | bytes 393224 | tf_op jit(solution)/shard_map/ppermute | solution.py:349
  15.0 0.9 copy-done.2
  15.8 0.8 broadcast_select_fusion.2
  16.6 0.9 pad_maximum_fusion.1
  17.7 1.1 collective-permute-done.5
  18.8 2.0 %collective-permute-start.3 = (bf16[512,128]{1,0:T(8,128)(2,1)S(1)}, bf16[512,128]{1,0:T(8,128)(2,1)S(1)}, u32[]{:S(2)}, u32[]{:S(2)}) collective-permute-start(bf16[512,128]{1,0:T(8,128)(2,1)S(1)} %collective-permute-done), channel_id=1, source_target_pairs={{0,24},{2,26},{4,28},{6,30},{8,0},{10,2},{12,4},{14,6},{16,8},{18,... | collective-permute-start | bytes 393224 | tf_op jit(solution)/shard_map/ppermute | solution.py:349
  21.2 3.0 %collective-permute-start.9 = (bf16[2048,128]{1,0:T(8,128)(2,1)S(1)}, bf16[2048,128]{1,0:T(8,128)(2,1)S(1)}, u32[]{:S(2)}, u32[]{:S(2)}) collective-permute-start(bf16[2048,128]{1,0:T(8,128)(2,1)S(1)} %constant_dynamic-update-slice_fusion.p0), channel_id=1, source_target_pairs={{0,24},{2,26},{4,28},{6,30},{8,0},{10,2},{12,4},{14,6},{16,8},{18,... | collective-permute-start | bytes 1572872 | tf_op jit(solution)/shard_map/ppermute | solution.py:349
  24.2 1.3 collective-permute-done.1
  25.4 1.0 collective-permute-done.2
  26.6 3.2 %collective-permute-start.11 = (bf16[2048,128]{1,0:T(8,128)(2,1)S(1)}, bf16[2048,128]{1,0:T(8,128)(2,1)S(1)}, u32[]{:S(2)}, u32[]{:S(2)}) collective-permute-start(bf16[2048,128]{1,0:T(8,128)(2,1)S(1)} %pad_maximum_fusion.p3), channel_id=1, source_target_pairs={{0,6},{2,0},{4,2},{6,4},{8,14},{10,8},{12,10},{14,12},{16,22},{18,... | collective-permute-start | bytes 1572872 | tf_op jit(solution)/shard_map/ppermute | solution.py:349
  29.8 4.8 %collective-permute-start.4 = (bf16[256,1024]{1,0:T(8,128)(2,1)}, bf16[256,1024]{1,0:T(8,128)(2,1)}, u32[]{:S(2)}, u32[]{:S(2)}) collective-permute-start(bf16[256,1024]{1,0:T(8,128)(2,1)} %pad_maximum_fusion.1), channel_id=1, source_target_pairs={{0,62},{2,60},{4,58},{6,56},{8,54},{10,52},{12,50},{14,48},{16,46}... | collective-permute-start | bytes 1572872 | tf_op jit(solution)/shard_map/ppermute | solution.py:349
  34.7 0.6 reshape.78.ids
  35.3 3.9 %block_table.1.tab = s32[76]{0:T(128)} custom-call(s32[1]{0:T(128)} %bitcast.place_ref, s32[64]{0:T(128)} %reshape.78.ids, s32[32]{0:T(128)} %counts.1), custom_call_target="tpu_custom_call" | custom-call | tf_op jit(solution)/shard_map/block_table/pallas_call | solution.py:392
  39.2 8.9 %collective-permute-done.8.p1 = bf16[2048,128]{1,0:T(8,128)(2,1)S(1)} collective-permute-done((bf16[2048,128]{1,0:T(8,128)(2,1)S(1)}, bf16[2048,128]{1,0:T(8,128)(2,1)S(1)}, u32[]{:S(2)}, u32[]{:S(2)}) %collective-permute-start.8) | collective-permute-done | bytes 524320 | tf_op jit(solution)/shard_map/ppermute | solution.py:349
  48.2 0.4 collective-permute-start.12
  48.5 2.9 %collective-permute-start.13 = (bf16[1024,128]{1,0:T(8,128)(2,1)S(1)}, bf16[1024,128]{1,0:T(8,128)(2,1)S(1)}, u32[]{:S(2)}, u32[]{:S(2)}) collective-permute-start(bf16[1024,128]{1,0:T(8,128)(2,1)S(1)} %slice.143), channel_id=1, source_target_pairs={{0,24},{2,26},{4,28},{6,30},{8,0},{10,2},{12,4},{14,6},{16,8},{18,... | collective-permute-start | bytes 786440 | tf_op jit(solution)/shard_map/ppermute | solution.py:349
  51.6 3.2 %collective-permute-start.15 = (bf16[1024,128]{1,0:T(8,128)(2,1)S(1)}, bf16[1024,128]{1,0:T(8,128)(2,1)S(1)}, u32[]{:S(2)}, u32[]{:S(2)}) collective-permute-start(bf16[1024,128]{1,0:T(8,128)(2,1)S(1)} %slice.145), channel_id=1, source_target_pairs={{0,6},{2,0},{4,2},{6,4},{8,14},{10,8},{12,10},{14,12},{16,22},{18,... | collective-permute-start | bytes 786440 | tf_op jit(solution)/shard_map/ppermute | solution.py:349
  54.9 1.1 fusion.6
  56.0 0.6 copy-done
  56.6 5.8 %near_stats.1 = (f32[4,8,512]{2,1,0:T(8,128)S(1)}, f32[4,8,512]{2,1,0:T(8,128)S(1)}, f32[4,8,512]{2,1,0:T(8,128)S(1)}) custom-call(s32[76]{0:T(128)S(1)} %copy-done, bf16[512,512]{1,0:T(8,128)(2,1)S(1)} %pad_maximum_fusion.2.q, bf16[512,512]{1,0:T(8,128)(2,1)S(1)} %pad_maximum_fusion.3.do, bf16[2048,128]{1,0:T(8,128)(2,1)S(1)} %constant_dynamic-update-slice_fusion.p0, ...), custom_call_target="tpu_custom_call" | custom-call | flops 6442450944 | bytes 6291456 | tf_op jit(solution)/shard_map/near_stats/pallas_call | solution.py:316
  62.5 5.2 %far_grads.1 = (bf16[1024,128]{1,0:T(8,128)(2,1)S(1)}, bf16[1024,128]{1,0:T(8,128)(2,1)S(1)}, bf16[1024,128]{1,0:T(8,128)(2,1)S(1)}, bf16[1024,128]{1,0:T(8,128)...) custom-call(s32[76]{0:T(128)S(1)} %copy-done, ...), custom_call_target="tpu_custom_call" | custom-call | flops 7516192768 | bytes 2097152 | tf_op jit(solution)/shard_map/far_grads/pallas_call | solution.py:316
  67.7 0.7 collective-permute-start.20
  68.4 3.2 %collective-permute-start.17 = (bf16[1024,128]{1,0:T(8,128)(2,1)S(1)}, bf16[1024,128]{1,0:T(8,128)(2,1)S(1)}, u32[]{:S(2)}, u32[]{:S(2)}) collective-permute-start(bf16[1024,128]{1,0:T(8,128)(2,1)S(1)} %get-tuple-element.129), channel_id=1, source_target_pairs={{0,6},{2,0},{4,2},{6,4},{8,14},{10,8},{12,10},{14,12},{16,22},{18,... | collective-permute-start | bytes 786440 | tf_op jit(solution)/shard_map/ppermute | solution.py:349
  71.6 3.3 %collective-permute-start.18 = (bf16[1024,128]{1,0:T(8,128)(2,1)S(1)}, bf16[1024,128]{1,0:T(8,128)(2,1)S(1)}, u32[]{:S(2)}, u32[]{:S(2)}) collective-permute-start(bf16[1024,128]{1,0:T(8,128)(2,1)S(1)} %get-tuple-element.130), channel_id=1, source_target_pairs={{0,8},{2,10},{4,12},{6,14},{8,16},{10,18},{12,20},{14,22},{16,24},... | collective-permute-start | bytes 786440 | tf_op jit(solution)/shard_map/ppermute | solution.py:349
  74.9 7.6 %collective-permute-start.19 = (bf16[1024,128]{1,0:T(8,128)(2,1)S(1)}, bf16[1024,128]{1,0:T(8,128)(2,1)S(1)}, u32[]{:S(2)}, u32[]{:S(2)}) collective-permute-start(bf16[1024,128]{1,0:T(8,128)(2,1)S(1)} %get-tuple-element.131), channel_id=1, source_target_pairs={{0,24},{2,26},{4,28},{6,30},{8,0},{10,2},{12,4},{14,6},{16,8},{18,... | collective-permute-start | bytes 786440 | tf_op jit(solution)/shard_map/ppermute | solution.py:349
  82.5 11.4 %near_grads.1 = (bf16[512,512]{1,0:T(8,128)(2,1)S(1)}, bf16[2048,128]{1,0:T(8,128)(2,1)S(1)}, bf16[2048,128]{1,0:T(8,128)(2,1)S(1)}, bf16[2048,128]{1,0:T(8,128)...) custom-call(s32[76]{0:T(128)S(1)} %copy-done, ...), custom_call_target="tpu_custom_call" | custom-call | flops 16106127360 | bytes 6291456 | tf_op jit(solution)/shard_map/near_grads/pallas_call | solution.py:316
  94.6 4.4 %collective-permute-start.28 = (bf16[2048,128]{1,0:T(8,128)(2,1)S(1)}, bf16[2048,128]{1,0:T(8,128)(2,1)S(1)}, u32[]{:S(2)}, u32[]{:S(2)}) collective-permute-start(bf16[2048,128]{1,0:T(8,128)(2,1)S(1)} %pad_maximum_fusion.8), channel_id=1, source_target_pairs={{0,6},{2,0},{4,2},{6,4},{8,14},{10,8},{12,10},{14,12},{16,22},{18,... | collective-permute-start | bytes 1572872 | tf_op jit(solution)/shard_map/ppermute | solution.py:349
  99.1 1.3 collective-permute-start.21
  100.4 6.4 %collective-permute-start.22 = (bf16[2048,128]{1,0:T(8,128)(2,1)S(1)}, bf16[2048,128]{1,0:T(8,128)(2,1)S(1)}, u32[]{:S(2)}, u32[]{:S(2)}) collective-permute-start(bf16[2048,128]{1,0:T(8,128)(2,1)S(1)} %pad_maximum_fusion.5), channel_id=1, source_target_pairs={{0,24},{2,26},{4,28},{6,30},{8,0},{10,2},{12,4},{14,6},{16,8},{18,... | collective-permute-start | bytes 1572872 | tf_op jit(solution)/shard_map/ppermute | solution.py:349
  106.8 8.0 %collective-permute-done.28 = bf16[2048,128]{1,0:T(8,128)(2,1)S(1)} collective-permute-done((bf16[2048,128]{1,0:T(8,128)(2,1)S(1)}, bf16[2048,128]{1,0:T(8,128)(2,1)S(1)}, u32[]{:S(2)}, u32[]{:S(2)}) %collective-permute-start.28) | collective-permute-done | bytes 524320 | tf_op jit(solution)/shard_map/ppermute | solution.py:349
  115.3 2.0 %collective-permute-start.31 = (bf16[512,128]{1,0:T(8,128)(2,1)S(1)}, bf16[512,128]{1,0:T(8,128)(2,1)S(1)}, u32[]{:S(2)}, u32[]{:S(2)}) collective-permute-start(bf16[512,128]{1,0:T(8,128)(2,1)S(1)} %get-tuple-element.160), channel_id=1, source_target_pairs={{0,8},{2,10},{4,12},{6,14},{8,16},{10,18},{12,20},{14,22},{16,24},... | collective-permute-start | bytes 393224 | tf_op jit(solution)/shard_map/ppermute | solution.py:349
  117.3 3.6 %collective-permute-done.22 = bf16[2048,128]{1,0:T(8,128)(2,1)S(1)} collective-permute-done((bf16[2048,128]{1,0:T(8,128)(2,1)S(1)}, bf16[2048,128]{1,0:T(8,128)(2,1)S(1)}, u32[]{:S(2)}, u32[]{:S(2)}) %collective-permute-start.22) | collective-permute-done | bytes 524320 | tf_op jit(solution)/shard_map/ppermute | solution.py:349
  121.1 4.1 %collective-permute-start.23 = (bf16[272,512]{1,0:T(8,128)(2,1)S(1)}, bf16[272,512]{1,0:T(8,128)(2,1)S(1)}, u32[]{:S(2)}, u32[]{:S(2)}) collective-permute-start(bf16[272,512]{1,0:T(8,128)(2,1)S(1)} %pad_maximum_fusion.9), channel_id=1, source_target_pairs={{0,62},{2,60},{4,58},{6,56},{8,54},{10,52},{12,50},{14,48},{16,46}... | collective-permute-start | bytes 835592 | tf_op jit(solution)/shard_map/ppermute | solution.py:349
  125.2 1.5 %collective-permute-start.24 = (bf16[512,128]{1,0:T(8,128)(2,1)S(1)}, bf16[512,128]{1,0:T(8,128)(2,1)S(1)}, u32[]{:S(2)}, u32[]{:S(2)}) collective-permute-start(bf16[512,128]{1,0:T(8,128)(2,1)S(1)} %get-tuple-element.143), channel_id=1, source_target_pairs={{0,4},{2,6},{4,0},{6,2},{8,12},{10,14},{12,8},{14,10},{16,20},{18,... | collective-permute-start | bytes 393224 | tf_op jit(solution)/shard_map/ppermute | solution.py:349
  126.7 4.2 %collective-permute-start.25 = (bf16[512,128]{1,0:T(8,128)(2,1)S(1)}, bf16[512,128]{1,0:T(8,128)(2,1)S(1)}, u32[]{:S(2)}, u32[]{:S(2)}) collective-permute-start(bf16[512,128]{1,0:T(8,128)(2,1)S(1)} %get-tuple-element.144), channel_id=1, source_target_pairs={{0,6},{2,0},{4,2},{6,4},{8,14},{10,8},{12,10},{14,12},{16,22},{18,... | collective-permute-start | bytes 393224 | tf_op jit(solution)/shard_map/ppermute | solution.py:349
  130.9 0.8 collective-permute-start.26
  131.8 0.9 collective-permute-start.32
  132.8 3.9 %collective-permute-done.25 = bf16[512,128]{1,0:T(8,128)(2,1)S(1)} collective-permute-done((bf16[512,128]{1,0:T(8,128)(2,1)S(1)}, bf16[512,128]{1,0:T(8,128)(2,1)S(1)}, u32[]{:S(2)}, u32[]{:S(2)}) %collective-permute-start.25) | collective-permute-done | bytes 131104 | tf_op jit(solution)/shard_map/ppermute | solution.py:349
  136.6 1.2 collective-permute-done.26
  137.9 4.7 %collective-permute-done.32 = bf16[512,128]{1,0:T(8,128)(2,1)S(1)} collective-permute-done((bf16[512,128]{1,0:T(8,128)(2,1)S(1)}, bf16[512,128]{1,0:T(8,128)(2,1)S(1)}, u32[]{:S(2)}, u32[]{:S(2)}) %collective-permute-start.32) | collective-permute-done | bytes 131104 | tf_op jit(solution)/shard_map/ppermute | solution.py:349
  142.6 0.7 pad_maximum_fusion.13
  143.3 0.7 pad_maximum_fusion.12
  144.0 0.6 add_multiply_fusion
  144.6 0.9 pad_maximum_fusion.6
  (90 shorter events, 2.9 us)
Async XLA Ops:
  0.6 1.0 copy-start.4
  0.6 14.1 %copy-start.3 = (bf16[256,1024]{1,0:T(8,128)(2,1)S(1)}, bf16[256,1024]{1,0:T(8,128)(2,1)}, u32[]{:S(2)}) copy-start(bf16[256,1024]{1,0:T(8,128)(2,1)} %param.10) | copy-start | bytes 1572868
  1.7 15.8 %collective-permute-start = (bf16[512,128]{1,0:T(8,128)(2,1)S(1)}, bf16[512,128]{1,0:T(8,128)(2,1)S(1)}, u32[]{:S(2)}, u32[]{:S(2)}) collective-permute-start(bf16[512,128]{1,0:T(8,128)(2,1)S(1)} %pad_maximum_fusion.10), channel_id=1, source_target_pairs={{0,62},{2,60},{4,58},{6,56},{8,54},{10,52},{12,50},{14,48},{16,46}... | collective-permute-start | bytes 393224 | tf_op jit(solution)/shard_map/ppermute | solution.py:349
  10.8 4.0 %copy-start.5 = (f32[256]{0:T(256)S(1)}, f32[256]{0:T(256)}, u32[]{:S(2)}) copy-start(f32[256]{0:T(256)} %param.11) | copy-start | bytes 3076
  10.8 8.0 %collective-permute-start.5 = (bf16[512,128]{1,0:T(8,128)(2,1)S(1)}, bf16[512,128]{1,0:T(8,128)(2,1)S(1)}, u32[]{:S(2)}, u32[]{:S(2)}) collective-permute-start(bf16[512,128]{1,0:T(8,128)(2,1)S(1)} %pad_maximum_fusion.11), channel_id=1, source_target_pairs={{0,4},{2,6},{4,0},{6,2},{8,12},{10,14},{12,8},{14,10},{16,20},{18,... | collective-permute-start | bytes 393224 | tf_op jit(solution)/shard_map/ppermute | solution.py:349
  11.5 9.2 %collective-permute-start.6 = (bf16[512,128]{1,0:T(8,128)(2,1)S(1)}, bf16[512,128]{1,0:T(8,128)(2,1)S(1)}, u32[]{:S(2)}, u32[]{:S(2)}) collective-permute-start(bf16[512,128]{1,0:T(8,128)(2,1)S(1)} %pad_maximum_fusion.11), channel_id=1, source_target_pairs={{0,2},{2,4},{4,6},{6,0},{8,10},{10,12},{12,14},{14,8},{16,18},{18,... | collective-permute-start | bytes 393224 | tf_op jit(solution)/shard_map/ppermute | solution.py:349
  12.0 8.8 %collective-permute-start.7 = (bf16[512,128]{1,0:T(8,128)(2,1)S(1)}, bf16[512,128]{1,0:T(8,128)(2,1)S(1)}, u32[]{:S(2)}, u32[]{:S(2)}) collective-permute-start(bf16[512,128]{1,0:T(8,128)(2,1)S(1)} %pad_maximum_fusion.11), channel_id=1, source_target_pairs={{0,6},{2,0},{4,2},{6,4},{8,14},{10,8},{12,10},{14,12},{16,22},{18,... | collective-permute-start | bytes 393224 | tf_op jit(solution)/shard_map/ppermute | solution.py:349
  14.8 1.1 copy-start.2
  17.5 7.9 %collective-permute-start.1 = (bf16[512,128]{1,0:T(8,128)(2,1)S(1)}, bf16[512,128]{1,0:T(8,128)(2,1)S(1)}, u32[]{:S(2)}, u32[]{:S(2)}) collective-permute-start(bf16[512,128]{1,0:T(8,128)(2,1)S(1)} %collective-permute-done), channel_id=1, source_target_pairs={{0,16},{2,18},{4,20},{6,22},{8,24},{10,26},{12,28},{14,30},{16,0},... | collective-permute-start | bytes 393224 | tf_op jit(solution)/shard_map/ppermute | solution.py:349
  17.5 9.0 %collective-permute-start.2 = (bf16[512,128]{1,0:T(8,128)(2,1)S(1)}, bf16[512,128]{1,0:T(8,128)(2,1)S(1)}, u32[]{:S(2)}, u32[]{:S(2)}) collective-permute-start(bf16[512,128]{1,0:T(8,128)(2,1)S(1)} %collective-permute-done), channel_id=1, source_target_pairs={{0,8},{2,10},{4,12},{6,14},{8,16},{10,18},{12,20},{14,22},{16,24},... | collective-permute-start | bytes 393224 | tf_op jit(solution)/shard_map/ppermute | solution.py:349
  18.8 7.7 %collective-permute-start.3 = (bf16[512,128]{1,0:T(8,128)(2,1)S(1)}, bf16[512,128]{1,0:T(8,128)(2,1)S(1)}, u32[]{:S(2)}, u32[]{:S(2)}) collective-permute-start(bf16[512,128]{1,0:T(8,128)(2,1)S(1)} %collective-permute-done), channel_id=1, source_target_pairs={{0,24},{2,26},{4,28},{6,30},{8,0},{10,2},{12,4},{14,6},{16,8},{18,... | collective-permute-start | bytes 393224 | tf_op jit(solution)/shard_map/ppermute | solution.py:349
  20.8 13.8 %copy-start.6 = (s32[32,2]{0,1:T(2,128)S(1)}, s32[32,2]{0,1:T(2,128)}, u32[]{:S(2)}) copy-start(s32[32,2]{0,1:T(2,128)} %param.12) | copy-start | bytes 772
  20.8 27.3 %collective-permute-start.8 = (bf16[2048,128]{1,0:T(8,128)(2,1)S(1)}, bf16[2048,128]{1,0:T(8,128)(2,1)S(1)}, u32[]{:S(2)}, u32[]{:S(2)}) collective-permute-start(bf16[2048,128]{1,0:T(8,128)(2,1)S(1)} %constant_dynamic-update-slice_fusion.p0), channel_id=1, source_target_pairs={{0,8},{2,10},{4,12},{6,14},{8,16},{10,18},{12,20},{14,22},{16,24},... | collective-permute-start | bytes 1572872 | tf_op jit(solution)/shard_map/ppermute | solution.py:349
  21.2 26.9 %collective-permute-start.9 = (bf16[2048,128]{1,0:T(8,128)(2,1)S(1)}, bf16[2048,128]{1,0:T(8,128)(2,1)S(1)}, u32[]{:S(2)}, u32[]{:S(2)}) collective-permute-start(bf16[2048,128]{1,0:T(8,128)(2,1)S(1)} %constant_dynamic-update-slice_fusion.p0), channel_id=1, source_target_pairs={{0,24},{2,26},{4,28},{6,30},{8,0},{10,2},{12,4},{14,6},{16,8},{18,... | collective-permute-start | bytes 1572872 | tf_op jit(solution)/shard_map/ppermute | solution.py:349
  26.5 25.0 %collective-permute-start.10 = (bf16[2048,128]{1,0:T(8,128)(2,1)S(1)}, bf16[2048,128]{1,0:T(8,128)(2,1)S(1)}, u32[]{:S(2)}, u32[]{:S(2)}) collective-permute-start(bf16[2048,128]{1,0:T(8,128)(2,1)S(1)} %pad_maximum_fusion.p3), channel_id=1, source_target_pairs={{0,2},{2,4},{4,6},{6,0},{8,10},{10,12},{12,14},{14,8},{16,18},{18,... | collective-permute-start | bytes 1572872 | tf_op jit(solution)/shard_map/ppermute | solution.py:349
  26.6 24.9 %collective-permute-start.11 = (bf16[2048,128]{1,0:T(8,128)(2,1)S(1)}, bf16[2048,128]{1,0:T(8,128)(2,1)S(1)}, u32[]{:S(2)}, u32[]{:S(2)}) collective-permute-start(bf16[2048,128]{1,0:T(8,128)(2,1)S(1)} %pad_maximum_fusion.p3), channel_id=1, source_target_pairs={{0,6},{2,0},{4,2},{6,4},{8,14},{10,8},{12,10},{14,12},{16,22},{18,... | collective-permute-start | bytes 1572872 | tf_op jit(solution)/shard_map/ppermute | solution.py:349
  29.8 25.0 %collective-permute-start.4 = (bf16[256,1024]{1,0:T(8,128)(2,1)}, bf16[256,1024]{1,0:T(8,128)(2,1)}, u32[]{:S(2)}, u32[]{:S(2)}) collective-permute-start(bf16[256,1024]{1,0:T(8,128)(2,1)} %pad_maximum_fusion.1), channel_id=1, source_target_pairs={{0,62},{2,60},{4,58},{6,56},{8,54},{10,52},{12,50},{14,48},{16,46}... | collective-permute-start | bytes 1572872 | tf_op jit(solution)/shard_map/ppermute | solution.py:349
  48.2 14.3 %collective-permute-start.12 = (bf16[1024,128]{1,0:T(8,128)(2,1)S(1)}, bf16[1024,128]{1,0:T(8,128)(2,1)S(1)}, u32[]{:S(2)}, u32[]{:S(2)}) collective-permute-start(bf16[1024,128]{1,0:T(8,128)(2,1)S(1)} %slice.142), channel_id=1, source_target_pairs={{0,8},{2,10},{4,12},{6,14},{8,16},{10,18},{12,20},{14,22},{16,24},... | collective-permute-start | bytes 786440 | tf_op jit(solution)/shard_map/ppermute | solution.py:349
  48.5 13.9 %collective-permute-start.13 = (bf16[1024,128]{1,0:T(8,128)(2,1)S(1)}, bf16[1024,128]{1,0:T(8,128)(2,1)S(1)}, u32[]{:S(2)}, u32[]{:S(2)}) collective-permute-start(bf16[1024,128]{1,0:T(8,128)(2,1)S(1)} %slice.143), channel_id=1, source_target_pairs={{0,24},{2,26},{4,28},{6,30},{8,0},{10,2},{12,4},{14,6},{16,8},{18,... | collective-permute-start | bytes 786440 | tf_op jit(solution)/shard_map/ppermute | solution.py:349
  51.5 4.4 %copy-start.1 = (bf16[256,512]{1,0:T(8,128)(2,1)S(1)}, bf16[256,512]{1,0:T(8,128)(2,1)}, u32[]{:S(2)}) copy-start(bf16[256,512]{1,0:T(8,128)(2,1)} %get-tuple-element.176) | copy-start | bytes 786436
  51.5 10.9 %collective-permute-start.14 = (bf16[1024,128]{1,0:T(8,128)(2,1)S(1)}, bf16[1024,128]{1,0:T(8,128)(2,1)S(1)}, u32[]{:S(2)}, u32[]{:S(2)}) collective-permute-start(bf16[1024,128]{1,0:T(8,128)(2,1)S(1)} %slice.144), channel_id=1, source_target_pairs={{0,2},{2,4},{4,6},{6,0},{8,10},{10,12},{12,14},{14,8},{16,18},{18,... | collective-permute-start | bytes 786440 | tf_op jit(solution)/shard_map/ppermute | solution.py:349
  51.6 10.8 %collective-permute-start.15 = (bf16[1024,128]{1,0:T(8,128)(2,1)S(1)}, bf16[1024,128]{1,0:T(8,128)(2,1)S(1)}, u32[]{:S(2)}, u32[]{:S(2)}) collective-permute-start(bf16[1024,128]{1,0:T(8,128)(2,1)S(1)} %slice.145), channel_id=1, source_target_pairs={{0,6},{2,0},{4,2},{6,4},{8,14},{10,8},{12,10},{14,12},{16,22},{18,... | collective-permute-start | bytes 786440 | tf_op jit(solution)/shard_map/ppermute | solution.py:349
  56.0 0.7 copy-start
  67.7 26.3 %collective-permute-start.20 = (f32[512]{0:T(512)S(1)}, f32[512]{0:T(512)S(1)}, u32[]{:S(2)}, u32[]{:S(2)}) collective-permute-start(f32[512]{0:T(512)S(1)} %bitcast.3), channel_id=1, source_target_pairs={{0,1},{1,0},{2,3},{3,2},{4,5},{5,4},{6,7},{7,6},{8,9},{9,8},{10,11... | collective-permute-start | bytes 6152 | tf_op jit(solution)/shard_map/ppermute | solution.py:445
  68.4 25.7 %collective-permute-start.16 = (bf16[1024,128]{1,0:T(8,128)(2,1)S(1)}, bf16[1024,128]{1,0:T(8,128)(2,1)S(1)}, u32[]{:S(2)}, u32[]{:S(2)}) collective-permute-start(bf16[1024,128]{1,0:T(8,128)(2,1)S(1)} %get-tuple-element.128), channel_id=1, source_target_pairs={{0,2},{2,4},{4,6},{6,0},{8,10},{10,12},{12,14},{14,8},{16,18},{18,... | collective-permute-start | bytes 786440 | tf_op jit(solution)/shard_map/ppermute | solution.py:349
  68.4 25.7 %collective-permute-start.17 = (bf16[1024,128]{1,0:T(8,128)(2,1)S(1)}, bf16[1024,128]{1,0:T(8,128)(2,1)S(1)}, u32[]{:S(2)}, u32[]{:S(2)}) collective-permute-start(bf16[1024,128]{1,0:T(8,128)(2,1)S(1)} %get-tuple-element.129), channel_id=1, source_target_pairs={{0,6},{2,0},{4,2},{6,4},{8,14},{10,8},{12,10},{14,12},{16,22},{18,... | collective-permute-start | bytes 786440 | tf_op jit(solution)/shard_map/ppermute | solution.py:349
  71.6 22.4 %collective-permute-start.18 = (bf16[1024,128]{1,0:T(8,128)(2,1)S(1)}, bf16[1024,128]{1,0:T(8,128)(2,1)S(1)}, u32[]{:S(2)}, u32[]{:S(2)}) collective-permute-start(bf16[1024,128]{1,0:T(8,128)(2,1)S(1)} %get-tuple-element.130), channel_id=1, source_target_pairs={{0,8},{2,10},{4,12},{6,14},{8,16},{10,18},{12,20},{14,22},{16,24},... | collective-permute-start | bytes 786440 | tf_op jit(solution)/shard_map/ppermute | solution.py:349
  74.9 19.1 %collective-permute-start.19 = (bf16[1024,128]{1,0:T(8,128)(2,1)S(1)}, bf16[1024,128]{1,0:T(8,128)(2,1)S(1)}, u32[]{:S(2)}, u32[]{:S(2)}) collective-permute-start(bf16[1024,128]{1,0:T(8,128)(2,1)S(1)} %get-tuple-element.131), channel_id=1, source_target_pairs={{0,24},{2,26},{4,28},{6,30},{8,0},{10,2},{12,4},{14,6},{16,8},{18,... | collective-permute-start | bytes 786440 | tf_op jit(solution)/shard_map/ppermute | solution.py:349
  94.5 12.3 %collective-permute-start.27 = (bf16[2048,128]{1,0:T(8,128)(2,1)S(1)}, bf16[2048,128]{1,0:T(8,128)(2,1)S(1)}, u32[]{:S(2)}, u32[]{:S(2)}) collective-permute-start(bf16[2048,128]{1,0:T(8,128)(2,1)S(1)} %pad_maximum_fusion.7), channel_id=1, source_target_pairs={{0,2},{2,4},{4,6},{6,0},{8,10},{10,12},{12,14},{14,8},{16,18},{18,... | collective-permute-start | bytes 1572872 | tf_op jit(solution)/shard_map/ppermute | solution.py:349
  94.6 20.3 %collective-permute-start.28 = (bf16[2048,128]{1,0:T(8,128)(2,1)S(1)}, bf16[2048,128]{1,0:T(8,128)(2,1)S(1)}, u32[]{:S(2)}, u32[]{:S(2)}) collective-permute-start(bf16[2048,128]{1,0:T(8,128)(2,1)S(1)} %pad_maximum_fusion.8), channel_id=1, source_target_pairs={{0,6},{2,0},{4,2},{6,4},{8,14},{10,8},{12,10},{14,12},{16,22},{18,... | collective-permute-start | bytes 1572872 | tf_op jit(solution)/shard_map/ppermute | solution.py:349
  99.1 18.2 %collective-permute-start.21 = (bf16[2048,128]{1,0:T(8,128)(2,1)S(1)}, bf16[2048,128]{1,0:T(8,128)(2,1)S(1)}, u32[]{:S(2)}, u32[]{:S(2)}) collective-permute-start(bf16[2048,128]{1,0:T(8,128)(2,1)S(1)} %pad_maximum_fusion.4), channel_id=1, source_target_pairs={{0,8},{2,10},{4,12},{6,14},{8,16},{10,18},{12,20},{14,22},{16,24},... | collective-permute-start | bytes 1572872 | tf_op jit(solution)/shard_map/ppermute | solution.py:349
  100.4 20.5 %collective-permute-start.22 = (bf16[2048,128]{1,0:T(8,128)(2,1)S(1)}, bf16[2048,128]{1,0:T(8,128)(2,1)S(1)}, u32[]{:S(2)}, u32[]{:S(2)}) collective-permute-start(bf16[2048,128]{1,0:T(8,128)(2,1)S(1)} %pad_maximum_fusion.5), channel_id=1, source_target_pairs={{0,24},{2,26},{4,28},{6,30},{8,0},{10,2},{12,4},{14,6},{16,8},{18,... | collective-permute-start | bytes 1572872 | tf_op jit(solution)/shard_map/ppermute | solution.py:349
  115.1 11.6 %collective-permute-start.29 = (bf16[512,128]{1,0:T(8,128)(2,1)S(1)}, bf16[512,128]{1,0:T(8,128)(2,1)S(1)}, u32[]{:S(2)}, u32[]{:S(2)}) collective-permute-start(bf16[512,128]{1,0:T(8,128)(2,1)S(1)} %get-tuple-element.158), channel_id=1, source_target_pairs={{0,16},{2,18},{4,20},{6,22},{8,24},{10,26},{12,28},{14,30},{16,0},... | collective-permute-start | bytes 393224 | tf_op jit(solution)/shard_map/ppermute | solution.py:349
  115.2 15.7 %collective-permute-start.30 = (bf16[512,128]{1,0:T(8,128)(2,1)S(1)}, bf16[512,128]{1,0:T(8,128)(2,1)S(1)}, u32[]{:S(2)}, u32[]{:S(2)}) collective-permute-start(bf16[512,128]{1,0:T(8,128)(2,1)S(1)} %get-tuple-element.159), channel_id=1, source_target_pairs={{0,24},{2,26},{4,28},{6,30},{8,0},{10,2},{12,4},{14,6},{16,8},{18,... | collective-permute-start | bytes 393224 | tf_op jit(solution)/shard_map/ppermute | solution.py:349
  115.3 16.5 %collective-permute-start.31 = (bf16[512,128]{1,0:T(8,128)(2,1)S(1)}, bf16[512,128]{1,0:T(8,128)(2,1)S(1)}, u32[]{:S(2)}, u32[]{:S(2)}) collective-permute-start(bf16[512,128]{1,0:T(8,128)(2,1)S(1)} %get-tuple-element.160), channel_id=1, source_target_pairs={{0,8},{2,10},{4,12},{6,14},{8,16},{10,18},{12,20},{14,22},{16,24},... | collective-permute-start | bytes 393224 | tf_op jit(solution)/shard_map/ppermute | solution.py:349
  121.1 22.9 %collective-permute-start.23 = (bf16[272,512]{1,0:T(8,128)(2,1)S(1)}, bf16[272,512]{1,0:T(8,128)(2,1)S(1)}, u32[]{:S(2)}, u32[]{:S(2)}) collective-permute-start(bf16[272,512]{1,0:T(8,128)(2,1)S(1)} %pad_maximum_fusion.9), channel_id=1, source_target_pairs={{0,62},{2,60},{4,58},{6,56},{8,54},{10,52},{12,50},{14,48},{16,46}... | collective-permute-start | bytes 835592 | tf_op jit(solution)/shard_map/ppermute | solution.py:349
  125.2 7.6 %collective-permute-start.24 = (bf16[512,128]{1,0:T(8,128)(2,1)S(1)}, bf16[512,128]{1,0:T(8,128)(2,1)S(1)}, u32[]{:S(2)}, u32[]{:S(2)}) collective-permute-start(bf16[512,128]{1,0:T(8,128)(2,1)S(1)} %get-tuple-element.143), channel_id=1, source_target_pairs={{0,4},{2,6},{4,0},{6,2},{8,12},{10,14},{12,8},{14,10},{16,20},{18,... | collective-permute-start | bytes 393224 | tf_op jit(solution)/shard_map/ppermute | solution.py:349
  126.7 9.9 %collective-permute-start.25 = (bf16[512,128]{1,0:T(8,128)(2,1)S(1)}, bf16[512,128]{1,0:T(8,128)(2,1)S(1)}, u32[]{:S(2)}, u32[]{:S(2)}) collective-permute-start(bf16[512,128]{1,0:T(8,128)(2,1)S(1)} %get-tuple-element.144), channel_id=1, source_target_pairs={{0,6},{2,0},{4,2},{6,4},{8,14},{10,8},{12,10},{14,12},{16,22},{18,... | collective-permute-start | bytes 393224 | tf_op jit(solution)/shard_map/ppermute | solution.py:349
  130.9 6.9 %collective-permute-start.26 = (bf16[512,128]{1,0:T(8,128)(2,1)S(1)}, bf16[512,128]{1,0:T(8,128)(2,1)S(1)}, u32[]{:S(2)}, u32[]{:S(2)}) collective-permute-start(bf16[512,128]{1,0:T(8,128)(2,1)S(1)} %get-tuple-element.145), channel_id=1, source_target_pairs={{0,2},{2,4},{4,6},{6,0},{8,10},{10,12},{12,14},{14,8},{16,18},{18,... | collective-permute-start | bytes 393224 | tf_op jit(solution)/shard_map/ppermute | solution.py:349
  131.8 10.8 %collective-permute-start.32 = (bf16[512,128]{1,0:T(8,128)(2,1)S(1)}, bf16[512,128]{1,0:T(8,128)(2,1)S(1)}, u32[]{:S(2)}, u32[]{:S(2)}) collective-permute-start(bf16[512,128]{1,0:T(8,128)(2,1)S(1)} %add_convert_fusion.6), channel_id=1, source_target_pairs={{0,62},{2,60},{4,58},{6,56},{8,54},{10,52},{12,50},{14,48},{16,46}... | collective-permute-start | bytes 393224 | tf_op jit(solution)/shard_map/ppermute | solution.py:349

commit v5 on v4

--- a/solution.py
+++ b/solution.py
@@ -475,10 +475,12 @@
     delta_in = dq_in[rows].astype(f32)
     dq_in = dq_in[:rows]
     delta_sum = delta_own + (delta_in[:rows] + delta_in[rows:])
-    query_grads = columns_of(dq[:rows], dq_in)
+    own_sum, query_grads, gate_grads = in_step(
+        own_sum, columns_of(dq[:rows], dq_in), (1.0 - gate) * delta_sum
+    )
     key_grads = columns_of(own_sum[:rows], back[:rows])
     value_grads = columns_of(own_sum[rows:], back[rows:])
-    return query_grads, key_grads, value_grads, (1.0 - gate) * delta_sum
+    return query_grads, key_grads, value_grads, gate_grads
 
 
 def solution(mesh):

time: 145 us -> 144 us (level)
  Pallas kernels: 26.3 us -> 38.1 us
  starting transfers between devices: 73.9 us -> 67.2 us
  waiting for transfers between devices: 33.7 us -> 27.5 us
    pallas_call x3, Pallas kernels: 22.4 us -> 34.1 us  [call(): pl.pallas_call(kernel, out_shape=outs, in_specs=[sm] + [vm] * (len(args)...]
    ppermute x32, starting transfers between devices: 73.2 us -> 66.5 us  [send(): return lax.ppermute(a, 'seq', perm)]
    ppermute x32, waiting for transfers between devices: 33.7 us -> 27.5 us  [send(): return lax.ppermute(a, 'seq', perm)]
  transfers between devices with their start and end apart: 33 -> 33, of which waited for: 9 -> 9; matrix products, arithmetic and copies ran while one was open for 4% -> 4% of each run, Pallas kernels for 14% -> 22%
where the time goes in v5:
time: 144 us
  starting transfers between devices  67.2 us (47%)
  Pallas kernels  38.1 us (26%)
  waiting for transfers between devices  27.5 us (19%)
  other arithmetic  6.85 us (5%)
  local copies, waits for them, and re-layouts  3.57 us (2%)
    ppermute x32, starting transfers between devices, send(): return lax.ppermute(a, 'seq', perm)  66.5 us
    pallas_call x3, Pallas kernels, call(): pl.pallas_call(kernel, out_shape=outs, in_specs=[sm] + [vm] * (len(args)...  34.1 us
    ppermute x32, waiting for transfers between devices, send(): return lax.ppermute(a, 'seq', perm)  27.5 us
    pallas_call x1, Pallas kernels, local(): pl.pallas_call(table_kernel, out_shape=shape(TABLE, dtype=jnp.int32), in_...  3.92 us
  transfers between devices with their start and end apart: 33, of which 9 were waited for; matrix products, arithmetic and copies ran while one was open for 4% of the time, Pallas kernels for 22%

profile of v5, /device:TPU:0, one launch (start us, length us, event | category | flops | bytes accessed | tf_op | source)
XLA Modules:
  0.0 144.4 jit_solution(3353256084824912142)
XLA Ops:
  0.7 1.0 constant_dynamic-update-slice_fusion.4
  1.7 9.1 %collective-permute-start = (bf16[512,128]{1,0:T(8,128)(2,1)S(1)}, bf16[512,128]{1,0:T(8,128)(2,1)S(1)}, u32[]{:S(2)}, u32[]{:S(2)}) collective-permute-start(bf16[512,128]{1,0:T(8,128)(2,1)S(1)} %pad_maximum_fusion.10), channel_id=1, source_target_pairs={{0,62},{2,60},{4,58},{6,56},{8,54},{10,52},{12,50},{14,48},{16,46}... | collective-permute-start | bytes 393224 | tf_op jit(solution)/shard_map/ppermute | solution.py:349
  10.8 0.7 collective-permute-start.5
  11.5 0.5 collective-permute-start.6
  12.0 2.8 %collective-permute-start.7 = (bf16[512,128]{1,0:T(8,128)(2,1)S(1)}, bf16[512,128]{1,0:T(8,128)(2,1)S(1)}, u32[]{:S(2)}, u32[]{:S(2)}) collective-permute-start(bf16[512,128]{1,0:T(8,128)(2,1)S(1)} %pad_maximum_fusion.11), channel_id=1, source_target_pairs={{0,6},{2,0},{4,2},{6,4},{8,14},{10,8},{12,10},{14,12},{16,22},{18,... | collective-permute-start | bytes 393224 | tf_op jit(solution)/shard_map/ppermute | solution.py:349
  15.0 0.9 copy-done.2
  15.8 0.8 broadcast_select_fusion.2
  16.6 0.9 pad_maximum_fusion.1
  17.5 0.2 collective-permute-start.2
  17.7 1.1 collective-permute-done.5
  18.8 2.0 %collective-permute-start.3 = (bf16[512,128]{1,0:T(8,128)(2,1)S(1)}, bf16[512,128]{1,0:T(8,128)(2,1)S(1)}, u32[]{:S(2)}, u32[]{:S(2)}) collective-permute-start(bf16[512,128]{1,0:T(8,128)(2,1)S(1)} %collective-permute-done), channel_id=1, source_target_pairs={{0,24},{2,26},{4,28},{6,30},{8,0},{10,2},{12,4},{14,6},{16,8},{18,... | collective-permute-start | bytes 393224 | tf_op jit(solution)/shard_map/ppermute | solution.py:349
  20.8 0.3 collective-permute-start.8
  21.2 3.0 %collective-permute-start.9 = (bf16[2048,128]{1,0:T(8,128)(2,1)S(1)}, bf16[2048,128]{1,0:T(8,128)(2,1)S(1)}, u32[]{:S(2)}, u32[]{:S(2)}) collective-permute-start(bf16[2048,128]{1,0:T(8,128)(2,1)S(1)} %constant_dynamic-update-slice_fusion.p0), channel_id=1, source_target_pairs={{0,24},{2,26},{4,28},{6,30},{8,0},{10,2},{12,4},{14,6},{16,8},{18,... | collective-permute-start | bytes 1572872 | tf_op jit(solution)/shard_map/ppermute | solution.py:349
  24.2 1.3 collective-permute-done.1
  25.4 1.0 collective-permute-done.2
  26.6 3.2 %collective-permute-start.11 = (bf16[2048,128]{1,0:T(8,128)(2,1)S(1)}, bf16[2048,128]{1,0:T(8,128)(2,1)S(1)}, u32[]{:S(2)}, u32[]{:S(2)}) collective-permute-start(bf16[2048,128]{1,0:T(8,128)(2,1)S(1)} %pad_maximum_fusion.p3), channel_id=1, source_target_pairs={{0,6},{2,0},{4,2},{6,4},{8,14},{10,8},{12,10},{14,12},{16,22},{18,... | collective-permute-start | bytes 1572872 | tf_op jit(solution)/shard_map/ppermute | solution.py:349
  29.8 4.8 %collective-permute-start.4 = (bf16[256,1024]{1,0:T(8,128)(2,1)}, bf16[256,1024]{1,0:T(8,128)(2,1)}, u32[]{:S(2)}, u32[]{:S(2)}) collective-permute-start(bf16[256,1024]{1,0:T(8,128)(2,1)} %pad_maximum_fusion.1), channel_id=1, source_target_pairs={{0,62},{2,60},{4,58},{6,56},{8,54},{10,52},{12,50},{14,48},{16,46}... | collective-permute-start | bytes 1572872 | tf_op jit(solution)/shard_map/ppermute | solution.py:349
  34.7 0.6 reshape.78.ids
  35.3 3.9 %block_table.1.tab = s32[76]{0:T(128)} custom-call(s32[1]{0:T(128)} %bitcast.place_ref, s32[64]{0:T(128)} %reshape.78.ids, s32[32]{0:T(128)} %counts.1), custom_call_target="tpu_custom_call" | custom-call | tf_op jit(solution)/shard_map/block_table/pallas_call | solution.py:392
  39.2 8.9 %collective-permute-done.8.p1 = bf16[2048,128]{1,0:T(8,128)(2,1)S(1)} collective-permute-done((bf16[2048,128]{1,0:T(8,128)(2,1)S(1)}, bf16[2048,128]{1,0:T(8,128)(2,1)S(1)}, u32[]{:S(2)}, u32[]{:S(2)}) %collective-permute-start.8) | collective-permute-done | bytes 524320 | tf_op jit(solution)/shard_map/ppermute | solution.py:349
  48.2 0.4 collective-permute-start.12
  48.5 2.9 %collective-permute-start.13 = (bf16[1024,128]{1,0:T(8,128)(2,1)S(1)}, bf16[1024,128]{1,0:T(8,128)(2,1)S(1)}, u32[]{:S(2)}, u32[]{:S(2)}) collective-permute-start(bf16[1024,128]{1,0:T(8,128)(2,1)S(1)} %slice.143), channel_id=1, source_target_pairs={{0,24},{2,26},{4,28},{6,30},{8,0},{10,2},{12,4},{14,6},{16,8},{18,... | collective-permute-start | bytes 786440 | tf_op jit(solution)/shard_map/ppermute | solution.py:349
  51.6 3.2 %collective-permute-start.15 = (bf16[1024,128]{1,0:T(8,128)(2,1)S(1)}, bf16[1024,128]{1,0:T(8,128)(2,1)S(1)}, u32[]{:S(2)}, u32[]{:S(2)}) collective-permute-start(bf16[1024,128]{1,0:T(8,128)(2,1)S(1)} %slice.145), channel_id=1, source_target_pairs={{0,6},{2,0},{4,2},{6,4},{8,14},{10,8},{12,10},{14,12},{16,22},{18,... | collective-permute-start | bytes 786440 | tf_op jit(solution)/shard_map/ppermute | solution.py:349
  54.9 1.1 fusion.6
  56.0 0.6 copy-done
  56.6 9.8 %near_stats.1 = (f32[4,8,512]{2,1,0:T(8,128)S(1)}, f32[4,8,512]{2,1,0:T(8,128)S(1)}, f32[4,8,512]{2,1,0:T(8,128)S(1)}) custom-call(s32[76]{0:T(128)S(1)} %copy-done, bf16[512,512]{1,0:T(8,128)(2,1)S(1)} %pad_maximum_fusion.2.q, bf16[512,512]{1,0:T(8,128)(2,1)S(1)} %pad_maximum_fusion.3.do, bf16[2048,128]{1,0:T(8,128)(2,1)S(1)} %constant_dynamic-update-slice_fusion.p0, ...), custom_call_target="tpu_custom_call" | custom-call | flops 6442450944 | bytes 6291456 | tf_op jit(solution)/shard_map/near_stats/pallas_call | solution.py:316
  66.5 6.3 %far_grads.1 = (bf16[1024,128]{1,0:T(8,128)(2,1)S(1)}, bf16[1024,128]{1,0:T(8,128)(2,1)S(1)}, bf16[1024,128]{1,0:T(8,128)(2,1)S(1)}, bf16[1024,128]{1,0:T(8,128)...) custom-call(s32[76]{0:T(128)S(1)} %copy-done, ...), custom_call_target="tpu_custom_call" | custom-call | flops 7516192768 | bytes 2097152 | tf_op jit(solution)/shard_map/far_grads/pallas_call | solution.py:316
  72.7 0.7 collective-permute-start.20
  73.4 3.2 %collective-permute-start.17 = (bf16[1024,128]{1,0:T(8,128)(2,1)S(1)}, bf16[1024,128]{1,0:T(8,128)(2,1)S(1)}, u32[]{:S(2)}, u32[]{:S(2)}) collective-permute-start(bf16[1024,128]{1,0:T(8,128)(2,1)S(1)} %get-tuple-element.131), channel_id=1, source_target_pairs={{0,6},{2,0},{4,2},{6,4},{8,14},{10,8},{12,10},{14,12},{16,22},{18,... | collective-permute-start | bytes 786440 | tf_op jit(solution)/shard_map/ppermute | solution.py:349
  76.6 5.8 %collective-permute-start.19 = (bf16[1024,128]{1,0:T(8,128)(2,1)S(1)}, bf16[1024,128]{1,0:T(8,128)(2,1)S(1)}, u32[]{:S(2)}, u32[]{:S(2)}) collective-permute-start(bf16[1024,128]{1,0:T(8,128)(2,1)S(1)} %get-tuple-element.133), channel_id=1, source_target_pairs={{0,24},{2,26},{4,28},{6,30},{8,0},{10,2},{12,4},{14,6},{16,8},{18,... | collective-permute-start | bytes 786440 | tf_op jit(solution)/shard_map/ppermute | solution.py:349
  82.5 18.1 %near_grads.1 = (bf16[512,512]{1,0:T(8,128)(2,1)S(1)}, bf16[2048,128]{1,0:T(8,128)(2,1)S(1)}, bf16[2048,128]{1,0:T(8,128)(2,1)S(1)}, bf16[2048,128]{1,0:T(8,128)...) custom-call(s32[76]{0:T(128)S(1)} %copy-done, ...), custom_call_target="tpu_custom_call" | custom-call | flops 16106127360 | bytes 6291456 | tf_op jit(solution)/shard_map/near_grads/pallas_call | solution.py:316
  101.3 3.2 %collective-permute-start.28 = (bf16[2048,128]{1,0:T(8,128)(2,1)S(1)}, bf16[2048,128]{1,0:T(8,128)(2,1)S(1)}, u32[]{:S(2)}, u32[]{:S(2)}) collective-permute-start(bf16[2048,128]{1,0:T(8,128)(2,1)S(1)} %pad_maximum_fusion.8), channel_id=1, source_target_pairs={{0,6},{2,0},{4,2},{6,4},{8,14},{10,8},{12,10},{14,12},{16,22},{18,... | collective-permute-start | bytes 1572872 | tf_op jit(solution)/shard_map/ppermute | solution.py:349
  104.7 3.2 %collective-permute-start.22 = (bf16[2048,128]{1,0:T(8,128)(2,1)S(1)}, bf16[2048,128]{1,0:T(8,128)(2,1)S(1)}, u32[]{:S(2)}, u32[]{:S(2)}) collective-permute-start(bf16[2048,128]{1,0:T(8,128)(2,1)S(1)} %pad_maximum_fusion.5), channel_id=1, source_target_pairs={{0,24},{2,26},{4,28},{6,30},{8,0},{10,2},{12,4},{14,6},{16,8},{18,... | collective-permute-start | bytes 1572872 | tf_op jit(solution)/shard_map/ppermute | solution.py:349
  108.0 3.7 %collective-permute-done.27 = bf16[2048,128]{1,0:T(8,128)(2,1)S(1)} collective-permute-done((bf16[2048,128]{1,0:T(8,128)(2,1)S(1)}, bf16[2048,128]{1,0:T(8,128)(2,1)S(1)}, u32[]{:S(2)}, u32[]{:S(2)}) %collective-permute-start.27) | collective-permute-done | bytes 524320 | tf_op jit(solution)/shard_map/ppermute | solution.py:349
  111.6 2.0 %collective-permute-done.28 = bf16[2048,128]{1,0:T(8,128)(2,1)S(1)} collective-permute-done((bf16[2048,128]{1,0:T(8,128)(2,1)S(1)}, bf16[2048,128]{1,0:T(8,128)(2,1)S(1)}, u32[]{:S(2)}, u32[]{:S(2)}) %collective-permute-start.28) | collective-permute-done | bytes 524320 | tf_op jit(solution)/shard_map/ppermute | solution.py:349
  113.6 0.2 add_convert_fusion
  114.0 4.5 %collective-permute-start.30 = (bf16[512,128]{1,0:T(8,128)(2,1)S(1)}, bf16[512,128]{1,0:T(8,128)(2,1)S(1)}, u32[]{:S(2)}, u32[]{:S(2)}) collective-permute-start(bf16[512,128]{1,0:T(8,128)(2,1)S(1)} %get-tuple-element.164), channel_id=1, source_target_pairs={{0,24},{2,26},{4,28},{6,30},{8,0},{10,2},{12,4},{14,6},{16,8},{18,... | collective-permute-start | bytes 393224 | tf_op jit(solution)/shard_map/ppermute | solution.py:349
  118.5 0.8 collective-permute-start.31
  119.5 8.8 %collective-permute-start.26 = (bf16[272,512]{1,0:T(8,128)(2,1)S(1)}, bf16[272,512]{1,0:T(8,128)(2,1)S(1)}, u32[]{:S(2)}, u32[]{:S(2)}) collective-permute-start(bf16[272,512]{1,0:T(8,128)(2,1)S(1)} %pad_maximum_fusion.9), channel_id=1, source_target_pairs={{0,62},{2,60},{4,58},{6,56},{8,54},{10,52},{12,50},{14,48},{16,46}... | collective-permute-start | bytes 835592 | tf_op jit(solution)/shard_map/ppermute | solution.py:349
  128.4 2.6 %collective-permute-start.24 = (bf16[512,128]{1,0:T(8,128)(2,1)S(1)}, bf16[512,128]{1,0:T(8,128)(2,1)S(1)}, u32[]{:S(2)}, u32[]{:S(2)}) collective-permute-start(bf16[512,128]{1,0:T(8,128)(2,1)S(1)} %get-tuple-element.146), channel_id=1, source_target_pairs={{0,6},{2,0},{4,2},{6,4},{8,14},{10,8},{12,10},{14,12},{16,22},{18,... | collective-permute-start | bytes 393224 | tf_op jit(solution)/shard_map/ppermute | solution.py:349
  131.2 0.7 collective-permute-start.32
  131.9 4.5 %collective-permute-done.23 = bf16[512,128]{1,0:T(8,128)(2,1)S(1)} collective-permute-done((bf16[512,128]{1,0:T(8,128)(2,1)S(1)}, bf16[512,128]{1,0:T(8,128)(2,1)S(1)}, u32[]{:S(2)}, u32[]{:S(2)}) %collective-permute-start.23) | collective-permute-done | bytes 131104 | tf_op jit(solution)/shard_map/ppermute | solution.py:349
  136.3 4.3 %collective-permute-done.24 = bf16[512,128]{1,0:T(8,128)(2,1)S(1)} collective-permute-done((bf16[512,128]{1,0:T(8,128)(2,1)S(1)}, bf16[512,128]{1,0:T(8,128)(2,1)S(1)}, u32[]{:S(2)}, u32[]{:S(2)}) %collective-permute-start.24) | collective-permute-done | bytes 131104 | tf_op jit(solution)/shard_map/ppermute | solution.py:349
  140.6 0.8 collective-permute-done.25
  141.6 0.6 add_multiply_fusion
  142.1 0.9 pad_maximum_fusion.6
  143.0 0.7 pad_maximum_fusion.13
  143.7 0.7 pad_maximum_fusion.12
  (90 shorter events, 2.4 us)
Async XLA Ops:
  0.6 1.0 copy-start.4
  0.6 14.1 %copy-start.3 = (bf16[256,1024]{1,0:T(8,128)(2,1)S(1)}, bf16[256,1024]{1,0:T(8,128)(2,1)}, u32[]{:S(2)}) copy-start(bf16[256,1024]{1,0:T(8,128)(2,1)} %param.10) | copy-start | bytes 1572868
  1.7 15.8 %collective-permute-start = (bf16[512,128]{1,0:T(8,128)(2,1)S(1)}, bf16[512,128]{1,0:T(8,128)(2,1)S(1)}, u32[]{:S(2)}, u32[]{:S(2)}) collective-permute-start(bf16[512,128]{1,0:T(8,128)(2,1)S(1)} %pad_maximum_fusion.10), channel_id=1, source_target_pairs={{0,62},{2,60},{4,58},{6,56},{8,54},{10,52},{12,50},{14,48},{16,46}... | collective-permute-start | bytes 393224 | tf_op jit(solution)/shard_map/ppermute | solution.py:349
  10.8 4.0 %copy-start.5 = (f32[256]{0:T(256)S(1)}, f32[256]{0:T(256)}, u32[]{:S(2)}) copy-start(f32[256]{0:T(256)} %param.11) | copy-start | bytes 3076
  10.8 8.0 %collective-permute-start.5 = (bf16[512,128]{1,0:T(8,128)(2,1)S(1)}, bf16[512,128]{1,0:T(8,128)(2,1)S(1)}, u32[]{:S(2)}, u32[]{:S(2)}) collective-permute-start(bf16[512,128]{1,0:T(8,128)(2,1)S(1)} %pad_maximum_fusion.11), channel_id=1, source_target_pairs={{0,4},{2,6},{4,0},{6,2},{8,12},{10,14},{12,8},{14,10},{16,20},{18,... | collective-permute-start | bytes 393224 | tf_op jit(solution)/shard_map/ppermute | solution.py:349
  11.5 9.2 %collective-permute-start.6 = (bf16[512,128]{1,0:T(8,128)(2,1)S(1)}, bf16[512,128]{1,0:T(8,128)(2,1)S(1)}, u32[]{:S(2)}, u32[]{:S(2)}) collective-permute-start(bf16[512,128]{1,0:T(8,128)(2,1)S(1)} %pad_maximum_fusion.11), channel_id=1, source_target_pairs={{0,2},{2,4},{4,6},{6,0},{8,10},{10,12},{12,14},{14,8},{16,18},{18,... | collective-permute-start | bytes 393224 | tf_op jit(solution)/shard_map/ppermute | solution.py:349
  12.0 8.8 %collective-permute-start.7 = (bf16[512,128]{1,0:T(8,128)(2,1)S(1)}, bf16[512,128]{1,0:T(8,128)(2,1)S(1)}, u32[]{:S(2)}, u32[]{:S(2)}) collective-permute-start(bf16[512,128]{1,0:T(8,128)(2,1)S(1)} %pad_maximum_fusion.11), channel_id=1, source_target_pairs={{0,6},{2,0},{4,2},{6,4},{8,14},{10,8},{12,10},{14,12},{16,22},{18,... | collective-permute-start | bytes 393224 | tf_op jit(solution)/shard_map/ppermute | solution.py:349
  14.8 1.1 copy-start.2
  17.5 7.9 %collective-permute-start.1 = (bf16[512,128]{1,0:T(8,128)(2,1)S(1)}, bf16[512,128]{1,0:T(8,128)(2,1)S(1)}, u32[]{:S(2)}, u32[]{:S(2)}) collective-permute-start(bf16[512,128]{1,0:T(8,128)(2,1)S(1)} %collective-permute-done), channel_id=1, source_target_pairs={{0,16},{2,18},{4,20},{6,22},{8,24},{10,26},{12,28},{14,30},{16,0},... | collective-permute-start | bytes 393224 | tf_op jit(solution)/shard_map/ppermute | solution.py:349
  17.5 9.0 %collective-permute-start.2 = (bf16[512,128]{1,0:T(8,128)(2,1)S(1)}, bf16[512,128]{1,0:T(8,128)(2,1)S(1)}, u32[]{:S(2)}, u32[]{:S(2)}) collective-permute-start(bf16[512,128]{1,0:T(8,128)(2,1)S(1)} %collective-permute-done), channel_id=1, source_target_pairs={{0,8},{2,10},{4,12},{6,14},{8,16},{10,18},{12,20},{14,22},{16,24},... | collective-permute-start | bytes 393224 | tf_op jit(solution)/shard_map/ppermute | solution.py:349
  18.8 7.7 %collective-permute-start.3 = (bf16[512,128]{1,0:T(8,128)(2,1)S(1)}, bf16[512,128]{1,0:T(8,128)(2,1)S(1)}, u32[]{:S(2)}, u32[]{:S(2)}) collective-permute-start(bf16[512,128]{1,0:T(8,128)(2,1)S(1)} %collective-permute-done), channel_id=1, source_target_pairs={{0,24},{2,26},{4,28},{6,30},{8,0},{10,2},{12,4},{14,6},{16,8},{18,... | collective-permute-start | bytes 393224 | tf_op jit(solution)/shard_map/ppermute | solution.py:349
  20.8 13.8 %copy-start.6 = (s32[32,2]{0,1:T(2,128)S(1)}, s32[32,2]{0,1:T(2,128)}, u32[]{:S(2)}) copy-start(s32[32,2]{0,1:T(2,128)} %param.12) | copy-start | bytes 772
  20.8 27.3 %collective-permute-start.8 = (bf16[2048,128]{1,0:T(8,128)(2,1)S(1)}, bf16[2048,128]{1,0:T(8,128)(2,1)S(1)}, u32[]{:S(2)}, u32[]{:S(2)}) collective-permute-start(bf16[2048,128]{1,0:T(8,128)(2,1)S(1)} %constant_dynamic-update-slice_fusion.p0), channel_id=1, source_target_pairs={{0,8},{2,10},{4,12},{6,14},{8,16},{10,18},{12,20},{14,22},{16,24},... | collective-permute-start | bytes 1572872 | tf_op jit(solution)/shard_map/ppermute | solution.py:349
  21.2 26.9 %collective-permute-start.9 = (bf16[2048,128]{1,0:T(8,128)(2,1)S(1)}, bf16[2048,128]{1,0:T(8,128)(2,1)S(1)}, u32[]{:S(2)}, u32[]{:S(2)}) collective-permute-start(bf16[2048,128]{1,0:T(8,128)(2,1)S(1)} %constant_dynamic-update-slice_fusion.p0), channel_id=1, source_target_pairs={{0,24},{2,26},{4,28},{6,30},{8,0},{10,2},{12,4},{14,6},{16,8},{18,... | collective-permute-start | bytes 1572872 | tf_op jit(solution)/shard_map/ppermute | solution.py:349
  26.5 25.0 %collective-permute-start.10 = (bf16[2048,128]{1,0:T(8,128)(2,1)S(1)}, bf16[2048,128]{1,0:T(8,128)(2,1)S(1)}, u32[]{:S(2)}, u32[]{:S(2)}) collective-permute-start(bf16[2048,128]{1,0:T(8,128)(2,1)S(1)} %pad_maximum_fusion.p3), channel_id=1, source_target_pairs={{0,2},{2,4},{4,6},{6,0},{8,10},{10,12},{12,14},{14,8},{16,18},{18,... | collective-permute-start | bytes 1572872 | tf_op jit(solution)/shard_map/ppermute | solution.py:349
  26.6 24.9 %collective-permute-start.11 = (bf16[2048,128]{1,0:T(8,128)(2,1)S(1)}, bf16[2048,128]{1,0:T(8,128)(2,1)S(1)}, u32[]{:S(2)}, u32[]{:S(2)}) collective-permute-start(bf16[2048,128]{1,0:T(8,128)(2,1)S(1)} %pad_maximum_fusion.p3), channel_id=1, source_target_pairs={{0,6},{2,0},{4,2},{6,4},{8,14},{10,8},{12,10},{14,12},{16,22},{18,... | collective-permute-start | bytes 1572872 | tf_op jit(solution)/shard_map/ppermute | solution.py:349
  29.8 25.0 %collective-permute-start.4 = (bf16[256,1024]{1,0:T(8,128)(2,1)}, bf16[256,1024]{1,0:T(8,128)(2,1)}, u32[]{:S(2)}, u32[]{:S(2)}) collective-permute-start(bf16[256,1024]{1,0:T(8,128)(2,1)} %pad_maximum_fusion.1), channel_id=1, source_target_pairs={{0,62},{2,60},{4,58},{6,56},{8,54},{10,52},{12,50},{14,48},{16,46}... | collective-permute-start | bytes 1572872 | tf_op jit(solution)/shard_map/ppermute | solution.py:349
  48.2 18.2 %collective-permute-start.12 = (bf16[1024,128]{1,0:T(8,128)(2,1)S(1)}, bf16[1024,128]{1,0:T(8,128)(2,1)S(1)}, u32[]{:S(2)}, u32[]{:S(2)}) collective-permute-start(bf16[1024,128]{1,0:T(8,128)(2,1)S(1)} %slice.142), channel_id=1, source_target_pairs={{0,8},{2,10},{4,12},{6,14},{8,16},{10,18},{12,20},{14,22},{16,24},... | collective-permute-start | bytes 786440 | tf_op jit(solution)/shard_map/ppermute | solution.py:349
  48.5 17.9 %collective-permute-start.13 = (bf16[1024,128]{1,0:T(8,128)(2,1)S(1)}, bf16[1024,128]{1,0:T(8,128)(2,1)S(1)}, u32[]{:S(2)}, u32[]{:S(2)}) collective-permute-start(bf16[1024,128]{1,0:T(8,128)(2,1)S(1)} %slice.143), channel_id=1, source_target_pairs={{0,24},{2,26},{4,28},{6,30},{8,0},{10,2},{12,4},{14,6},{16,8},{18,... | collective-permute-start | bytes 786440 | tf_op jit(solution)/shard_map/ppermute | solution.py:349
  51.5 4.4 %copy-start.1 = (bf16[256,512]{1,0:T(8,128)(2,1)S(1)}, bf16[256,512]{1,0:T(8,128)(2,1)}, u32[]{:S(2)}) copy-start(bf16[256,512]{1,0:T(8,128)(2,1)} %get-tuple-element.182) | copy-start | bytes 786436
  51.5 14.9 %collective-permute-start.14 = (bf16[1024,128]{1,0:T(8,128)(2,1)S(1)}, bf16[1024,128]{1,0:T(8,128)(2,1)S(1)}, u32[]{:S(2)}, u32[]{:S(2)}) collective-permute-start(bf16[1024,128]{1,0:T(8,128)(2,1)S(1)} %slice.144), channel_id=1, source_target_pairs={{0,2},{2,4},{4,6},{6,0},{8,10},{10,12},{12,14},{14,8},{16,18},{18,... | collective-permute-start | bytes 786440 | tf_op jit(solution)/shard_map/ppermute | solution.py:349
  51.6 14.8 %collective-permute-start.15 = (bf16[1024,128]{1,0:T(8,128)(2,1)S(1)}, bf16[1024,128]{1,0:T(8,128)(2,1)S(1)}, u32[]{:S(2)}, u32[]{:S(2)}) collective-permute-start(bf16[1024,128]{1,0:T(8,128)(2,1)S(1)} %slice.145), channel_id=1, source_target_pairs={{0,6},{2,0},{4,2},{6,4},{8,14},{10,8},{12,10},{14,12},{16,22},{18,... | collective-permute-start | bytes 786440 | tf_op jit(solution)/shard_map/ppermute | solution.py:349
  56.0 0.7 copy-start
  72.7 28.0 %collective-permute-start.20 = (f32[512]{0:T(512)S(1)}, f32[512]{0:T(512)S(1)}, u32[]{:S(2)}, u32[]{:S(2)}) collective-permute-start(f32[512]{0:T(512)S(1)} %bitcast.3), channel_id=1, source_target_pairs={{0,1},{1,0},{2,3},{3,2},{4,5},{5,4},{6,7},{7,6},{8,9},{9,8},{10,11... | collective-permute-start | bytes 6152 | tf_op jit(solution)/shard_map/ppermute | solution.py:445
  73.4 27.3 %collective-permute-start.16 = (bf16[1024,128]{1,0:T(8,128)(2,1)S(1)}, bf16[1024,128]{1,0:T(8,128)(2,1)S(1)}, u32[]{:S(2)}, u32[]{:S(2)}) collective-permute-start(bf16[1024,128]{1,0:T(8,128)(2,1)S(1)} %get-tuple-element.130), channel_id=1, source_target_pairs={{0,2},{2,4},{4,6},{6,0},{8,10},{10,12},{12,14},{14,8},{16,18},{18,... | collective-permute-start | bytes 786440 | tf_op jit(solution)/shard_map/ppermute | solution.py:349
  73.4 27.3 %collective-permute-start.17 = (bf16[1024,128]{1,0:T(8,128)(2,1)S(1)}, bf16[1024,128]{1,0:T(8,128)(2,1)S(1)}, u32[]{:S(2)}, u32[]{:S(2)}) collective-permute-start(bf16[1024,128]{1,0:T(8,128)(2,1)S(1)} %get-tuple-element.131), channel_id=1, source_target_pairs={{0,6},{2,0},{4,2},{6,4},{8,14},{10,8},{12,10},{14,12},{16,22},{18,... | collective-permute-start | bytes 786440 | tf_op jit(solution)/shard_map/ppermute | solution.py:349
  76.6 24.1 %collective-permute-start.18 = (bf16[1024,128]{1,0:T(8,128)(2,1)S(1)}, bf16[1024,128]{1,0:T(8,128)(2,1)S(1)}, u32[]{:S(2)}, u32[]{:S(2)}) collective-permute-start(bf16[1024,128]{1,0:T(8,128)(2,1)S(1)} %get-tuple-element.132), channel_id=1, source_target_pairs={{0,8},{2,10},{4,12},{6,14},{8,16},{10,18},{12,20},{14,22},{16,24},... | collective-permute-start | bytes 786440 | tf_op jit(solution)/shard_map/ppermute | solution.py:349
  76.6 24.1 %collective-permute-start.19 = (bf16[1024,128]{1,0:T(8,128)(2,1)S(1)}, bf16[1024,128]{1,0:T(8,128)(2,1)S(1)}, u32[]{:S(2)}, u32[]{:S(2)}) collective-permute-start(bf16[1024,128]{1,0:T(8,128)(2,1)S(1)} %get-tuple-element.133), channel_id=1, source_target_pairs={{0,24},{2,26},{4,28},{6,30},{8,0},{10,2},{12,4},{14,6},{16,8},{18,... | collective-permute-start | bytes 786440 | tf_op jit(solution)/shard_map/ppermute | solution.py:349
  101.2 10.5 %collective-permute-start.27 = (bf16[2048,128]{1,0:T(8,128)(2,1)S(1)}, bf16[2048,128]{1,0:T(8,128)(2,1)S(1)}, u32[]{:S(2)}, u32[]{:S(2)}) collective-permute-start(bf16[2048,128]{1,0:T(8,128)(2,1)S(1)} %pad_maximum_fusion.7), channel_id=1, source_target_pairs={{0,2},{2,4},{4,6},{6,0},{8,10},{10,12},{12,14},{14,8},{16,18},{18,... | collective-permute-start | bytes 1572872 | tf_op jit(solution)/shard_map/ppermute | solution.py:349
  101.3 12.4 %collective-permute-start.28 = (bf16[2048,128]{1,0:T(8,128)(2,1)S(1)}, bf16[2048,128]{1,0:T(8,128)(2,1)S(1)}, u32[]{:S(2)}, u32[]{:S(2)}) collective-permute-start(bf16[2048,128]{1,0:T(8,128)(2,1)S(1)} %pad_maximum_fusion.8), channel_id=1, source_target_pairs={{0,6},{2,0},{4,2},{6,4},{8,14},{10,8},{12,10},{14,12},{16,22},{18,... | collective-permute-start | bytes 1572872 | tf_op jit(solution)/shard_map/ppermute | solution.py:349
  104.6 14.6 %collective-permute-start.21 = (bf16[2048,128]{1,0:T(8,128)(2,1)S(1)}, bf16[2048,128]{1,0:T(8,128)(2,1)S(1)}, u32[]{:S(2)}, u32[]{:S(2)}) collective-permute-start(bf16[2048,128]{1,0:T(8,128)(2,1)S(1)} %pad_maximum_fusion.4), channel_id=1, source_target_pairs={{0,8},{2,10},{4,12},{6,14},{8,16},{10,18},{12,20},{14,22},{16,24},... | collective-permute-start | bytes 1572872 | tf_op jit(solution)/shard_map/ppermute | solution.py:349
  104.7 14.6 %collective-permute-start.22 = (bf16[2048,128]{1,0:T(8,128)(2,1)S(1)}, bf16[2048,128]{1,0:T(8,128)(2,1)S(1)}, u32[]{:S(2)}, u32[]{:S(2)}) collective-permute-start(bf16[2048,128]{1,0:T(8,128)(2,1)S(1)} %pad_maximum_fusion.5), channel_id=1, source_target_pairs={{0,24},{2,26},{4,28},{6,30},{8,0},{10,2},{12,4},{14,6},{16,8},{18,... | collective-permute-start | bytes 1572872 | tf_op jit(solution)/shard_map/ppermute | solution.py:349
  113.9 14.5 %collective-permute-start.29 = (bf16[512,128]{1,0:T(8,128)(2,1)S(1)}, bf16[512,128]{1,0:T(8,128)(2,1)S(1)}, u32[]{:S(2)}, u32[]{:S(2)}) collective-permute-start(bf16[512,128]{1,0:T(8,128)(2,1)S(1)} %get-tuple-element.163), channel_id=1, source_target_pairs={{0,16},{2,18},{4,20},{6,22},{8,24},{10,26},{12,28},{14,30},{16,0},... | collective-permute-start | bytes 393224 | tf_op jit(solution)/shard_map/ppermute | solution.py:349
  114.0 16.9 %collective-permute-start.30 = (bf16[512,128]{1,0:T(8,128)(2,1)S(1)}, bf16[512,128]{1,0:T(8,128)(2,1)S(1)}, u32[]{:S(2)}, u32[]{:S(2)}) collective-permute-start(bf16[512,128]{1,0:T(8,128)(2,1)S(1)} %get-tuple-element.164), channel_id=1, source_target_pairs={{0,24},{2,26},{4,28},{6,30},{8,0},{10,2},{12,4},{14,6},{16,8},{18,... | collective-permute-start | bytes 393224 | tf_op jit(solution)/shard_map/ppermute | solution.py:349
  118.5 12.6 %collective-permute-start.31 = (bf16[512,128]{1,0:T(8,128)(2,1)S(1)}, bf16[512,128]{1,0:T(8,128)(2,1)S(1)}, u32[]{:S(2)}, u32[]{:S(2)}) collective-permute-start(bf16[512,128]{1,0:T(8,128)(2,1)S(1)} %get-tuple-element.165), channel_id=1, source_target_pairs={{0,8},{2,10},{4,12},{6,14},{8,16},{10,18},{12,20},{14,22},{16,24},... | collective-permute-start | bytes 393224 | tf_op jit(solution)/shard_map/ppermute | solution.py:349
  119.5 22.0 %collective-permute-start.26 = (bf16[272,512]{1,0:T(8,128)(2,1)S(1)}, bf16[272,512]{1,0:T(8,128)(2,1)S(1)}, u32[]{:S(2)}, u32[]{:S(2)}) collective-permute-start(bf16[272,512]{1,0:T(8,128)(2,1)S(1)} %pad_maximum_fusion.9), channel_id=1, source_target_pairs={{0,62},{2,60},{4,58},{6,56},{8,54},{10,52},{12,50},{14,48},{16,46}... | collective-permute-start | bytes 835592 | tf_op jit(solution)/shard_map/ppermute | solution.py:349
  128.3 8.1 %collective-permute-start.23 = (bf16[512,128]{1,0:T(8,128)(2,1)S(1)}, bf16[512,128]{1,0:T(8,128)(2,1)S(1)}, u32[]{:S(2)}, u32[]{:S(2)}) collective-permute-start(bf16[512,128]{1,0:T(8,128)(2,1)S(1)} %get-tuple-element.145), channel_id=1, source_target_pairs={{0,4},{2,6},{4,0},{6,2},{8,12},{10,14},{12,8},{14,10},{16,20},{18,... | collective-permute-start | bytes 393224 | tf_op jit(solution)/shard_map/ppermute | solution.py:349
  128.4 12.2 %collective-permute-start.24 = (bf16[512,128]{1,0:T(8,128)(2,1)S(1)}, bf16[512,128]{1,0:T(8,128)(2,1)S(1)}, u32[]{:S(2)}, u32[]{:S(2)}) collective-permute-start(bf16[512,128]{1,0:T(8,128)(2,1)S(1)} %get-tuple-element.146), channel_id=1, source_target_pairs={{0,6},{2,0},{4,2},{6,4},{8,14},{10,8},{12,10},{14,12},{16,22},{18,... | collective-permute-start | bytes 393224 | tf_op jit(solution)/shard_map/ppermute | solution.py:349
  130.9 10.5 %collective-permute-start.25 = (bf16[512,128]{1,0:T(8,128)(2,1)S(1)}, bf16[512,128]{1,0:T(8,128)(2,1)S(1)}, u32[]{:S(2)}, u32[]{:S(2)}) collective-permute-start(bf16[512,128]{1,0:T(8,128)(2,1)S(1)} %get-tuple-element.147), channel_id=1, source_target_pairs={{0,2},{2,4},{4,6},{6,0},{8,10},{10,12},{12,14},{14,8},{16,18},{18,... | collective-permute-start | bytes 393224 | tf_op jit(solution)/shard_map/ppermute | solution.py:349
  131.2 11.8 %collective-permute-start.32 = (bf16[512,128]{1,0:T(8,128)(2,1)S(1)}, bf16[512,128]{1,0:T(8,128)(2,1)S(1)}, u32[]{:S(2)}, u32[]{:S(2)}) collective-permute-start(bf16[512,128]{1,0:T(8,128)(2,1)S(1)} %add_convert_fusion.6), channel_id=1, source_target_pairs={{0,62},{2,60},{4,58},{6,56},{8,54},{10,52},{12,50},{14,48},{16,46}... | collective-permute-start | bytes 393224 | tf_op jit(solution)/shard_map/ppermute | solution.py:349
